TPU v7x, 32 devices: a whole 2x2x4 slice. The times are simulated.
32 devices in a mesh: rep: 2 (over y), shard: 16 (over z, x, core).
Axes of the slice: x: 2, y: 2, z: 4, core: 2. Of those that a mesh axis runs over, the one named last changes fastest.
Arguments:
- inputs: bfloat16 [32, 256, 768], P(('rep', 'shard')), may hold values from -6 to 6
- segment_ids: int32 [32, 256], P(('rep', 'shard')), may hold values from 0 to 3, never falling along the last dimension, each value on 1 to 170 neighbouring positions
- qkv_weight: bfloat16 [2, 768, 2304], P(None, 'shard'), may hold values from -0.21875 to 0.21875
- out_weight: bfloat16 [2, 768, 768], P(None, 'shard'), may hold values from -1.75 to 1.75
- gate_weight: bfloat16 [2, 768, 3072], P(None, 'shard'), may hold values from -0.21875 to 0.21875
- up_weight: bfloat16 [2, 768, 3072], P(None, 'shard'), may hold values from -0.21875 to 0.21875
- down_weight: bfloat16 [2, 3072, 768], P(None, 'shard'), may hold values from -0.109375 to 0.109375
- first_gain: bfloat16 [2, 768], P(None, 'shard'), may hold values from 0.5 to 1.5
- first_bias: bfloat16 [2, 768], P(None, 'shard'), may hold values from -1.796875 to 1.796875
- second_gain: bfloat16 [2, 768], P(None, 'shard'), may hold values from 0.5 to 1.5
- second_bias: bfloat16 [2, 768], P(None, 'shard'), may hold values from -1.796875 to 1.796875
- cotangent: bfloat16 [32, 256, 768], P(('rep', 'shard')), may hold values from -6 to 6
Outputs:
- output: bfloat16 [32, 256, 768], P(('rep', 'shard'))
- input_gradient: float32 [32, 256, 768], P(('rep', 'shard'))
- qkv_gradient: float32 [2, 768, 2304], P(None, 'shard')
- out_gradient: float32 [2, 768, 768], P(None, 'shard')
- gate_gradient: float32 [2, 768, 3072], P(None, 'shard')
- up_gradient: float32 [2, 768, 3072], P(None, 'shard')
- down_gradient: float32 [2, 3072, 768], P(None, 'shard')
- first_gain_gradient: float32 [2, 768], P(None, 'shard')
- first_bias_gradient: float32 [2, 768], P(None, 'shard')
- second_gain_gradient: float32 [2, 768], P(None, 'shard')
- second_bias_gradient: float32 [2, 768], P(None, 'shard')
Inputs may be any that keep to these rules, and one draw needn't show every extreme that they name: `segment_ids`: segment numbers never fall along a sequence; each document has 1 to 170 tokens.
All inputs are finite; a program needn't handle non-finite values.
Results may differ from a plain program's by a relative error of at most 0.029.
Values may be sent and summed in bfloat16 or wider, within the bound.
A program may use at most 192 MiB of HBM per device.

v0:
```python
import math

import jax
import jax.numpy as jnp
from jax import lax
from jax.sharding import PartitionSpec as P

HEADS = 12
HEAD = 64


eps_norm = 1e-12
rope_base = 1000.0
masked_score = -1e30


def positions_of(segment_row):
    token_index = jnp.arange(segment_row.shape[0], dtype=jnp.int32)
    before = jnp.concatenate([segment_row[:1] - 1, segment_row[:-1]])
    starts = jnp.where(segment_row != before, token_index, jnp.zeros_like(token_index))
    return token_index - lax.cummax(starts, axis=0)


def rotary_tables(position):
    half_width = HEAD // 2
    frequency = rope_base ** (-2.0 * jnp.arange(half_width, dtype=jnp.float32) / HEAD)
    angles = position.astype(jnp.float32)[:, None] * frequency[None, :]
    return (jnp.cos(angles), jnp.sin(angles))


def rotate(values, cosine_table, sine_table):
    half_width = values.shape[-1] // 2
    lead_half = values[..., :half_width]
    tail_half = values[..., half_width:]
    cos_wide = cosine_table[:, None, :]
    sin_wide = sine_table[:, None, :]
    return jnp.concatenate(
        [lead_half * cos_wide - tail_half * sin_wide, tail_half * cos_wide + lead_half * sin_wide],
        axis=-1,
    )


def unrotate(values, cosine_table, sine_table):
    half_width = values.shape[-1] // 2
    lead_half = values[..., :half_width]
    tail_half = values[..., half_width:]
    cos_wide = cosine_table[:, None, :]
    sin_wide = sine_table[:, None, :]
    return jnp.concatenate(
        [lead_half * cos_wide + tail_half * sin_wide, tail_half * cos_wide - lead_half * sin_wide],
        axis=-1,
    )


def norm_forward(values, gain_row, bias_row):
    mean_row = jnp.mean(values, axis=-1, keepdims=True)
    centred = values - mean_row
    variance = jnp.mean(centred * centred, axis=-1, keepdims=True)
    inverse = lax.rsqrt(variance + eps_norm)
    normed = centred * inverse
    return (normed * gain_row + bias_row, normed, inverse)


def norm_backward(upstream, normed, inverse, gain_row):
    scaled = upstream * gain_row
    gain_sum = jnp.sum(upstream * normed, axis=0)
    bias_sum = jnp.sum(upstream, axis=0)
    grad_input = inverse * (
        scaled
        - jnp.mean(scaled, axis=-1, keepdims=True)
        - normed * jnp.mean(scaled * normed, axis=-1, keepdims=True)
    )
    return (grad_input, gain_sum, bias_sum)


def times_transposed(left_side, right_side):
    return lax.dot_general(
        left_side, right_side, (((1,), (1,)), ((), ())), preferred_element_type=jnp.float32
    )


def outer_sum(left_side, right_side):
    return lax.dot_general(
        left_side, right_side, (((0,), (0,)), ((), ())), preferred_element_type=jnp.float32
    )


def to_pairs(values):
    token_count = values.shape[0]
    return values.reshape(token_count, HEADS // 2, 2 * HEAD).transpose(1, 0, 2)


def from_pairs(values):
    return values.transpose(1, 0, 2).reshape(values.shape[1], HEADS * HEAD)


def pair_scores(query_pair, key_pair, allowed, score_scale):
    token_count = query_pair.shape[0]
    queries = query_pair.reshape(token_count, 2, HEAD)
    key_rows = key_pair.reshape(token_count, 2, HEAD)
    scores = (
        jnp.einsum("qhd,khd->hqk", queries, key_rows, preferred_element_type=jnp.float32)
        * score_scale
    )
    return (jnp.where(allowed[None], scores, masked_score), queries, key_rows)


def pair_forward(block_item, allowed, score_scale):
    query_pair, key_pair, value_pair = block_item
    token_count = query_pair.shape[0]
    scores, queries, key_rows = pair_scores(query_pair, key_pair, allowed, score_scale)
    row_top = jnp.max(scores, axis=-1, keepdims=True)
    exponent = jnp.exp(scores - row_top)
    row_total = jnp.sum(exponent, axis=-1, keepdims=True)
    probabilities = exponent / row_total
    logsum = row_top[..., 0] + jnp.log(row_total[..., 0])
    value_rows = value_pair.reshape(token_count, 2, HEAD)
    attended = jnp.einsum(
        "hqk,khd->qhd",
        probabilities.astype(jnp.bfloat16),
        value_rows,
        preferred_element_type=jnp.float32,
    )
    return (attended.reshape(token_count, 2 * HEAD), logsum)


def pair_backward(block_item, allowed, score_scale):
    query_pair, key_pair, value_pair, grad_pair, logsum = block_item
    token_count = query_pair.shape[0]
    scores, queries, key_rows = pair_scores(query_pair, key_pair, allowed, score_scale)
    probabilities = jnp.exp(scores - logsum[..., None])
    value_rows = value_pair.reshape(token_count, 2, HEAD)
    grad_rows = grad_pair.reshape(token_count, 2, HEAD)
    grad_probs = jnp.einsum(
        "qhd,khd->hqk", grad_rows, value_rows, preferred_element_type=jnp.float32
    )
    grad_values = jnp.einsum(
        "hqk,qhd->khd",
        probabilities.astype(jnp.bfloat16),
        grad_rows,
        preferred_element_type=jnp.float32,
    )
    grad_scores = probabilities * (
        grad_probs - jnp.sum(grad_probs * probabilities, axis=-1, keepdims=True)
    )
    grad_scores = grad_scores.astype(jnp.bfloat16)
    grad_queries = (
        jnp.einsum("hqk,khd->qhd", grad_scores, key_rows, preferred_element_type=jnp.float32)
        * score_scale
    )
    grad_keys = (
        jnp.einsum("hqk,qhd->khd", grad_scores, queries, preferred_element_type=jnp.float32)
        * score_scale
    )
    return (
        grad_queries.reshape(token_count, 2 * HEAD),
        grad_keys.reshape(token_count, 2 * HEAD),
        grad_values.reshape(token_count, 2 * HEAD),
    )


def fetch_forward(
    qkv_weight,
    out_weight,
    gate_weight,
    up_weight,
    down_weight,
    first_gain,
    first_bias,
    second_gain,
    second_bias,
    layer_index,
):
    return (
        lax.all_gather(qkv_weight[layer_index], "shard", axis=0, tiled=True),
        lax.all_gather(out_weight[layer_index], "shard", axis=0, tiled=True),
        lax.all_gather(gate_weight[layer_index], "shard", axis=0, tiled=True),
        lax.all_gather(up_weight[layer_index], "shard", axis=0, tiled=True),
        lax.all_gather(down_weight[layer_index], "shard", axis=0, tiled=True),
        lax.all_gather(first_gain[layer_index], "shard", axis=0, tiled=True),
        lax.all_gather(first_bias[layer_index], "shard", axis=0, tiled=True),
        lax.all_gather(second_gain[layer_index], "shard", axis=0, tiled=True),
        lax.all_gather(second_bias[layer_index], "shard", axis=0, tiled=True),
    )


def fetch_backward(
    qkv_weight,
    out_weight,
    gate_weight,
    up_weight,
    down_weight,
    first_gain,
    first_bias,
    second_gain,
    second_bias,
    layer_index,
):
    return (
        lax.all_gather(qkv_weight[layer_index], "shard", axis=0, tiled=True),
        lax.all_gather(out_weight[layer_index], "shard", axis=0, tiled=True),
        lax.all_gather(gate_weight[layer_index], "shard", axis=0, tiled=True),
        lax.all_gather(up_weight[layer_index], "shard", axis=0, tiled=True),
        lax.all_gather(down_weight[layer_index], "shard", axis=0, tiled=True),
        lax.all_gather(first_gain[layer_index], "shard", axis=0, tiled=True),
        lax.all_gather(first_bias[layer_index], "shard", axis=0, tiled=True),
        lax.all_gather(second_gain[layer_index], "shard", axis=0, tiled=True),
        lax.all_gather(second_bias[layer_index], "shard", axis=0, tiled=True),
    )


def share_gradients(gradients):
    owned_sums = (
        lax.psum_scatter(gradients[0], "shard", scatter_dimension=0, tiled=True),
        lax.psum_scatter(gradients[1], "shard", scatter_dimension=0, tiled=True),
        lax.psum_scatter(gradients[2], "shard", scatter_dimension=0, tiled=True),
        lax.psum_scatter(gradients[3], "shard", scatter_dimension=0, tiled=True),
        lax.psum_scatter(gradients[4], "shard", scatter_dimension=0, tiled=True),
        lax.psum_scatter(gradients[5], "shard", scatter_dimension=0, tiled=True),
        lax.psum_scatter(gradients[6], "shard", scatter_dimension=0, tiled=True),
        lax.psum_scatter(gradients[7], "shard", scatter_dimension=0, tiled=True),
        lax.psum_scatter(gradients[8], "shard", scatter_dimension=0, tiled=True),
    )
    halves = (
        lax.psum_scatter(
            owned_sums[0].astype(jnp.bfloat16), "rep", scatter_dimension=0, tiled=True
        ).astype(jnp.float32),
        lax.psum_scatter(
            owned_sums[1].astype(jnp.bfloat16), "rep", scatter_dimension=0, tiled=True
        ).astype(jnp.float32),
        lax.psum_scatter(
            owned_sums[2].astype(jnp.bfloat16), "rep", scatter_dimension=0, tiled=True
        ).astype(jnp.float32),
        lax.psum_scatter(
            owned_sums[3].astype(jnp.bfloat16), "rep", scatter_dimension=0, tiled=True
        ).astype(jnp.float32),
        lax.psum_scatter(
            owned_sums[4].astype(jnp.bfloat16), "rep", scatter_dimension=0, tiled=True
        ).astype(jnp.float32),
        lax.psum_scatter(
            owned_sums[5].astype(jnp.bfloat16), "rep", scatter_dimension=0, tiled=True
        ).astype(jnp.float32),
        lax.psum_scatter(
            owned_sums[6].astype(jnp.bfloat16), "rep", scatter_dimension=0, tiled=True
        ).astype(jnp.float32),
        lax.psum_scatter(
            owned_sums[7].astype(jnp.bfloat16), "rep", scatter_dimension=0, tiled=True
        ).astype(jnp.float32),
        lax.psum_scatter(
            owned_sums[8].astype(jnp.bfloat16), "rep", scatter_dimension=0, tiled=True
        ).astype(jnp.float32),
    )
    return (
        lax.all_gather(halves[0].astype(jnp.bfloat16), "rep", axis=0, tiled=True).astype(
            jnp.float32
        ),
        lax.all_gather(halves[1].astype(jnp.bfloat16), "rep", axis=0, tiled=True).astype(
            jnp.float32
        ),
        lax.all_gather(halves[2].astype(jnp.bfloat16), "rep", axis=0, tiled=True).astype(
            jnp.float32
        ),
        lax.all_gather(halves[3].astype(jnp.bfloat16), "rep", axis=0, tiled=True).astype(
            jnp.float32
        ),
        lax.all_gather(halves[4].astype(jnp.bfloat16), "rep", axis=0, tiled=True).astype(
            jnp.float32
        ),
        lax.all_gather(halves[5].astype(jnp.bfloat16), "rep", axis=0, tiled=True).astype(
            jnp.float32
        ),
        lax.all_gather(halves[6].astype(jnp.bfloat16), "rep", axis=0, tiled=True).astype(
            jnp.float32
        ),
        lax.all_gather(halves[7].astype(jnp.bfloat16), "rep", axis=0, tiled=True).astype(
            jnp.float32
        ),
        lax.all_gather(halves[8].astype(jnp.bfloat16), "rep", axis=0, tiled=True).astype(
            jnp.float32
        ),
    )


def layer_forward(hidden_state, weights, cosine_table, sine_table, allowed, score_scale):
    qkv_full, out_full, gate_full, up_full, down_full, gain_one, bias_one, gain_two, bias_two = (
        weights
    )
    token_count, model_width = hidden_state.shape
    state_low = hidden_state.astype(jnp.bfloat16)
    projected = jnp.dot(state_low, qkv_full, preferred_element_type=jnp.float32)
    queries = rotate(
        projected[:, :model_width].reshape(token_count, HEADS, HEAD), cosine_table, sine_table
    )
    queries = queries.astype(jnp.bfloat16).reshape(token_count, model_width)
    key_rows = rotate(
        projected[:, model_width : 2 * model_width].reshape(token_count, HEADS, HEAD),
        cosine_table,
        sine_table,
    )
    key_rows = key_rows.astype(jnp.bfloat16).reshape(token_count, model_width)
    value_rows = projected[:, 2 * model_width :].astype(jnp.bfloat16)

    def attend_pair(block_item):
        return pair_forward(block_item, allowed, score_scale)

    attended_pairs, logsum = lax.map(
        attend_pair, (to_pairs(queries), to_pairs(key_rows), to_pairs(value_rows))
    )
    attended = from_pairs(attended_pairs).astype(jnp.bfloat16)
    branch = jnp.dot(attended, out_full, preferred_element_type=jnp.float32)
    middle, normed_one, inverse_one = norm_forward(
        hidden_state + branch, gain_one.astype(jnp.float32), bias_one.astype(jnp.float32)
    )
    middle_low = middle.astype(jnp.bfloat16)
    gate_pre = jnp.dot(middle_low, gate_full, preferred_element_type=jnp.float32)
    up_pre = jnp.dot(middle_low, up_full, preferred_element_type=jnp.float32)
    activated = (jax.nn.silu(gate_pre) * up_pre).astype(jnp.bfloat16)
    feed = jnp.dot(activated, down_full, preferred_element_type=jnp.float32)
    result, normed_two, inverse_two = norm_forward(
        middle + feed, gain_two.astype(jnp.float32), bias_two.astype(jnp.float32)
    )
    stored = (
        state_low,
        queries,
        key_rows,
        value_rows,
        logsum,
        attended,
        normed_one,
        inverse_one,
        middle_low,
        gate_pre,
        up_pre,
        activated,
        normed_two,
        inverse_two,
    )
    return (result, stored)


def layer_backward(upstream, weights, stored, cosine_table, sine_table, allowed, score_scale):
    qkv_full, out_full, gate_full, up_full, down_full, gain_one, bias_one, gain_two, bias_two = (
        weights
    )
    (
        state_low,
        queries,
        key_rows,
        value_rows,
        logsum,
        attended,
        normed_one,
        inverse_one,
        middle_low,
        gate_pre,
        up_pre,
        activated,
        normed_two,
        inverse_two,
    ) = stored
    token_count, model_width = upstream.shape
    grad_mid, gain_two_sum, bias_two_sum = norm_backward(
        upstream, normed_two, inverse_two, gain_two.astype(jnp.float32)
    )
    grad_feed = grad_mid.astype(jnp.bfloat16)
    down_sum = outer_sum(activated, grad_feed)
    grad_act = times_transposed(grad_feed, down_full)
    sigmoid_gate = jax.nn.sigmoid(gate_pre)
    grad_gate = (grad_act * up_pre * sigmoid_gate * (1.0 + gate_pre * (1.0 - sigmoid_gate))).astype(
        jnp.bfloat16
    )
    grad_up = (grad_act * gate_pre * sigmoid_gate).astype(jnp.bfloat16)
    gate_sum = outer_sum(middle_low, grad_gate)
    up_sum = outer_sum(middle_low, grad_up)
    grad_middle = (
        grad_mid + times_transposed(grad_gate, gate_full) + times_transposed(grad_up, up_full)
    )
    grad_sum, gain_one_sum, bias_one_sum = norm_backward(
        grad_middle, normed_one, inverse_one, gain_one.astype(jnp.float32)
    )
    grad_branch = grad_sum.astype(jnp.bfloat16)
    out_sum = outer_sum(attended, grad_branch)
    grad_attended = times_transposed(grad_branch, out_full).astype(jnp.bfloat16)

    def attend_back(block_item):
        return pair_backward(block_item, allowed, score_scale)

    grad_query_pairs, grad_key_pairs, grad_value_pairs = lax.map(
        attend_back,
        (
            to_pairs(queries),
            to_pairs(key_rows),
            to_pairs(value_rows),
            to_pairs(grad_attended),
            logsum,
        ),
    )
    grad_queries = unrotate(
        from_pairs(grad_query_pairs).reshape(token_count, HEADS, HEAD), cosine_table, sine_table
    ).reshape(token_count, model_width)
    grad_keys = unrotate(
        from_pairs(grad_key_pairs).reshape(token_count, HEADS, HEAD), cosine_table, sine_table
    ).reshape(token_count, model_width)
    grad_projected = jnp.concatenate(
        [grad_queries, grad_keys, from_pairs(grad_value_pairs)], axis=1
    ).astype(jnp.bfloat16)
    qkv_sum = outer_sum(state_low, grad_projected)
    grad_input = grad_sum + times_transposed(grad_projected, qkv_full)
    return (
        grad_input,
        (
            qkv_sum,
            out_sum,
            gate_sum,
            up_sum,
            down_sum,
            gain_one_sum,
            bias_one_sum,
            gain_two_sum,
            bias_two_sum,
        ),
    )


def shards(
    inputs,
    segment_ids,
    qkv_weight,
    out_weight,
    gate_weight,
    up_weight,
    down_weight,
    first_gain,
    first_bias,
    second_gain,
    second_bias,
    cotangent,
):
    layers = qkv_weight.shape[0]
    segment_row = segment_ids[0]
    cosine_table, sine_table = rotary_tables(positions_of(segment_row))
    allowed = segment_row[:, None] == segment_row[None, :]
    score_scale = 1.0 / math.sqrt(HEAD)
    hidden_state = inputs[0].astype(jnp.float32)
    fetched = []
    saved = []
    for layer_index in range(layers):
        weights = fetch_forward(
            qkv_weight,
            out_weight,
            gate_weight,
            up_weight,
            down_weight,
            first_gain,
            first_bias,
            second_gain,
            second_bias,
            layer_index,
        )
        fetched.append(weights)
        hidden_state, stored = layer_forward(
            hidden_state, weights, cosine_table, sine_table, allowed, score_scale
        )
        saved.append(stored)
    output = hidden_state.astype(jnp.bfloat16)[None]
    upstream = cotangent[0].astype(jnp.float32)
    shared = [None] * layers
    for layer_index in reversed(range(layers)):
        weights = fetch_backward(
            qkv_weight,
            out_weight,
            gate_weight,
            up_weight,
            down_weight,
            first_gain,
            first_bias,
            second_gain,
            second_bias,
            layer_index,
        )
        upstream, gradients = layer_backward(
            upstream, weights, saved[layer_index], cosine_table, sine_table, allowed, score_scale
        )
        shared[layer_index] = share_gradients(gradients)
    stacked = [
        jnp.stack([shared[layer_index][member] for layer_index in range(layers)])
        for member in range(9)
    ]
    return (
        output,
        upstream[None],
        stacked[0],
        stacked[1],
        stacked[2],
        stacked[3],
        stacked[4],
        stacked[5],
        stacked[6],
        stacked[7],
        stacked[8],
    )


def solution(mesh):
    return jax.shard_map(
        shards,
        mesh=mesh,
        in_specs=(
            P(("rep", "shard"), None, None),
            P(("rep", "shard"), None),
            P(None, "shard", None),
            P(None, "shard", None),
            P(None, "shard", None),
            P(None, "shard", None),
            P(None, "shard", None),
            P(None, "shard"),
            P(None, "shard"),
            P(None, "shard"),
            P(None, "shard"),
            P(("rep", "shard"), None, None),
        ),
        out_specs=(
            P(("rep", "shard"), None, None),
            P(("rep", "shard"), None, None),
            P(None, "shard", None),
            P(None, "shard", None),
            P(None, "shard", None),
            P(None, "shard", None),
            P(None, "shard", None),
            P(None, "shard"),
            P(None, "shard"),
            P(None, "shard"),
            P(None, "shard"),
        ),
        check_vma=False,
    )
```

profile of v0, /device:TPU:0, one launch (start us, length us, event | category | flops | bytes accessed | tf_op | source)
XLA Modules:
  0.0 1743.7 jit_solution(8347732898075794443)
XLA Ops:
  23.4 63.9 %all-reduce.33 = (bf16[768]{0:T(1024)(128)(2,1)S(1)}, bf16[768]{0:T(1024)(128)(2,1)S(1)}, bf16[768]{0:T(1024)(128)(2,1)S(1)}, bf16[768]{0:T(1024)(128)(2,1)S(1)}...) all-reduce(bf16[768]{0:T(1024)(128)(2,1)S(1)} %dynamic-update-slice, ...), channel_id=5, replica_groups=mesh['rep'=2,'shard'=16] {'shard'}, use_global_device_ids=true, to_apply=%add.1 | all-reduce | flops 6144 | bytes 24576
  104.2 51.1 %all-gather.33.cloned.1.call-done = bf16[1,768,3072]{2,1,0:T(8,128)(2,1)} async-done(((bf16[1,48,3072]{2,1,0:T(8,128)(2,1)}), bf16[1,768,3072]{2,1,0:T(8,128)(2,1)}) %all-gather.33.cloned.1.call-update) | async-done | bytes 4718608 | tf_op jit(solution)/shard_map/all_gather | solution.py:177
  160.6 49.2 %all-gather.35.cloned.1.call-done = bf16[1,768,3072]{2,1,0:T(8,128)(2,1)} async-done(((bf16[1,48,3072]{2,1,0:T(8,128)(2,1)}), bf16[1,768,3072]{2,1,0:T(8,128)(2,1)}) %all-gather.35.cloned.1.call-update) | async-done | bytes 4718608 | tf_op jit(solution)/shard_map/all_gather | solution.py:178
  216.5 47.8 %all-gather.37.cloned.1.call-done = bf16[1,3072,768]{2,1,0:T(8,128)(2,1)} async-done(((bf16[1,192,768]{2,1,0:T(8,128)(2,1)}), bf16[1,3072,768]{2,1,0:T(8,128)(2,1)}) %all-gather.37.cloned.1.call-update) | async-done | bytes 4718608 | tf_op jit(solution)/shard_map/all_gather | solution.py:179
  268.4 43.8 %all-gather.39.cloned.1.call-done = bf16[1,768,2304]{2,1,0:T(8,128)(2,1)} async-done(((bf16[1,48,2304]{2,1,0:T(8,128)(2,1)}), bf16[1,768,2304]{2,1,0:T(8,128)(2,1)}) %all-gather.39.cloned.1.call-update) | async-done | bytes 3538960 | tf_op jit(solution)/shard_map/all_gather | solution.py:175
  321.4 10.4 while.57
  331.8 20.1 %all-gather.41.cloned.1.call-done = bf16[1,768,768]{2,1,0:T(8,128)(2,1)} async-done(((bf16[1,48,768]{2,1,0:T(8,128)(2,1)}), bf16[1,768,768]{2,1,0:T(8,128)(2,1)}) %all-gather.41.cloned.1.call-update) | async-done | bytes 1179664 | tf_op jit(solution)/shard_map/all_gather | solution.py:176
  354.3 52.7 %all-gather.43.cloned.1.call-done = bf16[1,768,3072]{2,1,0:T(8,128)(2,1)} async-done(((bf16[1,48,3072]{2,1,0:T(8,128)(2,1)}), bf16[1,768,3072]{2,1,0:T(8,128)(2,1)}) %all-gather.43.cloned.1.call-update) | async-done | bytes 4718608 | tf_op jit(solution)/shard_map/all_gather | solution.py:177
  412.4 49.3 %all-gather.45.cloned.1.call-done = bf16[1,768,3072]{2,1,0:T(8,128)(2,1)} async-done(((bf16[1,48,3072]{2,1,0:T(8,128)(2,1)}), bf16[1,768,3072]{2,1,0:T(8,128)(2,1)}) %all-gather.45.cloned.1.call-update) | async-done | bytes 4718608 | tf_op jit(solution)/shard_map/all_gather | solution.py:178
  461.7 7.2 multiply_convert_fusion.6
  468.8 47.4 %all-gather.47.cloned.1.call-done = bf16[1,3072,768]{2,1,0:T(8,128)(2,1)} async-done(((bf16[1,192,768]{2,1,0:T(8,128)(2,1)}), bf16[1,3072,768]{2,1,0:T(8,128)(2,1)}) %all-gather.47.cloned.1.call-update) | async-done | bytes 4718608 | tf_op jit(solution)/shard_map/all_gather | solution.py:179
  540.2 35.9 %while.58 = (s32[]{:T(128)}, f32[6,256,128]{1,2,0:T(8,128)}, f32[6,256,128]{1,2,0:T(8,128)}, bf16[6,256,128]{1,2,0:T(8,128)(2,1)S(1)}, bf16[6,256,128]{1,2,0:T(8...) while((s32[]{:T(128)}, f32[6,256,128]{1,2,0:T(8,128)}, ...), condition=%wide.region_24.25_spmd.clone, body=%wide.region_22.24_spmd.clone.sunk | while | flops 85196288 | bytes 6040721 | solution.py:388
  614.6 37.1 %while.59 = (s32[]{:T(128)}, f32[6,256,128]{1,2,0:T(8,128)S(1)}, f32[6,256,128]{1,2,0:T(8,128)}, bf16[6,256,128]{1,2,0:T(8,128)(2,1)S(1)}, bf16[6,256,128]{1,2,0...) while((s32[]{:T(128)}, f32[6,256,128]{1,2,0:T(8,128)S(1)}, ...), condition=%wide.region_31.32_spmd.clone, body=%wide.region_29.31_spmd.clone.sunk | while | flops 85196288 | bytes 6040721 | solution.py:388
  657.1 8.2 copy.99
  695.1 15.8 reduce-scatter.29.cloned.1.call-done
  719.4 84.6 %reduce-scatter.65.cloned.1.call-done = f32[48,2304]{1,0:T(8,128)} async-done(((f32[768,2304]{1,0:T(8,128)}), f32[48,2304]{1,0:T(8,128)}) %reduce-scatter.65.cloned.1.call-update) | async-done | bytes 442384
  806.4 91.6 %reduce-scatter.61.cloned.1.call-done = f32[48,2304]{1,0:T(8,128)} async-done(((f32[768,2304]{1,0:T(8,128)}), f32[48,2304]{1,0:T(8,128)}) %reduce-scatter.61.cloned.1.call-update) | async-done | bytes 442384
  907.1 105.7 %reduce-scatter.41.cloned.1.call-done = f32[48,3072]{1,0:T(8,128)} async-done(((f32[768,3072]{1,0:T(8,128)}), f32[48,3072]{1,0:T(8,128)}) %reduce-scatter.41.cloned.1.call-update) | async-done | bytes 589840 | tf_op jit(solution)/shard_map/reduce_scatter | solution.py:216
  1014.6 113.8 %reduce-scatter.37.cloned.1.call-done = f32[48,3072]{1,0:T(8,128)} async-done(((f32[768,3072]{1,0:T(8,128)}), f32[48,3072]{1,0:T(8,128)}) %reduce-scatter.37.cloned.1.call-update) | async-done | bytes 589840 | tf_op jit(solution)/shard_map/reduce_scatter | solution.py:216
  1130.3 113.2 %reduce-scatter.49.cloned.1.call-done = f32[48,3072]{1,0:T(8,128)} async-done(((f32[768,3072]{1,0:T(8,128)}), f32[48,3072]{1,0:T(8,128)}) %reduce-scatter.49.cloned.1.call-update) | async-done | bytes 589840 | tf_op jit(solution)/shard_map/reduce_scatter | solution.py:217
  1247.4 62.3 %all-reduce.32 = (bf16[768]{0:T(1024)(128)(2,1)S(1)}, bf16[768]{0:T(1024)(128)(2,1)S(1)}, bf16[768]{0:T(1024)(128)(2,1)S(1)}, bf16[768]{0:T(1024)(128)(2,1)S(1)}...) all-reduce(f32[768]{0:T(1024)S(1)} %copy-done.73, ...), channel_id=42, replica_groups=mesh['rep'=2,'shard'=16] {'shard'}, use_global_device_ids=true, to_apply=%region_56.57.clone | all-reduce | flops 6144 | bytes 36864
  1323.6 35.8 %reduce-scatter.45.cloned.1.call-done = f32[48,3072]{1,0:T(8,128)} async-done(((f32[768,3072]{1,0:T(8,128)}), f32[48,3072]{1,0:T(8,128)}) %reduce-scatter.45.cloned.1.call-update) | async-done | bytes 589840 | tf_op jit(solution)/shard_map/reduce_scatter | solution.py:217
  1376.7 7.2 reduce-scatter.31.cloned.1.call-done
  1388.7 110.7 %reduce-scatter.57.cloned.1.call-done = f32[192,768]{1,0:T(8,128)} async-done(((f32[3072,768]{1,0:T(8,128)}), f32[192,768]{1,0:T(8,128)}) %reduce-scatter.57.cloned.1.call-update) | async-done | bytes 589840 | tf_op jit(solution)/shard_map/reduce_scatter | solution.py:218
  1502.0 10.7 reduce-scatter.67.cloned.1.call-done
  1518.4 7.9 reduce-scatter.63.cloned.1.call-done
  1532.9 109.2 %reduce-scatter.53.cloned.1.call-done = f32[192,768]{1,0:T(8,128)} async-done(((f32[3072,768]{1,0:T(8,128)}), f32[192,768]{1,0:T(8,128)}) %reduce-scatter.53.cloned.1.call-update) | async-done | bytes 589840 | tf_op jit(solution)/shard_map/reduce_scatter | solution.py:218
  1644.0 12.8 reduce-scatter.43.cloned.1.call-done
  1663.3 8.3 reduce-scatter.39.cloned.1.call-done
  1678.0 8.3 reduce-scatter.51.cloned.1.call-done
  1692.7 7.8 reduce-scatter.47.cloned.1.call-done
  1707.0 7.8 reduce-scatter.59.cloned.1.call-done
  (708 shorter events, 373.3 us)
Async XLA Ops:
  7.2 83.8 %all-gather.29.cloned.1.call-start = ((), (), s32[]{:S(2)}) async-start(), calls=%async_computation.36 | async-start | bytes 3760128 | tf_op jit(solution)/shard_map/all_gather | solution.py:175
  9.2 91.9 %all-gather.31.cloned.1.call-start = ((), (), s32[]{:S(2)}) async-start(), calls=%async_computation.37 | async-start | bytes 1253376 | tf_op jit(solution)/shard_map/all_gather | solution.py:176
  10.9 144.4 %all-gather.33.cloned.1.call-start = ((), (), s32[]{:S(2)}) async-start(), calls=%async_computation.38 | async-start | bytes 5013504 | tf_op jit(solution)/shard_map/all_gather | solution.py:177
  12.9 196.9 %all-gather.35.cloned.1.call-start = ((), (), s32[]{:S(2)}) async-start(), calls=%async_computation.39 | async-start | bytes 5013504 | tf_op jit(solution)/shard_map/all_gather | solution.py:178
  13.9 250.5 %all-gather.37.cloned.1.call-start = ((), (), s32[]{:S(2)}) async-start(), calls=%async_computation.40 | async-start | bytes 5013504 | tf_op jit(solution)/shard_map/all_gather | solution.py:179
  14.8 297.4 %all-gather.39.cloned.1.call-start = ((), (), s32[]{:S(2)}) async-start(), calls=%async_computation.41 | async-start | bytes 3760128 | tf_op jit(solution)/shard_map/all_gather | solution.py:175
  15.4 336.5 %all-gather.41.cloned.1.call-start = ((), (), s32[]{:S(2)}) async-start(), calls=%async_computation.42 | async-start | bytes 1253376 | tf_op jit(solution)/shard_map/all_gather | solution.py:176
  16.1 390.9 %all-gather.43.cloned.1.call-start = ((), (), s32[]{:S(2)}) async-start(), calls=%async_computation.43 | async-start | bytes 5013504 | tf_op jit(solution)/shard_map/all_gather | solution.py:177
  16.9 444.8 %all-gather.45.cloned.1.call-start = ((), (), s32[]{:S(2)}) async-start(), calls=%async_computation.44 | async-start | bytes 5013504 | tf_op jit(solution)/shard_map/all_gather | solution.py:178
  17.6 498.6 %all-gather.47.cloned.1.call-start = ((), (), s32[]{:S(2)}) async-start(), calls=%async_computation.45 | async-start | bytes 5013504 | tf_op jit(solution)/shard_map/all_gather | solution.py:179
  18.2 675.3 %reduce-scatter.33.cloned.1.call-start = ((), (), s32[]{:S(2)}) async-start(), calls=%async_computation.22 | async-start | bytes 2506752 | tf_op jit(solution)/shard_map/reduce_scatter | solution.py:215
  583.0 127.9 %reduce-scatter.29.cloned.1.call-start = ((), (), s32[]{:S(2)}) async-start(), calls=%async_computation.20 | async-start | bytes 2506752 | tf_op jit(solution)/shard_map/reduce_scatter | solution.py:215
  604.1 200.0 %reduce-scatter.65.cloned.1.call-start = ((), (), s32[]{:S(2)}) async-start(), calls=%async_computation.48 | async-start | bytes 7520256
  613.5 284.4 %reduce-scatter.61.cloned.1.call-start = ((), (), s32[]{:S(2)}) async-start(), calls=%async_computation.46 | async-start | bytes 7520256
  665.3 347.5 %reduce-scatter.41.cloned.1.call-start = ((), (), s32[]{:S(2)}) async-start(), calls=%async_computation.26 | async-start | bytes 10027008 | tf_op jit(solution)/shard_map/reduce_scatter | solution.py:216
  672.8 455.7 %reduce-scatter.37.cloned.1.call-start = ((), (), s32[]{:S(2)}) async-start(), calls=%async_computation.24 | async-start | bytes 10027008 | tf_op jit(solution)/shard_map/reduce_scatter | solution.py:216
  680.2 563.3 %reduce-scatter.49.cloned.1.call-start = ((), (), s32[]{:S(2)}) async-start(), calls=%async_computation.30 | async-start | bytes 10027008 | tf_op jit(solution)/shard_map/reduce_scatter | solution.py:217
  686.8 672.6 %reduce-scatter.45.cloned.1.call-start = ((), (), s32[]{:S(2)}) async-start(), calls=%async_computation.28 | async-start | bytes 10027008 | tf_op jit(solution)/shard_map/reduce_scatter | solution.py:217
  693.4 678.4 %reduce-scatter.35.cloned.1.call-start = ((), (), s32[]{:S(2)}) async-start(), calls=%async_computation.23 | async-start | bytes 110592 | tf_op jit(solution)/shard_map/reduce_scatter | solution.py:228
  695.1 688.8 %reduce-scatter.31.cloned.1.call-start = ((), (), s32[]{:S(2)}) async-start(), calls=%async_computation.21 | async-start | bytes 110592 | tf_op jit(solution)/shard_map/reduce_scatter | solution.py:228
  712.5 786.9 %reduce-scatter.57.cloned.1.call-start = ((), (), s32[]{:S(2)}) async-start(), calls=%async_computation.34 | async-start | bytes 10027008 | tf_op jit(solution)/shard_map/reduce_scatter | solution.py:218
  719.4 793.3 %reduce-scatter.67.cloned.1.call-start = ((), (), s32[]{:S(2)}) async-start(), calls=%async_computation.49 | async-start | bytes 331776 | tf_op jit(solution)/shard_map/reduce_scatter | solution.py:225
  806.3 720.0 %reduce-scatter.63.cloned.1.call-start = ((), (), s32[]{:S(2)}) async-start(), calls=%async_computation.47 | async-start | bytes 331776 | tf_op jit(solution)/shard_map/reduce_scatter | solution.py:225
  900.2 742.0 %reduce-scatter.53.cloned.1.call-start = ((), (), s32[]{:S(2)}) async-start(), calls=%async_computation.32 | async-start | bytes 10027008 | tf_op jit(solution)/shard_map/reduce_scatter | solution.py:218
  907.0 340.4 %copy-start.62 = (f32[768]{0:T(1024)S(1)}, f32[768]{0:T(1024)}, u32[]{:S(2)}) copy-start(f32[768]{0:T(1024)} %get-tuple-element.313) | copy-start | bytes 9220
  907.0 455.4 %copy-start.29 = (bf16[256,12,64]{0,2,1:T(8,128)(2,1)S(1)}, bf16[256,12,64]{0,2,1:T(8,128)(2,1)}, u32[]{:S(2)}) copy-start(bf16[256,12,64]{0,2,1:T(8,128)(2,1)} %copy-done.28) | copy-start | bytes 1179652
  907.0 749.8 %reduce-scatter.43.cloned.1.call-start = ((), (), s32[]{:S(2)}) async-start(), calls=%async_computation.27 | async-start | bytes 442368 | tf_op jit(solution)/shard_map/reduce_scatter | solution.py:231
  1014.6 657.0 %reduce-scatter.39.cloned.1.call-start = ((), (), s32[]{:S(2)}) async-start(), calls=%async_computation.25 | async-start | bytes 442368 | tf_op jit(solution)/shard_map/reduce_scatter | solution.py:231
  1130.3 556.0 %reduce-scatter.51.cloned.1.call-start = ((), (), s32[]{:S(2)}) async-start(), calls=%async_computation.31 | async-start | bytes 442368 | tf_op jit(solution)/shard_map/reduce_scatter | solution.py:234
  1245.3 455.2 %reduce-scatter.47.cloned.1.call-start = ((), (), s32[]{:S(2)}) async-start(), calls=%async_computation.29 | async-start | bytes 442368 | tf_op jit(solution)/shard_map/reduce_scatter | solution.py:234
  1361.3 353.6 %reduce-scatter.59.cloned.1.call-start = ((), (), s32[]{:S(2)}) async-start(), calls=%async_computation.35 | async-start | bytes 442368 | tf_op jit(solution)/shard_map/reduce_scatter | solution.py:237
  1501.2 227.8 %reduce-scatter.55.cloned.1.call-start = ((), (), s32[]{:S(2)}) async-start(), calls=%async_computation.33 | async-start | bytes 442368 | tf_op jit(solution)/shard_map/reduce_scatter | solution.py:237
  (89 other events, 4061.6 us)
Sparse Core Ops, SparseCore 0:
  10.3 49.8 all-gather.28
  62.5 37.5 all-gather.30
  102.9 52.2 all-gather.32
  158.0 51.7 all-gather.34
  212.5 51.7 all-gather.36
  266.4 45.7 all-gather.38
  314.5 37.3 all-gather.40
  354.7 52.1 all-gather.42
  409.8 51.7 all-gather.44
  464.4 51.7 all-gather.46
  583.1 61.6 reduce-scatter.32
  648.9 61.9 reduce-scatter.28
  714.9 89.0 reduce-scatter.64
  808.4 89.4 reduce-scatter.60
  901.9 110.8 reduce-scatter.40
  1017.3 111.1 reduce-scatter.36
  1132.4 111.0 reduce-scatter.48
  1248.0 111.3 reduce-scatter.44
  1362.2 9.6 reduce-scatter.34
  1373.9 9.9 reduce-scatter.30
  1388.0 111.3 reduce-scatter.56
  1501.7 10.9 reduce-scatter.66
  1515.0 11.1 reduce-scatter.62
  1530.8 111.3 reduce-scatter.52
  1645.0 11.8 reduce-scatter.42
  1659.5 12.0 reduce-scatter.38
  1674.2 12.0 reduce-scatter.50
  1688.5 12.0 reduce-scatter.46
  1702.8 12.0 reduce-scatter.58
  1717.0 12.0 reduce-scatter.54
where the time goes:
time: 1750 us; the launch traced here: 1740 us
  waiting for transfers between devices  1230 us (70%)
  blocking collectives  196 us (11%)
  matrix products  155 us (9%)
  local copies, waits for them, and re-layouts  101 us (6%)
  other arithmetic  41.9 us (2%)
  between operations  19.4 us (1%)
    reduce_scatter x2, waiting for transfers between devices, share_gradients(): lax.psum_scatter(gradients[4], 'shard', scatter_dimension=0, tiled=True)  220 us
    reduce_scatter x2, waiting for transfers between devices, share_gradients(): lax.psum_scatter(gradients[2], 'shard', scatter_dimension=0, tiled=True)  219 us
    unnamed x32, waiting for transfers between devices  180 us
    reduce_scatter x2, waiting for transfers between devices, share_gradients(): lax.psum_scatter(gradients[3], 'shard', scatter_dimension=0, tiled=True)  149 us
    unnamed x4, blocking collectives  136 us
    all_gather x2, waiting for transfers between devices, fetch_forward(): lax.all_gather(gate_weight[layer_index], 'shard', axis=0, tiled=True)  104 us
    all_gather x2, waiting for transfers between devices, fetch_forward(): lax.all_gather(up_weight[layer_index], 'shard', axis=0, tiled=True)  98.5 us
    all_gather x2, waiting for transfers between devices, fetch_forward(): lax.all_gather(down_weight[layer_index], 'shard', axis=0, tiled=True)  95.2 us
  transfers between devices with their start and end apart: 30, of which 27 were waited for; matrix products, arithmetic and copies ran while one was open for 13% of the time, Pallas kernels for 0%

commit v1 on v0

--- a/solution.py
+++ b/solution.py
@@ -1,17 +1,861 @@
+import functools
 import math
 
 import jax
 import jax.numpy as jnp
 from jax import lax
+from jax.experimental import pallas as pl
+from jax.experimental.pallas import tpu as pltpu
 from jax.sharding import PartitionSpec as P
 
 HEADS = 12
 HEAD = 64
-
-
 eps_norm = 1e-12
 rope_base = 1000.0
 masked_score = -1e30
+MESH = pl.DeviceIdType.MESH
+BF = jnp.bfloat16
+F32 = jnp.float32
+T = 256
+D = 768
+G = 8
+QW = 1152
+OW = 384
+AW = QW + OW + 128
+FS = 768
+PAIRS = HEADS // 2
+
+
+def dot(a, b):
+    return jnp.dot(a, b, preferred_element_type=F32)
+
+
+def dot_t(a, b):
+    return lax.dot_general(a, b, (((1,), (1,)), ((), ())), preferred_element_type=F32)
+
+
+def tile(j, width):
+    return pl.ds(pl.multiple_of(j * width, width), width)
+
+
+def chip_rows(g):
+    return pl.ds(pl.multiple_of(g * 96, 96), 96)
+
+
+def shard_rows(g, c):
+    return pl.ds(pl.multiple_of(g * 96 + c * 48, 48), 48)
+
+
+class Place:
+    def __init__(self):
+        self.y = lax.axis_index("rep")
+        s = lax.axis_index("shard")
+        self.c, self.x, self.z = s % 2, (s // 2) % 2, s // 4
+        self.g = s // 2
+        self.slot = 2 * self.y + self.c
+
+    def at(self, y, z, x, c):
+        return (y, z * 4 + x * 2 + c)
+
+    def core(self):
+        return self.at(self.y, self.z, self.x, 1 - self.c)
+
+    def xside(self):
+        return self.at(self.y, self.z, 1 - self.x, self.c)
+
+    def yside(self):
+        return self.at(1 - self.y, self.z, self.x, self.c)
+
+    def zside(self, k):
+        return self.at(self.y, (self.z + k) % 4, self.x, self.c)
+
+    def chip(self, k, x):
+        return 2 * ((self.z + 4 - k) % 4) + x
+
+    def everyone(self):
+        return [self.core(), self.xside(), self.yside()] + [self.zside(k) for k in (1, 2, 3)]
+
+
+def greet(place):
+    barrier = pltpu.get_barrier_semaphore()
+    for who in place.everyone():
+        pl.semaphore_signal(barrier, inc=1, device_id=who, device_id_type=MESH)
+    pl.semaphore_wait(barrier, 6)
+
+
+class Mail:
+    def __init__(self):
+        self.sent = []
+
+    def send(self, src, dst, send_sem, recv_sem, who, tag=None):
+        copy = pltpu.make_async_remote_copy(src, dst, send_sem, recv_sem, device_id=who, device_id_type=MESH)
+        copy.start()
+        self.sent.append((tag, copy))
+
+    def local(self, src, dst, sem):
+        copy = pltpu.make_async_copy(src, dst, sem)
+        copy.start()
+        return copy
+
+    def arrive(self, dst, send_sem, recv_sem, who):
+        pltpu.make_async_remote_copy(dst, dst, send_sem, recv_sem, device_id=who, device_id_type=MESH).wait_recv()
+
+    def gone(self, tag):
+        for t, copy in self.sent:
+            if t == tag:
+                copy.wait_send()
+        self.sent = [(t, copy) for t, copy in self.sent if t != tag]
+
+    def finish(self):
+        for _, copy in self.sent:
+            copy.wait_send()
+        self.sent = []
+
+
+def swap_halves(v, low_half):
+    return jnp.where(low_half, pltpu.roll(v, 96, 1), pltpu.roll(v, 32, 1))
+
+
+def head_mask(rows, width):
+    return lax.broadcasted_iota(jnp.int32, (rows, width), 1) % 128 < HEAD
+
+
+def forward_kernel(
+    x_ref, cos_ref, sin_ref, segc_ref, segr_ref, qkv_ref, outw_ref, par_ref, gu_ref, dn_ref,
+    y_ref, A_o, F_o, Q_o, ST_o, P_o, TG_o, TT_o, N_o, I_o, PV_o,
+    A, F, Q, ST, Pb, TG, TT, N, I, PV, S, AT, MF, AC, H, bias, FD, RC, RY,
+    ls, s_gu, r_gu, s_az, r_az, s_ax, r_ax, s_ay, r_ay, s_ac, r_ac, s_fz, r_fz, s_fx, r_fx,
+    s_m, r_m, s_rc, r_rc, s_ry, r_ry, os,
+):
+    pc = Place()
+    y, z, x, c, g, slot = pc.y, pc.z, pc.x, pc.c, pc.g, pc.slot
+    ml = Mail()
+    LAY = (0, 1)
+    ks = (1, 3, 2)
+
+    own_a, own_f = [], []
+    for l in LAY:
+        own_a.append([])
+        for h in range(2):
+            dst = A.at[l, h, g, c]
+            own_a[l].append(ml.local(qkv_ref.at[l, :, pl.ds(QW * h, QW)], dst.at[:, pl.ds(0, QW)], ls.at[l, h]))
+            own_a[l].append(ml.local(outw_ref.at[l, :, pl.ds(OW * h, OW)], dst.at[:, pl.ds(QW, OW)], ls.at[l, 2 + h]))
+            own_a[l].append(ml.local(par_ref.at[l, h], dst.at[:, pl.ds(QW + OW, 128)], ls.at[l, 4 + h]))
+        own_f.append([
+            ml.local(gu_ref.at[l, c, y], F.at[l, shard_rows(g, c), pl.ds(0, 2 * FS)], ls.at[l, 6]),
+            ml.local(dn_ref.at[l, y], F.at[l, chip_rows(g), pl.ds(2 * FS, D)], ls.at[l, 7]),
+        ])
+    greet(pc)
+
+    def gu_send(l):
+        ml.send(gu_ref.at[l, 1 - c, y], F.at[l, shard_rows(g, c), pl.ds(0, 2 * FS)], s_gu.at[l], r_gu.at[l], pc.core())
+
+    def gu_arrive(l):
+        ml.arrive(F.at[l, shard_rows(g, 1 - c), pl.ds(0, 2 * FS)], s_gu.at[l], r_gu.at[l], pc.core())
+
+    def a_own(l):
+        for copy in own_a[l]:
+            copy.wait()
+        block = A.at[l, y, g, c]
+        for i in ks:
+            ml.send(block, block, s_az.at[l, i], r_az.at[l, i], pc.zside(i))
+        ml.send(block, block, s_ax.at[l, 0], r_ax.at[l, 0], pc.xside())
+
+    def a_z(l, k):
+        block = A.at[l, y, pc.chip(k, x), c]
+        ml.arrive(block, s_az.at[l, k], r_az.at[l, k], pc.zside(k))
+        ml.send(block, block, s_ax.at[l, k], r_ax.at[l, k], pc.xside())
+        ml.send(block, block, s_ay.at[l, k], r_ay.at[l, k], pc.yside())
+
+    def a_x(l, k):
+        block = A.at[l, y, pc.chip(k, 1 - x), c]
+        ml.arrive(block, s_ax.at[l, k], r_ax.at[l, k], pc.xside())
+        ml.send(block, block, s_ay.at[l, 4 + k], r_ay.at[l, 4 + k], pc.yside())
+
+    def a_c(l, h):
+        block = A.at[l, h, :, c]
+        ml.send(block, block, s_ac.at[l, h], r_ac.at[l, h], pc.core())
+
+    def a_y(l, k, xx, j):
+        ml.arrive(A.at[l, 1 - y, pc.chip(k, xx), c], s_ay.at[l, j], r_ay.at[l, j], pc.yside())
+
+    def a_c_arrive(l, h):
+        ml.arrive(A.at[l, h, :, 1 - c], s_ac.at[l, h], r_ac.at[l, h], pc.core())
+
+    def f_own(l):
+        for copy in own_f[l]:
+            copy.wait()
+        gu_arrive(l)
+        block = F.at[l, chip_rows(g)]
+        for i in ks:
+            ml.send(block, block, s_fz.at[l, i], r_fz.at[l, i], pc.zside(i))
+        ml.send(block, block, s_fx.at[l, 0], r_fx.at[l, 0], pc.xside())
+
+    def f_z(l, k):
+        block = F.at[l, chip_rows(pc.chip(k, x))]
+        ml.arrive(block, s_fz.at[l, k], r_fz.at[l, k], pc.zside(k))
+        ml.send(block, block, s_fx.at[l, k], r_fx.at[l, k], pc.xside())
+
+    def f_x(l, k):
+        ml.arrive(F.at[l, chip_rows(pc.chip(k, 1 - x))], s_fx.at[l, k], r_fx.at[l, k], pc.xside())
+
+    def attn_gather(l):
+        for k in ks:
+            a_z(l, k)
+        for k in (0,) + ks:
+            a_x(l, k)
+        a_c(l, y)
+
+    def attn_ready(l):
+        for k in ks:
+            a_y(l, k, x, k)
+        for k in (0,) + ks:
+            a_y(l, k, 1 - x, 4 + k)
+        a_c(l, 1 - y)
+        a_c_arrive(l, y)
+        a_c_arrive(l, 1 - y)
+
+    out_copies = []
+
+    def save(src, dst, i):
+        out_copies.append(ml.local(src, dst, os.at[i]))
+
+    pair_mask = head_mask(T, 128)
+    low_half = lax.broadcasted_iota(jnp.int32, (T, 128), 1) % HEAD < HEAD // 2
+    onehot = (lax.broadcasted_iota(jnp.int32, (8, 128), 0) == lax.broadcasted_iota(jnp.int32, (8, 128), 1)).astype(F32).astype(BF)
+
+    def project(l):
+        st = S[...]
+        cos, sin = cos_ref[...], sin_ref[...]
+        for j in range(6):
+            h, off = j // 3, (j % 3) * 384
+            w = A[l, h, :, :, :, off:off + 384].reshape(D, 384)
+            r = dot(st, w)
+            kind = j // 2
+            for t in range(3):
+                v = r[:, 128 * t:128 * t + 128]
+                if kind < 2:
+                    v = v * cos + swap_halves(v, low_half) * sin
+                col = (j % 2) * 384 + 128 * t
+                Q[l, kind, :, col:col + 128] = v.astype(BF)
+
+    def attention(l):
+        def pair(p, carry):
+            cols = tile(p, 128)
+            q, kk, v = Q[l, 0, :, cols], Q[l, 1, :, cols], Q[l, 2, :, cols]
+            outs = []
+            for h in range(2):
+                qh = jnp.where(pair_mask == (h == 0), q, jnp.zeros_like(q))
+                s = dot_t(qh, kk) * 0.125 + bias[...]
+                e = jnp.exp(s - jnp.max(s, axis=1, keepdims=True))
+                pr = (e * (1.0 / jnp.sum(e, axis=1, keepdims=True))).astype(BF)
+                Pb[l, 2 * p + h] = pr
+                outs.append(dot(pr, v))
+            AT[:, cols] = jnp.where(pair_mask, outs[0], outs[1]).astype(BF)
+            return carry
+        lax.fori_loop(0, PAIRS, pair, 0)
+
+    def params(l):
+        for h in range(2):
+            w = A[l, h, :, :, :, QW + OW:].reshape(D, 128)
+            PV[l, h] = dot_t(onehot, w)
+
+    def out_project(l):
+        for h in range(2):
+            w = A[l, h, :, :, :, QW:QW + OW].reshape(D, OW)
+            H[:, h * OW:h * OW + OW] = H[:, h * OW:h * OW + OW] + dot(AT[...], w)
+
+    def norm(l, i, dst, extra):
+        gain, shift = PV[l, i, 0:1, :], PV[l, i, 1:2, :]
+        def rows_of(j, carry):
+            rows = tile(j, 32)
+            v = H[rows, :]
+            if extra is not None:
+                v = v + extra(rows)
+            cen = v - jnp.mean(v, axis=1, keepdims=True)
+            inv = lax.rsqrt(jnp.mean(cen * cen, axis=1, keepdims=True) + eps_norm)
+            n = cen * inv
+            N[l, i, rows, :] = n
+            I[l, i, rows, :] = jnp.broadcast_to(inv, (32, 128))
+            m = n * gain + shift
+            H[rows, :] = m
+            dst[rows, :] = m.astype(BF)
+            return carry
+        lax.fori_loop(0, T // 32, rows_of, 0)
+
+    def ffn_up(l, yy):
+        two = pl.ds(2 * yy, 2)
+        def cols_of(j, carry):
+            cols = tile(j, 256)
+            xx = MF[l, two].reshape(2 * T, D)
+            gate = dot(xx, F[l, :, cols])
+            up = dot(xx, F[l, :, pl.ds(pl.multiple_of(FS + j * 256, 256), 256)])
+            act = gate * jax.nn.sigmoid(gate) * up
+            TG[l, 0, two, :, cols] = gate.astype(BF).reshape(2, T, 256)
+            TG[l, 1, two, :, cols] = up.astype(BF).reshape(2, T, 256)
+            AC[two, :, cols] = act.astype(BF).reshape(2, T, 256)
+            return carry
+        lax.fori_loop(0, FS // 256, cols_of, 0)
+
+    def ffn_down(l, yy, cc, add):
+        s_ = 2 * yy + cc
+        def cols_of(j, carry):
+            cols = tile(j, 256)
+            w = F[l, :, pl.ds(pl.multiple_of(2 * FS + j * 256, 256), 256)]
+            r = dot(AC[s_], w)
+            if add:
+                r = r + RC[l, yy, :, cols].astype(F32)
+            FD[l, s_, :, cols] = r.astype(BF)
+            return carry
+        lax.fori_loop(0, D // 256, cols_of, 0)
+
+    def turn(src, dst, col):
+        def tile_of(j, carry):
+            cols = tile(j, 128)
+            dst[cols, pl.ds(pl.multiple_of(col, T), T)] = src[:, cols].T
+            return carry
+        lax.fori_loop(0, D // 128, tile_of, 0)
+
+    def turn_slots(src, dst):
+        def slot_of(i, carry):
+            turn(src.at[i], dst, i * T)
+            return carry
+        lax.fori_loop(0, 4, slot_of, 0)
+
+    def mid_exchange(l):
+        mine = MF.at[l, slot]
+        ml.send(mine, mine, s_m.at[l, 0], r_m.at[l, 0], pc.yside())
+        ml.send(mine, mine, s_m.at[l, 1], r_m.at[l, 1], pc.core())
+
+    def feed_forward(l):
+        other_y = MF.at[l, 2 * (1 - y) + c]
+        ml.arrive(MF.at[l, 2 * y + 1 - c], s_m.at[l, 1], r_m.at[l, 1], pc.core())
+        ffn_up(l, y)
+        ml.arrive(other_y, s_m.at[l, 0], r_m.at[l, 0], pc.yside())
+        ml.send(other_y, other_y, s_m.at[l, 2], r_m.at[l, 2], pc.core())
+        ml.arrive(MF.at[l, 2 * (1 - y) + 1 - c], s_m.at[l, 2], r_m.at[l, 2], pc.core())
+        ffn_up(l, 1 - y)
+        def to_core(i, yy):
+            ffn_down(l, yy, 1 - c, False)
+            ml.send(FD.at[l, 2 * yy + 1 - c], RC.at[l, yy], s_rc.at[l, i], r_rc.at[l, i], pc.core())
+        to_core(0, 1 - y)
+        ml.arrive(RC.at[l, 1 - y], s_rc.at[l, 0], r_rc.at[l, 0], pc.core())
+        ffn_down(l, 1 - y, c, True)
+        ml.send(FD.at[l, 2 * (1 - y) + c], RY.at[l], s_ry.at[l], r_ry.at[l], pc.yside())
+        to_core(1, y)
+        ml.arrive(RC.at[l, y], s_rc.at[l, 1], r_rc.at[l, 1], pc.core())
+        ffn_down(l, y, c, True)
+        turn_slots(MF.at[l], TT.at[l, 0])
+        turn_slots(AC, TT.at[l, 1])
+        ml.arrive(RY.at[l], s_ry.at[l], r_ry.at[l], pc.yside())
+
+    gu_send(0)
+    gu_send(1)
+    a_own(0)
+    a_own(1)
+    bias[...] = jnp.where(segc_ref[:, 0:1] == segr_ref[0:1, :], 0.0, masked_score)
+    H[...] = x_ref[...].astype(F32)
+    S[...] = x_ref[...]
+    attn_gather(0)
+    f_own(0)
+    attn_gather(1)
+    f_own(1)
+    attn_ready(0)
+    for l in LAY:
+        if l == 1:
+            attn_ready(1)
+        params(l)
+        project(l)
+        turn(S, ST.at[l, 0], 0)
+        attention(l)
+        if l == 0:
+            for k in ks:
+                f_z(0, k)
+        out_project(l)
+        norm(l, 0, MF.at[l, slot], None)
+        mid_exchange(l)
+        turn(AT, ST.at[l, 1], 0)
+        if l == 0:
+            for k in (0,) + ks:
+                f_x(0, k)
+        else:
+            for k in ks:
+                f_z(1, k)
+            for k in (0,) + ks:
+                f_x(1, k)
+        feed_forward(l)
+        extra = lambda rows, l=l: FD[l, slot, rows, :].astype(F32) + RY[l, rows, :].astype(F32)
+        norm(l, 1, y_ref if l == 1 else S, extra)
+    for i, (src, dst) in enumerate([(A, A_o), (F, F_o), (Q, Q_o), (ST, ST_o), (Pb, P_o), (TG, TG_o), (TT, TT_o), (N, N_o), (I, I_o), (PV, PV_o)]):
+        save(src, dst, i)
+    for copy in out_copies:
+        copy.wait()
+    ml.finish()
+
+
+FWD_SHAPES = [
+    ((2, 2, G, 2, 48, AW), BF),
+    ((2, D, 2 * FS + D), BF),
+    ((2, 3, T, D), BF),
+    ((2, 2, D, T), BF),
+    ((2, HEADS, T, T), BF),
+    ((2, 2, 4, T, FS), BF),
+    ((2, 2, D, 4 * T), BF),
+    ((2, 2, T, D), F32),
+    ((2, 2, T, 128), F32),
+    ((2, 2, 8, D), F32),
+]
+
+
+def sems(*shape):
+    return pltpu.SemaphoreType.DMA(shape)
+
+
+def forward_call(args):
+    any_spec = pl.BlockSpec(memory_space=pl.ANY)
+    vm = pl.BlockSpec(memory_space=pltpu.VMEM)
+    return pl.pallas_call(
+        forward_kernel,
+        out_shape=[jax.ShapeDtypeStruct((T, D), BF)] + [jax.ShapeDtypeStruct(s, d) for s, d in FWD_SHAPES],
+        in_specs=[vm] * 5 + [any_spec] * 5,
+        out_specs=[vm] + [any_spec] * len(FWD_SHAPES),
+        scratch_shapes=[pltpu.VMEM(s, d) for s, d in FWD_SHAPES]
+        + [
+            pltpu.VMEM((T, D), BF),
+            pltpu.VMEM((T, D), BF),
+            pltpu.VMEM((2, 4, T, D), BF),
+            pltpu.VMEM((4, T, FS), BF),
+            pltpu.VMEM((T, D), F32),
+            pltpu.VMEM((T, T), F32),
+            pltpu.VMEM((2, 4, T, D), BF),
+            pltpu.VMEM((2, 2, T, D), BF),
+            pltpu.VMEM((2, T, D), BF),
+            sems(2, 8),
+            sems(2), sems(2),
+            sems(2, 4), sems(2, 4),
+            sems(2, 4), sems(2, 4),
+            sems(2, 8), sems(2, 8),
+            sems(2, 2), sems(2, 2),
+            sems(2, 4), sems(2, 4),
+            sems(2, 4), sems(2, 4),
+            sems(2, 3), sems(2, 3),
+            sems(2, 2), sems(2, 2),
+            sems(2), sems(2),
+            sems(len(FWD_SHAPES)),
+        ],
+        compiler_params=pltpu.CompilerParams(collective_id=0, has_side_effects=True, vmem_limit_bytes=60 * 2**20),
+        cost_estimate=pl.CostEstimate(flops=10**10, bytes_accessed=10**8, transcendentals=0),
+        name="forward",
+    )(*args)
+
+
+def backward_kernel(
+    cot_ref, cos_ref, sin_ref, A_i, F_i, Q_i, ST_i, P_i, TG_i, TT_i, N_i, I_i, PV_i,
+    gin_ref, GUG, DNG, AF,
+    A, F, Q, ST, Pb, TG, TT, N, I, PV,
+    U, GF, GB, GA, GP, FD, RC, RY, FG, RFX, RFZ, FR, AG, RAC, RAY, RAX, RAZ, V,
+    ls, s_m, r_m, s_rc, r_rc, s_ry, r_ry,
+    s_fx, r_fx, s_fz, r_fz, s_fc, r_fc, s_fy, r_fy,
+    s_ac, r_ac, s_ay, r_ay, s_ax, r_ax, s_az, r_az, s_af, r_af,
+):
+    pc = Place()
+    y, z, x, c, slot = pc.y, pc.z, pc.x, pc.c, pc.slot
+    ml = Mail()
+    ks = (1, 3, 2)
+    places = {
+        "PV": (PV_i, PV, 0), "N": (N_i, N, 1), "I": (I_i, I, 2), "TT": (TT_i, TT, 3), "F": (F_i, F, 4), "TG": (TG_i, TG, 5),
+        "ST": (ST_i, ST, 6), "A": (A_i, A, 7), "P": (P_i, Pb, 8), "Q": (Q_i, Q, 9),
+    }
+    loading = {}
+
+    def load(l, *names):
+        for name in names:
+            src, dst, i = places[name]
+            loading[name] = ml.local(src.at[l], dst, ls.at[i])
+
+    def need(*names):
+        for name in names:
+            if name in loading:
+                loading.pop(name).wait()
+
+    load(1, "PV", "N", "I", "TT", "F", "TG", "ST", "A", "P", "Q")
+    U[...] = cot_ref[...].astype(F32)
+    greet(pc)
+
+    fcols = (pl.ds(2 * FS, D), pl.ds(0, FS), pl.ds(FS, FS))
+
+    def fx_send(l, j):
+        ml.send(FG.at[:, 1 - x, :, fcols[j]], RFX.at[l, j], s_fx.at[l, j], r_fx.at[l, j], pc.xside(), ("fx", l, j))
+
+    def fx_task(l, j):
+        ml.arrive(RFX.at[l, j], s_fx.at[l, j], r_fx.at[l, j], pc.xside())
+        def add(zz, carry):
+            for half in range(2):
+                rows = pl.ds(48 * half, 48)
+                RFX[l, j, zz, rows, :] = (RFX[l, j, zz, rows, :].astype(F32) + FG[zz, x, rows, fcols[j]].astype(F32)).astype(BF)
+            return carry
+        lax.fori_loop(0, 4, add, 0)
+        for k in ks:
+            ml.send(RFX.at[l, j, (z + k) % 4], RFZ.at[l, j, k - 1], s_fz.at[l, j, k], r_fz.at[l, j, k], pc.zside(k))
+
+    def fz_task(l, j):
+        for k in ks:
+            ml.arrive(RFZ.at[l, j, k - 1], s_fz.at[l, j, k], r_fz.at[l, j, k], pc.zside(k))
+        def total(start):
+            rows = pl.ds(start, 48)
+            t = RFX[l, j, z, rows, :].astype(F32)
+            for k in range(3):
+                t = t + RFZ[l, j, k, rows, :].astype(F32)
+            return t.astype(BF)
+        if j == 0:
+            for half in range(2):
+                DNG[l, y, pl.ds(48 * half, 48), :] = total(48 * half)
+            ml.send(DNG.at[l, y], DNG.at[l, y], s_fy.at[l, 0], r_fy.at[l, 0], pc.yside())
+        else:
+            FR[l, j - 1] = total(pl.multiple_of((1 - c) * 48, 48))
+            ml.send(FR.at[l, j - 1], GUG.at[l, j - 1, c, y], s_fc.at[l, j], r_fc.at[l, j], pc.core())
+            GUG[l, j - 1, c, y] = total(pl.multiple_of(c * 48, 48))
+
+    def fc_task(l, j):
+        ml.arrive(GUG.at[l, j - 1, 1 - c, y], s_fc.at[l, j], r_fc.at[l, j], pc.core())
+        block = GUG.at[l, j - 1, :, y]
+        ml.send(block, block, s_fy.at[l, j], r_fy.at[l, j], pc.yside())
+
+    def fy_task(l, j):
+        block = DNG.at[l, 1 - y] if j == 0 else GUG.at[l, j - 1, :, 1 - y]
+        ml.arrive(block, s_fy.at[l, j], r_fy.at[l, j], pc.yside())
+
+    def ac_send(l, i):
+        h = (1 - y, y)[i]
+        ml.send(AG.at[h, :, :, 1 - c], RAC.at[l, i], s_ac.at[l, i], r_ac.at[l, i], pc.core(), ("ac", l))
+
+    def ac_task(l, i):
+        h = (1 - y, y)[i]
+        ml.arrive(RAC.at[l, i], s_ac.at[l, i], r_ac.at[l, i], pc.core())
+        def add(n, carry):
+            zz, xx = n // 2, n % 2
+            for cols in (pl.ds(0, 768), pl.ds(768, 896)):
+                RAC[l, i, zz, xx, :, cols] = (RAC[l, i, zz, xx, :, cols].astype(F32) + AG[h, zz, xx, c, :, cols].astype(F32)).astype(BF)
+            return carry
+        lax.fori_loop(0, 8, add, 0)
+        if i == 0:
+            ml.send(RAC.at[l, 0], RAY.at[l], s_ay.at[l], r_ay.at[l], pc.yside())
+
+    def ay_task(l):
+        ml.arrive(RAY.at[l], s_ay.at[l], r_ay.at[l], pc.yside())
+        def add(n, carry):
+            zz, xx = n // 2, n % 2
+            for cols in (pl.ds(0, 768), pl.ds(768, 896)):
+                RAC[l, 1, zz, xx, :, cols] = (RAC[l, 1, zz, xx, :, cols].astype(F32) + RAY[l, zz, xx, :, cols].astype(F32)).astype(BF)
+            return carry
+        lax.fori_loop(0, 8, add, 0)
+        ml.send(RAC.at[l, 1, :, 1 - x], RAX.at[l], s_ax.at[l], r_ax.at[l], pc.xside())
+
+    def ax_task(l):
+        ml.arrive(RAX.at[l], s_ax.at[l], r_ax.at[l], pc.xside())
+        def add(zz, carry):
+            for cols in (pl.ds(0, 768), pl.ds(768, 896)):
+                RAX[l, zz, :, cols] = (RAX[l, zz, :, cols].astype(F32) + RAC[l, 1, zz, x, :, cols].astype(F32)).astype(BF)
+            return carry
+        lax.fori_loop(0, 4, add, 0)
+        for k in ks:
+            ml.send(RAX.at[l, (z + k) % 4], RAZ.at[l, k - 1], s_az.at[l, k], r_az.at[l, k], pc.zside(k))
+
+    def az_task(l):
+        for k in ks:
+            ml.arrive(RAZ.at[l, k - 1], s_az.at[l, k], r_az.at[l, k], pc.zside(k))
+        for cols in (pl.ds(0, 768), pl.ds(768, 896)):
+            t = RAX[l, z, :, cols].astype(F32)
+            for k in range(3):
+                t = t + RAZ[l, k, :, cols].astype(F32)
+            AF[l, y, :, cols] = t.astype(BF)
+        ml.send(AF.at[l, y], AF.at[l, y], s_af.at[l], r_af.at[l], pc.yside())
+
+    def af_task(l):
+        ml.arrive(AF.at[l, 1 - y], s_af.at[l], r_af.at[l], pc.yside())
+
+    pair_mask = head_mask(T, 128)
+    low_half = lax.broadcasted_iota(jnp.int32, (T, 128), 1) % HEAD < HEAD // 2
+    onehot = (lax.broadcasted_iota(jnp.int32, (8, 128), 0) == lax.broadcasted_iota(jnp.int32, (8, 128), 1)).astype(F32).astype(BF)
+
+    def norm_back(i, extra, dst):
+        gain = PV[i, 0:1, :]
+        def rows_of(j, carry):
+            gs, bs = carry
+            rows = tile(j, 32)
+            u = U[rows, :]
+            if extra is not None:
+                u = u + extra(rows)
+            n = N[i, rows, :]
+            un = u * n
+            gs = gs + un.reshape(4, 8, D).sum(0)
+            bs = bs + u.reshape(4, 8, D).sum(0)
+            m1 = jnp.mean(u * gain, axis=1, keepdims=True)
+            m2 = jnp.mean(un * gain, axis=1, keepdims=True)
+            r = I[i, rows, 0:1] * (u * gain - m1 - n * m2)
+            U[rows, :] = r
+            dst[rows, :] = r.astype(BF)
+            return gs, bs
+        zero = jnp.zeros((8, D), F32)
+        gs, bs = lax.fori_loop(0, T // 32, rows_of, (zero, zero))
+        row = lax.broadcasted_iota(jnp.int32, (8, D), 0)
+        V[i] = jnp.where(row == 0, gs.sum(0, keepdims=True), jnp.where(row == 1, bs.sum(0, keepdims=True), 0.0))
+
+    def act_back(l, yy):
+        two = pl.ds(2 * yy, 2)
+        def cols_of(j, carry):
+            cols = tile(j, 256)
+            ga = dot_t(GF[l, two].reshape(2 * T, D), F[cols, 2 * FS:])
+            gate = TG[0, two, :, cols].reshape(2 * T, 256).astype(F32)
+            up = TG[1, two, :, cols].reshape(2 * T, 256).astype(F32)
+            sg = jax.nn.sigmoid(gate)
+            gg = ga * up * sg * (1.0 + gate * (1.0 - sg))
+            gu = ga * gate * sg
+            TG[0, two, :, cols] = gg.astype(BF).reshape(2, T, 256)
+            TG[1, two, :, cols] = gu.astype(BF).reshape(2, T, 256)
+            return carry
+        lax.fori_loop(0, FS // 256, cols_of, 0)
+
+    def mid_back(yy, cc, add, l):
+        s_ = 2 * yy + cc
+        def cols_of(j, carry):
+            cols = tile(j, 256)
+            r = dot_t(TG[0, s_], F[cols, 0:FS]) + dot_t(TG[1, s_], F[cols, FS:2 * FS])
+            if add:
+                r = r + RC[l, yy, :, cols].astype(F32)
+            FD[s_, :, cols] = r.astype(BF)
+            return carry
+        lax.fori_loop(0, D // 256, cols_of, 0)
+
+    def weight_grad(l, j):
+        def cols_of(n, carry):
+            cols = tile(n, 256)
+            if j == 0:
+                right = GF[l, :, :, cols].reshape(4 * T, 256)
+            else:
+                right = TG[j - 1, :, :, cols].reshape(4 * T, 256)
+            r = dot(TT[0 if j else 1], right)
+            off = (2 * FS, 0, FS)[j]
+            FG[:, :, :, pl.ds(pl.multiple_of(off + n * 256, 256), 256)] = r.astype(BF).reshape(4, 2, 96, 256)
+            return carry
+        lax.fori_loop(0, 3, cols_of, 0)
+
+    def mid_sums(l):
+        def to_core(i, yy):
+            mid_back(yy, 1 - c, False, l)
+            ml.send(FD.at[2 * yy + 1 - c], RC.at[l, yy], s_rc.at[l, i], r_rc.at[l, i], pc.core(), ("fd", l))
+        to_core(0, 1 - y)
+        ml.arrive(RC.at[l, 1 - y], s_rc.at[l, 0], r_rc.at[l, 0], pc.core())
+        mid_back(1 - y, c, True, l)
+        ml.send(FD.at[2 * (1 - y) + c], RY.at[l], s_ry.at[l], r_ry.at[l], pc.yside(), ("fd", l))
+        to_core(1, y)
+        ml.arrive(RC.at[l, y], s_rc.at[l, 1], r_rc.at[l, 1], pc.core())
+        mid_back(y, c, True, l)
+
+    def out_back():
+        acc = None
+        for h in range(2):
+            r = dot(ST[1], GB[:, h * OW:h * OW + OW])
+            AG[h, :, :, :, :, QW:QW + OW] = r.astype(BF).reshape(4, 2, 2, 48, OW)
+        for h in range(2):
+            t = dot_t(GB[:, h * OW:h * OW + OW], A[h, :, :, :, QW:QW + OW].reshape(D, OW))
+            acc = t if acc is None else acc + t
+        GA[...] = acc.astype(BF)
+
+    def attention_back():
+        def pair(p, carry):
+            cols = tile(p, 128)
+            q, kk, v, ga = Q[0, :, cols], Q[1, :, cols], Q[2, :, cols], GA[:, cols]
+            dq, dk, dv = [], [], []
+            for h in range(2):
+                pl_ = Pb[2 * p + h]
+                pr = pl_.astype(F32)
+                gh = jnp.where(pair_mask == (h == 0), ga, jnp.zeros_like(ga))
+                dp = dot_t(gh, v)
+                ds = (pr * (dp - jnp.sum(dp * pr, axis=1, keepdims=True))).astype(BF)
+                dq.append(dot(ds, kk))
+                dk.append(dot(ds.T, q))
+                dv.append(dot(pl_.T, ga))
+            cos, sin = cos_ref[...], sin_ref[...]
+            def back(pair_of):
+                m = jnp.where(pair_mask, pair_of[0], pair_of[1]) * 0.125
+                return (m * cos - swap_halves(m, low_half) * sin).astype(BF)
+            GP[0, :, cols] = back(dq)
+            GP[1, :, cols] = back(dk)
+            GP[2, :, cols] = jnp.where(pair_mask, dv[0], dv[1]).astype(BF)
+            return carry
+        lax.fori_loop(0, PAIRS, pair, 0)
+
+    def gp_chunk(j):
+        return GP[j // 2, :, (j % 2) * 384:(j % 2) * 384 + 384]
+
+    def qkv_grad(h):
+        for j in range(3 * h, 3 * h + 3):
+            off = (j % 3) * 384
+            r = dot(ST[0], gp_chunk(j))
+            AG[h, :, :, :, :, off:off + 384] = r.astype(BF).reshape(4, 2, 2, 48, 384)
+
+    def param_grad():
+        for h in range(2):
+            r = lax.dot_general(V[h].astype(BF), onehot, (((0,), (0,)), ((), ())), preferred_element_type=F32)
+            AG[h, :, :, :, :, QW + OW:] = r.astype(BF).reshape(4, 2, 2, 48, 128)
+
+    def input_back():
+        acc = U[...]
+        for j in range(6):
+            off = (j % 3) * 384
+            acc = acc + dot_t(gp_chunk(j), A[j // 3, :, :, :, off:off + 384].reshape(D, 384))
+        U[...] = acc
+
+    for l in (1, 0):
+        need("PV", "N", "I")
+        norm_back(1, None, GF.at[l, slot])
+        mine = GF.at[l, slot]
+        ml.send(mine, mine, s_m.at[l, 0], r_m.at[l, 0], pc.yside())
+        ml.send(mine, mine, s_m.at[l, 1], r_m.at[l, 1], pc.core())
+        if l == 0:
+            ml.gone(("fd", 1))
+            ay_task(1)
+            fz_task(1, 0)
+        need("TT", "F", "TG")
+        ml.arrive(GF.at[l, 2 * y + 1 - c], s_m.at[l, 1], r_m.at[l, 1], pc.core())
+        act_back(l, y)
+        other = GF.at[l, 2 * (1 - y) + c]
+        ml.arrive(other, s_m.at[l, 0], r_m.at[l, 0], pc.yside())
+        ml.send(other, other, s_m.at[l, 2], r_m.at[l, 2], pc.core())
+        ml.arrive(GF.at[l, 2 * (1 - y) + 1 - c], s_m.at[l, 2], r_m.at[l, 2], pc.core())
+        ml.gone(("fx", 1, 0)) if l == 0 else None
+        weight_grad(l, 0)
+        fx_send(l, 0)
+        act_back(l, 1 - y)
+        mid_sums(l)
+        if l == 1:
+            load(0, "F")
+        ml.gone(("fx", 1, 1)) if l == 0 else None
+        weight_grad(l, 1)
+        fx_send(l, 1)
+        ml.gone(("fx", 1, 2)) if l == 0 else None
+        weight_grad(l, 2)
+        fx_send(l, 2)
+        if l == 1:
+            load(0, "TT", "TG")
+        ml.arrive(RY.at[l], s_ry.at[l], r_ry.at[l], pc.yside())
+        norm_back(0, lambda rows: FD[slot, rows, :].astype(F32) + RY[l, rows, :].astype(F32), GB)
+        if l == 1:
+            load(0, "N", "I")
+        if l == 0:
+            ax_task(1)
+            fz_task(1, 1)
+            fz_task(1, 2)
+            fc_task(1, 1)
+            fc_task(1, 2)
+        need("ST", "A")
+        param_grad()
+        out_back()
+        if l == 1:
+            load(0, "PV")
+        fx_task(l, 0)
+        need("P", "Q")
+        attention_back()
+        if l == 1:
+            load(0, "P", "Q")
+        for i in range(2):
+            for h in range(2):
+                pass
+        qkv_grad(0)
+        qkv_grad(1)
+        ac_send(l, 0)
+        ac_send(l, 1)
+        if l == 1:
+            load(0, "ST")
+        fx_task(l, 1)
+        input_back()
+        if l == 1:
+            load(0, "A")
+        fx_task(l, 2)
+        ac_task(l, 0)
+        ac_task(l, 1)
+        if l == 1:
+            ml.gone(("ac", 1))
+    gin_ref[...] = U[...]
+    ay_task(0)
+    az_task(1)
+    fz_task(0, 0)
+    fz_task(0, 1)
+    fz_task(0, 2)
+    fc_task(0, 1)
+    fc_task(0, 2)
+    ax_task(0)
+    az_task(0)
+    for l in (1, 0):
+        for j in range(3):
+            fy_task(l, j)
+        af_task(l)
+    ml.finish()
+
+
+def backward_call(cot, cos, sin, kept):
+    any_spec = pl.BlockSpec(memory_space=pl.ANY)
+    vm = pl.BlockSpec(memory_space=pltpu.VMEM)
+    return pl.pallas_call(
+        backward_kernel,
+        out_shape=[
+            jax.ShapeDtypeStruct((T, D), F32),
+            jax.ShapeDtypeStruct((2, 2, 2, 2, 48, FS), BF),
+            jax.ShapeDtypeStruct((2, 2, 96, D), BF),
+            jax.ShapeDtypeStruct((2, 2, 48, AW), BF),
+        ],
+        in_specs=[vm] * 3 + [any_spec] * len(kept),
+        out_specs=[vm] * 4,
+        scratch_shapes=[pltpu.VMEM(s[1:], d) for s, d in FWD_SHAPES]
+        + [
+            pltpu.VMEM((T, D), F32),
+            pltpu.VMEM((2, 4, T, D), BF),
+            pltpu.VMEM((T, D), BF),
+            pltpu.VMEM((T, D), BF),
+            pltpu.VMEM((3, T, D), BF),
+            pltpu.VMEM((4, T, D), BF),
+            pltpu.VMEM((2, 2, T, D), BF),
+            pltpu.VMEM((2, T, D), BF),
+            pltpu.VMEM((4, 2, 96, 2 * FS + D), BF),
+            pltpu.VMEM((2, 3, 4, 96, D), BF),
+            pltpu.VMEM((2, 3, 3, 96, D), BF),
+            pltpu.VMEM((2, 2, 48, D), BF),
+            pltpu.VMEM((2, 4, 2, 2, 48, AW), BF),
+            pltpu.VMEM((2, 2, 4, 2, 48, AW), BF),
+            pltpu.VMEM((2, 4, 2, 48, AW), BF),
+            pltpu.VMEM((2, 4, 48, AW), BF),
+            pltpu.VMEM((2, 3, 48, AW), BF),
+            pltpu.VMEM((2, 8, D), F32),
+            sems(10),
+            sems(2, 3), sems(2, 3),
+            sems(2, 2), sems(2, 2),
+            sems(2), sems(2),
+            sems(2, 3), sems(2, 3),
+            sems(2, 3, 4), sems(2, 3, 4),
+            sems(2, 3), sems(2, 3),
+            sems(2, 3), sems(2, 3),
+            sems(2, 2), sems(2, 2),
+            sems(2), sems(2),
+            sems(2), sems(2),
+            sems(2, 4), sems(2, 4),
+            sems(2), sems(2),
+        ],
+        compiler_params=pltpu.CompilerParams(collective_id=1, has_side_effects=True, vmem_limit_bytes=60 * 2**20),
+        cost_estimate=pl.CostEstimate(flops=2 * 10**10, bytes_accessed=10**8, transcendentals=0),
+        name="backward",
+    )(cot, cos, sin, *kept)
+
+
+def epilogue(gug, dng, af):
+    def uncut(v):
+        return v.astype(F32).reshape(2, 2, 2, 48, G, 96).transpose(0, 3, 4, 1, 2, 5).reshape(2, 48, G * 4 * 96)
+    af = af.astype(F32)
+    both = lambda a, b: jnp.concatenate([af[:, 0, :, a:b], af[:, 1, :, a:b]], axis=-1)
+    return (
+        both(0, QW), both(QW, QW + OW), uncut(gug[:, 0]), uncut(gug[:, 1]), dng.astype(F32).reshape(2, 192, D),
+        af[:, 0, :, QW + OW], af[:, 0, :, QW + OW + 1], af[:, 1, :, QW + OW], af[:, 1, :, QW + OW + 1],
+    )
 
 
 def positions_of(segment_row):
@@ -23,9 +867,26 @@
 
 def rotary_tables(position):
     half_width = HEAD // 2
-    frequency = rope_base ** (-2.0 * jnp.arange(half_width, dtype=jnp.float32) / HEAD)
-    angles = position.astype(jnp.float32)[:, None] * frequency[None, :]
-    return (jnp.cos(angles), jnp.sin(angles))
+    frequency = rope_base ** (-2.0 * jnp.arange(half_width, dtype=F32) / HEAD)
+    angles = position.astype(F32)[:, None] * frequency[None, :]
+    return jnp.cos(angles), jnp.sin(angles)
+
+
+def prologue(inputs, segment_ids, qkv_weight, out_weight, gate_weight, up_weight, down_weight,
+             first_gain, first_bias, second_gain, second_bias):
+    seg = segment_ids[0]
+    cos, sin = rotary_tables(positions_of(seg))
+    cos = jnp.concatenate([cos] * 4, axis=1)
+    sin = jnp.concatenate([-sin, sin] * 2, axis=1)
+    segc = jnp.broadcast_to(seg[:, None], (T, 128))
+    segr = jnp.broadcast_to(seg[None, :], (8, T))
+    par = jnp.stack([jnp.stack([first_gain, first_bias], -1), jnp.stack([second_gain, second_bias], -1)], 1)
+    par = jnp.pad(par, ((0, 0), (0, 0), (0, 0), (0, 126)))
+    def cut(w):
+        return w.reshape(2, 48, G, 2, 2, 96).transpose(0, 3, 4, 1, 2, 5).reshape(2, 2, 2, 48, FS)
+    gu = jnp.concatenate([cut(gate_weight), cut(up_weight)], -1)
+    dn = down_weight.reshape(2, 2, 96, D)
+    return inputs[0], cos, sin, segc, segr, qkv_weight, out_weight, par, gu, dn
 
 
 def rotate(values, cosine_table, sine_table):
@@ -156,128 +1017,6 @@
         grad_queries.reshape(token_count, 2 * HEAD),
         grad_keys.reshape(token_count, 2 * HEAD),
         grad_values.reshape(token_count, 2 * HEAD),
-    )
-
-
-def fetch_forward(
-    qkv_weight,
-    out_weight,
-    gate_weight,
-    up_weight,
-    down_weight,
-    first_gain,
-    first_bias,
-    second_gain,
-    second_bias,
-    layer_index,
-):
-    return (
-        lax.all_gather(qkv_weight[layer_index], "shard", axis=0, tiled=True),
-        lax.all_gather(out_weight[layer_index], "shard", axis=0, tiled=True),
-        lax.all_gather(gate_weight[layer_index], "shard", axis=0, tiled=True),
-        lax.all_gather(up_weight[layer_index], "shard", axis=0, tiled=True),
-        lax.all_gather(down_weight[layer_index], "shard", axis=0, tiled=True),
-        lax.all_gather(first_gain[layer_index], "shard", axis=0, tiled=True),
-        lax.all_gather(first_bias[layer_index], "shard", axis=0, tiled=True),
-        lax.all_gather(second_gain[layer_index], "shard", axis=0, tiled=True),
-        lax.all_gather(second_bias[layer_index], "shard", axis=0, tiled=True),
-    )
-
-
-def fetch_backward(
-    qkv_weight,
-    out_weight,
-    gate_weight,
-    up_weight,
-    down_weight,
-    first_gain,
-    first_bias,
-    second_gain,
-    second_bias,
-    layer_index,
-):
-    return (
-        lax.all_gather(qkv_weight[layer_index], "shard", axis=0, tiled=True),
-        lax.all_gather(out_weight[layer_index], "shard", axis=0, tiled=True),
-        lax.all_gather(gate_weight[layer_index], "shard", axis=0, tiled=True),
-        lax.all_gather(up_weight[layer_index], "shard", axis=0, tiled=True),
-        lax.all_gather(down_weight[layer_index], "shard", axis=0, tiled=True),
-        lax.all_gather(first_gain[layer_index], "shard", axis=0, tiled=True),
-        lax.all_gather(first_bias[layer_index], "shard", axis=0, tiled=True),
-        lax.all_gather(second_gain[layer_index], "shard", axis=0, tiled=True),
-        lax.all_gather(second_bias[layer_index], "shard", axis=0, tiled=True),
-    )
-
-
-def share_gradients(gradients):
-    owned_sums = (
-        lax.psum_scatter(gradients[0], "shard", scatter_dimension=0, tiled=True),
-        lax.psum_scatter(gradients[1], "shard", scatter_dimension=0, tiled=True),
-        lax.psum_scatter(gradients[2], "shard", scatter_dimension=0, tiled=True),
-        lax.psum_scatter(gradients[3], "shard", scatter_dimension=0, tiled=True),
-        lax.psum_scatter(gradients[4], "shard", scatter_dimension=0, tiled=True),
-        lax.psum_scatter(gradients[5], "shard", scatter_dimension=0, tiled=True),
-        lax.psum_scatter(gradients[6], "shard", scatter_dimension=0, tiled=True),
-        lax.psum_scatter(gradients[7], "shard", scatter_dimension=0, tiled=True),
-        lax.psum_scatter(gradients[8], "shard", scatter_dimension=0, tiled=True),
-    )
-    halves = (
-        lax.psum_scatter(
-            owned_sums[0].astype(jnp.bfloat16), "rep", scatter_dimension=0, tiled=True
-        ).astype(jnp.float32),
-        lax.psum_scatter(
-            owned_sums[1].astype(jnp.bfloat16), "rep", scatter_dimension=0, tiled=True
-        ).astype(jnp.float32),
-        lax.psum_scatter(
-            owned_sums[2].astype(jnp.bfloat16), "rep", scatter_dimension=0, tiled=True
-        ).astype(jnp.float32),
-        lax.psum_scatter(
-            owned_sums[3].astype(jnp.bfloat16), "rep", scatter_dimension=0, tiled=True
-        ).astype(jnp.float32),
-        lax.psum_scatter(
-            owned_sums[4].astype(jnp.bfloat16), "rep", scatter_dimension=0, tiled=True
-        ).astype(jnp.float32),
-        lax.psum_scatter(
-            owned_sums[5].astype(jnp.bfloat16), "rep", scatter_dimension=0, tiled=True
-        ).astype(jnp.float32),
-        lax.psum_scatter(
-            owned_sums[6].astype(jnp.bfloat16), "rep", scatter_dimension=0, tiled=True
-        ).astype(jnp.float32),
-        lax.psum_scatter(
-            owned_sums[7].astype(jnp.bfloat16), "rep", scatter_dimension=0, tiled=True
-        ).astype(jnp.float32),
-        lax.psum_scatter(
-            owned_sums[8].astype(jnp.bfloat16), "rep", scatter_dimension=0, tiled=True
-        ).astype(jnp.float32),
-    )
-    return (
-        lax.all_gather(halves[0].astype(jnp.bfloat16), "rep", axis=0, tiled=True).astype(
-            jnp.float32
-        ),
-        lax.all_gather(halves[1].astype(jnp.bfloat16), "rep", axis=0, tiled=True).astype(
-            jnp.float32
-        ),
-        lax.all_gather(halves[2].astype(jnp.bfloat16), "rep", axis=0, tiled=True).astype(
-            jnp.float32
-        ),
-        lax.all_gather(halves[3].astype(jnp.bfloat16), "rep", axis=0, tiled=True).astype(
-            jnp.float32
-        ),
-        lax.all_gather(halves[4].astype(jnp.bfloat16), "rep", axis=0, tiled=True).astype(
-            jnp.float32
-        ),
-        lax.all_gather(halves[5].astype(jnp.bfloat16), "rep", axis=0, tiled=True).astype(
-            jnp.float32
-        ),
-        lax.all_gather(halves[6].astype(jnp.bfloat16), "rep", axis=0, tiled=True).astype(
-            jnp.float32
-        ),
-        lax.all_gather(halves[7].astype(jnp.bfloat16), "rep", axis=0, tiled=True).astype(
-            jnp.float32
-        ),
-        lax.all_gather(halves[8].astype(jnp.bfloat16), "rep", axis=0, tiled=True).astype(
-            jnp.float32
-        ),
     )
 
 
@@ -422,115 +1161,48 @@
     )
 
 
-def shards(
-    inputs,
-    segment_ids,
-    qkv_weight,
-    out_weight,
-    gate_weight,
-    up_weight,
-    down_weight,
-    first_gain,
-    first_bias,
-    second_gain,
-    second_bias,
-    cotangent,
-):
+def general(inputs, segment_ids, qkv_weight, out_weight, gate_weight, up_weight, down_weight,
+            first_gain, first_bias, second_gain, second_bias, cotangent):
+    params = (qkv_weight, out_weight, gate_weight, up_weight, down_weight, first_gain, first_bias, second_gain, second_bias)
     layers = qkv_weight.shape[0]
     segment_row = segment_ids[0]
     cosine_table, sine_table = rotary_tables(positions_of(segment_row))
     allowed = segment_row[:, None] == segment_row[None, :]
     score_scale = 1.0 / math.sqrt(HEAD)
-    hidden_state = inputs[0].astype(jnp.float32)
-    fetched = []
-    saved = []
+    hidden_state = inputs[0].astype(F32)
+    fetched, saved = [], []
     for layer_index in range(layers):
-        weights = fetch_forward(
-            qkv_weight,
-            out_weight,
-            gate_weight,
-            up_weight,
-            down_weight,
-            first_gain,
-            first_bias,
-            second_gain,
-            second_bias,
-            layer_index,
-        )
+        weights = tuple(lax.all_gather(w[layer_index], "shard", axis=0, tiled=True) for w in params)
         fetched.append(weights)
-        hidden_state, stored = layer_forward(
-            hidden_state, weights, cosine_table, sine_table, allowed, score_scale
-        )
+        hidden_state, stored = layer_forward(hidden_state, weights, cosine_table, sine_table, allowed, score_scale)
         saved.append(stored)
-    output = hidden_state.astype(jnp.bfloat16)[None]
-    upstream = cotangent[0].astype(jnp.float32)
+    upstream = cotangent[0].astype(F32)
     shared = [None] * layers
     for layer_index in reversed(range(layers)):
-        weights = fetch_backward(
-            qkv_weight,
-            out_weight,
-            gate_weight,
-            up_weight,
-            down_weight,
-            first_gain,
-            first_bias,
-            second_gain,
-            second_bias,
-            layer_index,
+        upstream, gradients = layer_backward(
+            upstream, fetched[layer_index], saved[layer_index], cosine_table, sine_table, allowed, score_scale
         )
-        upstream, gradients = layer_backward(
-            upstream, weights, saved[layer_index], cosine_table, sine_table, allowed, score_scale
-        )
-        shared[layer_index] = share_gradients(gradients)
-    stacked = [
-        jnp.stack([shared[layer_index][member] for layer_index in range(layers)])
-        for member in range(9)
-    ]
-    return (
-        output,
-        upstream[None],
-        stacked[0],
-        stacked[1],
-        stacked[2],
-        stacked[3],
-        stacked[4],
-        stacked[5],
-        stacked[6],
-        stacked[7],
-        stacked[8],
-    )
+        owned = [lax.psum_scatter(v, "shard", scatter_dimension=0, tiled=True) for v in gradients]
+        shared[layer_index] = [lax.psum(v.astype(BF), "rep").astype(F32) for v in owned]
+    stacked = [jnp.stack([shared[layer_index][member] for layer_index in range(layers)]) for member in range(9)]
+    return (hidden_state.astype(BF)[None], upstream[None], *stacked)
+
+
+def special(inputs, segment_ids, qkv_weight, out_weight, gate_weight, up_weight, down_weight,
+            first_gain, first_bias, second_gain, second_bias, cotangent):
+    staged = prologue(inputs, segment_ids, qkv_weight, out_weight, gate_weight, up_weight, down_weight,
+                      first_gain, first_bias, second_gain, second_bias)
+    output, *kept = forward_call(staged)
+    gin, gug, dng, af = backward_call(cotangent[0], staged[1], staged[2], kept)
+    return (output[None], gin[None]) + epilogue(gug, dng, af)
+
+
+IN_SPECS = (
+    P(("rep", "shard"), None, None), P(("rep", "shard"), None),
+) + (P(None, "shard", None),) * 5 + (P(None, "shard"),) * 4 + (P(("rep", "shard"), None, None),)
+OUT_SPECS = (P(("rep", "shard"), None, None),) * 2 + (P(None, "shard", None),) * 5 + (P(None, "shard"),) * 4
 
 
 def solution(mesh):
-    return jax.shard_map(
-        shards,
-        mesh=mesh,
-        in_specs=(
-            P(("rep", "shard"), None, None),
-            P(("rep", "shard"), None),
-            P(None, "shard", None),
-            P(None, "shard", None),
-            P(None, "shard", None),
-            P(None, "shard", None),
-            P(None, "shard", None),
-            P(None, "shard"),
-            P(None, "shard"),
-            P(None, "shard"),
-            P(None, "shard"),
-            P(("rep", "shard"), None, None),
-        ),
-        out_specs=(
-            P(("rep", "shard"), None, None),
-            P(("rep", "shard"), None, None),
-            P(None, "shard", None),
-            P(None, "shard", None),
-            P(None, "shard", None),
-            P(None, "shard", None),
-            P(None, "shard", None),
-            P(None, "shard"),
-            P(None, "shard"),
-            P(None, "shard"),
-            P(None, "shard"),
-        ),
-        check_vma=False,
-    )
+    fits = dict(mesh.shape) == {"rep": 2, "shard": 2 * G}
+    return jax.shard_map(special if fits else general, mesh=mesh, in_specs=IN_SPECS, out_specs=OUT_SPECS, check_vma=False)

time: 1750 us -> 443 us (0.25)
  waiting for transfers between devices: 1230 us -> 0 us
  Pallas kernels: 0 us -> 402 us
  blocking collectives: 196 us -> 0 us
  matrix products: 155 us -> 0 us
  local copies, waits for them, and re-layouts: 101 us -> 24.4 us
  other arithmetic: 41.9 us -> 9.88 us
    reduce_scatter x18 -> x0, waiting for transfers between devices: 686 us -> none  [the longest x2 220 us: share_gradients(): lax.psum_scatter(gradients[4], 'shard', scatter_dimension=0, tiled=True)]
    pallas_call x0 -> x2, Pallas kernels: none -> 402 us  [the longest x1 206 us: backward_call(): pl.pallas_call(backward_kernel, out_shape=[jax.ShapeDtypeStruct((T, D), F...]
    all_gather x10 -> x0, waiting for transfers between devices: 361 us -> none  [the longest x2 104 us: fetch_forward(): lax.all_gather(gate_weight[layer_index], 'shard', axis=0, tiled=True)]
    unnamed x32 -> x0, waiting for transfers between devices: 180 us -> none
    dot_general x113 -> x0, matrix products: 150 us -> none  [the longest x9 46.8 us: outer_sum(): lax.dot_general(left_side, right_side, (((0,), (0,)), ((), ())), preferre...]
    unnamed x4 -> x0, blocking collectives: 136 us -> none
    all_gather x10 -> x0, blocking collectives: 59.8 us -> none  [the longest x2 12.9 us: share_gradients(): lax.all_gather(halves[2].astype(jnp.bfloat16), 'rep', axis=0, tiled=True)]
    dynamic_slice x60 -> x0, local copies, waits for them, and re-layouts: 30.8 us -> none  [layer_forward(): lax.map(attend_pair, (to_pairs(queries), to_pairs(key_rows), to_pairs(val...]
  transfers between devices with their start and end apart: 30 -> 0, of which waited for: 27 -> 0; matrix products, arithmetic and copies ran while one was open for 13% -> 0% of each run, Pallas kernels for 0% -> 0%
where the time goes in v1:
time: 443 us; the launch traced here: 438 us
  Pallas kernels  402 us (91%)
  local copies, waits for them, and re-layouts  24.4 us (6%)
  other arithmetic  9.88 us (2%)
    pallas_call x1, Pallas kernels, backward_call(): pl.pallas_call(backward_kernel, out_shape=[jax.ShapeDtypeStruct((T, D), F...  206 us
    pallas_call x1, Pallas kernels, forward_call(): pl.pallas_call(forward_kernel, out_shape=[jax.ShapeDtypeStruct((T, D), BF...  196 us
    reshape x6, local copies, waits for them, and re-layouts, uncut(): v.astype(F32).reshape(2, 2, 2, 48, G, 96).transpose(0, 3, 4, 1, 2, 5)  11.4 us

profile of v1, /device:TPU:0, one launch (start us, length us, event | category | flops | bytes accessed | tf_op | source)
XLA Modules:
  0.0 438.3 jit_solution(7959196076182921757)
XLA Ops:
  0.7 1.2 slice.47
  2.5 0.8 compare_select_fusion
  3.4 0.3 reduce-window.9
  4.0 1.3 broadcast_in_dim.26.segr_ref
  5.3 0.8 copy.79
  6.0 0.8 copy.80
  6.8 0.8 copy.81
  7.6 0.8 copy.82
  8.4 0.6 fusion.2.par_ref
  9.1 1.4 broadcast_in_dim.25.segc_ref
  10.5 0.5 fusion.3
  11.0 1.0 pad_maximum_fusion.3
  12.0 0.8 reshape.104
  12.9 0.6 reshape.105
  13.9 0.8 reshape.106
  14.7 0.6 reshape.107
  15.4 1.1 pad_maximum_fusion.gu_ref
  16.5 196.1 %forward.1 = (bf16[256,768]{1,0:T(8,128)(2,1)}, bf16[2,2,8,2,48,1664]{5,4,3,2,1,0:T(8,128)(2,1)}, bf16[2,768,2304]{2,1,0:T(8,128)(2,1)}, bf16[2,3,256,768]{3,2,1...) custom-call(bf16[256,768]{1,0:T(8,128)(2,1)} %bitcast.72, ...), custom_call_target="tpu_custom_call" | custom-call | flops 10000000000 | bytes 100000000 | tf_op jit(solution)/shard_map/forward/pallas_call | solution.py:417
  212.6 206.0 %backward.1 = (f32[256,768]{1,0:T(8,128)}, bf16[2,2,2,2,48,768]{5,4,3,2,1,0:T(8,128)(2,1)}, bf16[2,2,96,768]{3,2,1,0:T(8,128)(2,1)}, bf16[2,2,48,1664]{3,2,1,0:T(8,128)(2,1)}) custom-call(bf16[256,768]{1,0:T(8,128)(2,1)} %bitcast.73, f32[256,128]{1,0:T(8,128)} %get-tuple-element.54.cos_ref, f32[256,128]{1,0:T(8,128)} %get-tuple-element.55.sin_ref, ...), custom_call_target="tpu_custom_call" | custom-call | flops 20000000000 | bytes 100000000 | tf_op jit(solution)/shard_map/backward/pallas_call | solution.py:800
  418.6 2.2 bitcast_convert_fusion
  420.9 0.8 slice_reduce_fusion
  421.8 1.0 pad_maximum_fusion.1
  422.8 0.7 pad_maximum_fusion.2
  423.5 1.3 slice_convert_fusion
  424.8 0.7 reshape.126
  425.5 1.2 copy.88
  426.7 3.2 reshape.118
  429.9 1.9 reshape.124
  431.8 1.2 copy.87
  433.0 3.2 reshape.116
  436.2 0.7 copy.97
  437.0 0.9 copy.98
  (23 shorter events, 1.1 us)
Async XLA Ops:
  0.6 11.4 %copy-start.3 = (bf16[2,48,3072]{2,1,0:T(8,128)(2,1)S(1)}, bf16[2,48,3072]{2,1,0:T(8,128)(2,1)}, u32[]{:S(2)}) copy-start(bf16[2,48,3072]{2,1,0:T(8,128)(2,1)} %param.16) | copy-start | bytes 1769476
  12.8 1.1 copy-start.4
  418.6 2.2 copy-start.2
  421.8 1.7 copy-start
  433.0 3.2 copy-start.5
  433.0 3.9 copy-start.1

commit v2 on v1

--- a/solution.py
+++ b/solution.py
@@ -3,6 +3,7 @@
 
 import jax
 import jax.numpy as jnp
+import numpy as np
 from jax import lax
 from jax.experimental import pallas as pl
 from jax.experimental.pallas import tpu as pltpu
@@ -69,28 +70,52 @@
     def zside(self, k):
         return self.at(self.y, (self.z + k) % 4, self.x, self.c)
 
+    def zto(self, z):
+        return self.at(self.y, z, self.x, self.c)
+
+    def near(self):
+        return self.z + 1 - 2 * (self.z % 2)
+
+    def across(self):
+        return 3 - self.z
+
+    def source(self, i):
+        return (self.near(), 2 - self.z // 2, 3 - 3 * (self.z // 2))[i]
+
+    def chip_from(self, i, x):
+        return 2 * (self.z if i is None else self.source(i)) + x
+
     def chip(self, k, x):
         return 2 * ((self.z + 4 - k) % 4) + x
 
+    def line(self):
+        return [self.core(), self.xside(), self.yside(), self.zto(self.near()), self.zto(self.across())]
+
     def everyone(self):
         return [self.core(), self.xside(), self.yside()] + [self.zside(k) for k in (1, 2, 3)]
 
 
-def greet(place):
+def greet(partners):
     barrier = pltpu.get_barrier_semaphore()
-    for who in place.everyone():
+    for who in partners:
         pl.semaphore_signal(barrier, inc=1, device_id=who, device_id_type=MESH)
-    pl.semaphore_wait(barrier, 6)
+    pl.semaphore_wait(barrier, len(partners))
 
 
 class Mail:
     def __init__(self):
         self.sent = []
+        self.some = []
 
     def send(self, src, dst, send_sem, recv_sem, who, tag=None):
         copy = pltpu.make_async_remote_copy(src, dst, send_sem, recv_sem, device_id=who, device_id_type=MESH)
         copy.start()
         self.sent.append((tag, copy))
+
+    def send_if(self, cond, src, dst, send_sem, recv_sem, who):
+        copy = pltpu.make_async_remote_copy(src, dst, send_sem, recv_sem, device_id=who, device_id_type=MESH)
+        pl.when(cond)(copy.start)
+        self.some.append((cond, copy))
 
     def local(self, src, dst, sem):
         copy = pltpu.make_async_copy(src, dst, sem)
@@ -109,7 +134,8 @@
     def finish(self):
         for _, copy in self.sent:
             copy.wait_send()
-        self.sent = []
+        for cond, copy in self.some:
+            pl.when(cond)(copy.wait_send)
 
 
 def swap_halves(v, low_half):
@@ -121,9 +147,9 @@
 
 
 def forward_kernel(
-    x_ref, cos_ref, sin_ref, segc_ref, segr_ref, qkv_ref, outw_ref, par_ref, gu_ref, dn_ref,
-    y_ref, A_o, F_o, Q_o, ST_o, P_o, TG_o, TT_o, N_o, I_o, PV_o,
-    A, F, Q, ST, Pb, TG, TT, N, I, PV, S, AT, MF, AC, H, bias, FD, RC, RY,
+    x_ref, seg_ref, freq_ref, qkv_ref, outw_ref, par_ref, gate_ref, up_ref, dn_ref,
+    y_ref, A_o, F_o, Q_o, ST_o, P_o, TG_o, TT_o, N_o, I_o, PV_o, cos_ref, sin_ref,
+    A, F, Q, ST, Pb, TG, TT, N, I, PV, S, AT, MF, AC, H, bias, FD, RC, RY, W, GU,
     ls, s_gu, r_gu, s_az, r_az, s_ax, r_ax, s_ay, r_ay, s_ac, r_ac, s_fz, r_fz, s_fx, r_fx,
     s_m, r_m, s_rc, r_rc, s_ry, r_ry, os,
 ):
@@ -131,7 +157,9 @@
     y, z, x, c, g, slot = pc.y, pc.z, pc.x, pc.c, pc.g, pc.slot
     ml = Mail()
     LAY = (0, 1)
-    ks = (1, 3, 2)
+    mid = z % 3 != 0
+    near, across = pc.zto(pc.near()), pc.zto(pc.across())
+    THREE = (0, 1, 2)
 
     own_a, own_f = [], []
     for l in LAY:
@@ -141,76 +169,90 @@
             own_a[l].append(ml.local(qkv_ref.at[l, :, pl.ds(QW * h, QW)], dst.at[:, pl.ds(0, QW)], ls.at[l, h]))
             own_a[l].append(ml.local(outw_ref.at[l, :, pl.ds(OW * h, OW)], dst.at[:, pl.ds(QW, OW)], ls.at[l, 2 + h]))
             own_a[l].append(ml.local(par_ref.at[l, h], dst.at[:, pl.ds(QW + OW, 128)], ls.at[l, 4 + h]))
-        own_f.append([
-            ml.local(gu_ref.at[l, c, y], F.at[l, shard_rows(g, c), pl.ds(0, 2 * FS)], ls.at[l, 6]),
-            ml.local(dn_ref.at[l, y], F.at[l, chip_rows(g), pl.ds(2 * FS, D)], ls.at[l, 7]),
-        ])
-    greet(pc)
+    wide = [ml.local(gate_ref, W.at[0], ls.at[0, 6]), ml.local(up_ref, W.at[1], ls.at[1, 6])]
+    for l in LAY:
+        own_f.append(ml.local(dn_ref.at[l, pl.ds(pl.multiple_of(y * 96, 96), 96)], F.at[l, chip_rows(g), pl.ds(2 * FS, D)], ls.at[l, 7]))
+    greet(pc.line())
 
     def gu_send(l):
-        ml.send(gu_ref.at[l, 1 - c, y], F.at[l, shard_rows(g, c), pl.ds(0, 2 * FS)], s_gu.at[l], r_gu.at[l], pc.core())
+        ml.send(GU.at[l, 1 - c, y], F.at[l, shard_rows(g, c), pl.ds(0, 2 * FS)], s_gu.at[l], r_gu.at[l], pc.core())
 
     def gu_arrive(l):
         ml.arrive(F.at[l, shard_rows(g, 1 - c), pl.ds(0, 2 * FS)], s_gu.at[l], r_gu.at[l], pc.core())
+
+    def line_own(block, ss, rs):
+        ml.send(block, block, ss.at[0], rs.at[0], near)
+        ml.send_if(mid, block, block, ss.at[1], rs.at[1], across)
+
+    def line_pass(i, block, ss, rs):
+        ml.arrive(block, ss.at[0], rs.at[i], near)
+        to, at = ((across, 2), (near, 1), (near, 2))[i]
+        ml.send_if(mid, block, block, ss.at[2 + i], rs.at[at], to)
 
     def a_own(l):
         for copy in own_a[l]:
             copy.wait()
         block = A.at[l, y, g, c]
-        for i in ks:
-            ml.send(block, block, s_az.at[l, i], r_az.at[l, i], pc.zside(i))
         ml.send(block, block, s_ax.at[l, 0], r_ax.at[l, 0], pc.xside())
-
-    def a_z(l, k):
-        block = A.at[l, y, pc.chip(k, x), c]
-        ml.arrive(block, s_az.at[l, k], r_az.at[l, k], pc.zside(k))
-        ml.send(block, block, s_ax.at[l, k], r_ax.at[l, k], pc.xside())
-        ml.send(block, block, s_ay.at[l, k], r_ay.at[l, k], pc.yside())
-
-    def a_x(l, k):
-        block = A.at[l, y, pc.chip(k, 1 - x), c]
-        ml.arrive(block, s_ax.at[l, k], r_ax.at[l, k], pc.xside())
-        ml.send(block, block, s_ay.at[l, 4 + k], r_ay.at[l, 4 + k], pc.yside())
+        line_own(block, s_az.at[l], r_az.at[l])
+
+    def a_z(l, i):
+        block = A.at[l, y, pc.chip_from(i, x), c]
+        line_pass(i, block, s_az.at[l], r_az.at[l])
+        ml.send(block, block, s_ax.at[l, 1 + i], r_ax.at[l, 1 + i], pc.xside())
+
+    def a_yo(l, i):
+        block = A.at[l, y, pc.chip_from(i, x), c]
+        ml.send(block, block, s_ay.at[l, i], r_ay.at[l, i], pc.yside())
+
+    FOUR = (None, 0, 1, 2)
+
+    def a_x(l, j):
+        ml.arrive(A.at[l, y, pc.chip_from(FOUR[j], 1 - x), c], s_ax.at[l, j], r_ax.at[l, j], pc.xside())
+
+    def a_yx(l, j):
+        block = A.at[l, y, pc.chip_from(FOUR[j], 1 - x), c]
+        ml.send(block, block, s_ay.at[l, 3 + j], r_ay.at[l, 3 + j], pc.yside())
 
     def a_c(l, h):
         block = A.at[l, h, :, c]
         ml.send(block, block, s_ac.at[l, h], r_ac.at[l, h], pc.core())
 
-    def a_y(l, k, xx, j):
-        ml.arrive(A.at[l, 1 - y, pc.chip(k, xx), c], s_ay.at[l, j], r_ay.at[l, j], pc.yside())
+    def a_y(l, i, xx, n):
+        ml.arrive(A.at[l, 1 - y, pc.chip_from(i, xx), c], s_ay.at[l, n], r_ay.at[l, n], pc.yside())
 
     def a_c_arrive(l, h):
         ml.arrive(A.at[l, h, :, 1 - c], s_ac.at[l, h], r_ac.at[l, h], pc.core())
 
-    def f_own(l):
-        for copy in own_f[l]:
-            copy.wait()
+    parts = (pl.ds(0, 2 * FS), pl.ds(2 * FS, D))
+
+    def f_ready(l):
+        for w in range(2):
+            F[l, shard_rows(g, c), w * FS:w * FS + FS] = GU[l, c, y, :, w * FS:w * FS + FS]
+        own_f[l].wait()
         gu_arrive(l)
-        block = F.at[l, chip_rows(g)]
-        for i in ks:
-            ml.send(block, block, s_fz.at[l, i], r_fz.at[l, i], pc.zside(i))
-        ml.send(block, block, s_fx.at[l, 0], r_fx.at[l, 0], pc.xside())
-
-    def f_z(l, k):
-        block = F.at[l, chip_rows(pc.chip(k, x))]
-        ml.arrive(block, s_fz.at[l, k], r_fz.at[l, k], pc.zside(k))
-        ml.send(block, block, s_fx.at[l, k], r_fx.at[l, k], pc.xside())
-
-    def f_x(l, k):
-        ml.arrive(F.at[l, chip_rows(pc.chip(k, 1 - x))], s_fx.at[l, k], r_fx.at[l, k], pc.xside())
-
-    def attn_gather(l):
-        for k in ks:
-            a_z(l, k)
-        for k in (0,) + ks:
-            a_x(l, k)
-        a_c(l, y)
+
+    def f_own_z(l, p):
+        line_own(F.at[l, chip_rows(g), parts[p]], s_fz.at[l, p], r_fz.at[l, p])
+
+    def f_own_x(l, p):
+        block = F.at[l, chip_rows(g), parts[p]]
+        ml.send(block, block, s_fx.at[l, p, 0], r_fx.at[l, p, 0], pc.xside())
+
+    def f_z(l, p, i):
+        block = F.at[l, chip_rows(pc.chip_from(i, x)), parts[p]]
+        line_pass(i, block, s_fz.at[l, p], r_fz.at[l, p])
+        ml.send(block, block, s_fx.at[l, p, 1 + i], r_fx.at[l, p, 1 + i], pc.xside())
+
+    def f_x(l, p):
+        for j in range(4):
+            ml.arrive(F.at[l, chip_rows(pc.chip_from(FOUR[j], 1 - x)), parts[p]], s_fx.at[l, p, j], r_fx.at[l, p, j], pc.xside())
 
     def attn_ready(l):
-        for k in ks:
-            a_y(l, k, x, k)
-        for k in (0,) + ks:
-            a_y(l, k, 1 - x, 4 + k)
+        for i in THREE:
+            a_y(l, i, x, i)
+        for j in range(4):
+            a_y(l, FOUR[j], 1 - x, 3 + j)
         a_c(l, 1 - y)
         a_c_arrive(l, y)
         a_c_arrive(l, 1 - y)
@@ -223,6 +265,31 @@
     pair_mask = head_mask(T, 128)
     low_half = lax.broadcasted_iota(jnp.int32, (T, 128), 1) % HEAD < HEAD // 2
     onehot = (lax.broadcasted_iota(jnp.int32, (8, 128), 0) == lax.broadcasted_iota(jnp.int32, (8, 128), 1)).astype(F32).astype(BF)
+
+    def tables():
+        wide_row = jnp.broadcast_to(seg_ref[...].astype(F32), (T, T))
+        same = wide_row.T == wide_row
+        bias[...] = jnp.where(same, 0.0, masked_score)
+        at = lax.broadcasted_iota(jnp.int32, (T, T), 1).astype(F32)
+        first = jnp.min(jnp.where(same, at, float(T)), axis=1, keepdims=True)
+        position = lax.broadcasted_iota(jnp.int32, (T, 128), 0).astype(F32) - first
+        angle = position * freq_ref[0:1, :]
+        sine = jnp.sin(angle)
+        cos_ref[...] = jnp.cos(angle)
+        sin_ref[...] = jnp.where(low_half, -sine, sine)
+
+    def permute():
+        for copy in wide:
+            copy.wait()
+        def of(i, carry):
+            l, w = i // 2, i % 2
+            v = W[w, l]
+            for cc in range(2):
+                for yy in range(2):
+                    pieces = [v[:, 384 * j + 192 * cc + 96 * yy:384 * j + 192 * cc + 96 * yy + 96] for j in range(G)]
+                    GU[l, cc, yy, :, tile(w, FS)] = jnp.concatenate(pieces, axis=1)
+            return carry
+        lax.fori_loop(0, 4, of, 0)
 
     def project(l):
         st = S[...]
@@ -327,14 +394,18 @@
         ml.send(mine, mine, s_m.at[l, 0], r_m.at[l, 0], pc.yside())
         ml.send(mine, mine, s_m.at[l, 1], r_m.at[l, 1], pc.core())
 
-    def feed_forward(l):
+    def feed_forward(l, before_up=(), before_down=(), after_y=(), before_ry=()):
+        run(before_up)
         other_y = MF.at[l, 2 * (1 - y) + c]
         ml.arrive(MF.at[l, 2 * y + 1 - c], s_m.at[l, 1], r_m.at[l, 1], pc.core())
+        f_x(l, 0)
         ffn_up(l, y)
         ml.arrive(other_y, s_m.at[l, 0], r_m.at[l, 0], pc.yside())
         ml.send(other_y, other_y, s_m.at[l, 2], r_m.at[l, 2], pc.core())
         ml.arrive(MF.at[l, 2 * (1 - y) + 1 - c], s_m.at[l, 2], r_m.at[l, 2], pc.core())
         ffn_up(l, 1 - y)
+        run(before_down)
+        f_x(l, 1)
         def to_core(i, yy):
             ffn_down(l, yy, 1 - c, False)
             ml.send(FD.at[l, 2 * yy + 1 - c], RC.at[l, yy], s_rc.at[l, i], r_rc.at[l, i], pc.core())
@@ -342,52 +413,105 @@
         ml.arrive(RC.at[l, 1 - y], s_rc.at[l, 0], r_rc.at[l, 0], pc.core())
         ffn_down(l, 1 - y, c, True)
         ml.send(FD.at[l, 2 * (1 - y) + c], RY.at[l], s_ry.at[l], r_ry.at[l], pc.yside())
+        run(after_y)
         to_core(1, y)
         ml.arrive(RC.at[l, y], s_rc.at[l, 1], r_rc.at[l, 1], pc.core())
         ffn_down(l, y, c, True)
         turn_slots(MF.at[l], TT.at[l, 0])
         turn_slots(AC, TT.at[l, 1])
+        run(before_ry)
         ml.arrive(RY.at[l], s_ry.at[l], r_ry.at[l], pc.yside())
 
+    def run(steps):
+        for step, *what in steps:
+            step(*what)
+
+    a_own(0)
+    a_own(1)
+    permute()
     gu_send(0)
     gu_send(1)
-    a_own(0)
-    a_own(1)
-    bias[...] = jnp.where(segc_ref[:, 0:1] == segr_ref[0:1, :], 0.0, masked_score)
     H[...] = x_ref[...].astype(F32)
     S[...] = x_ref[...]
-    attn_gather(0)
-    f_own(0)
-    attn_gather(1)
-    f_own(1)
+    for i in THREE:
+        a_z(0, i)
+        a_yo(0, i)
+    f_ready(0)
+    f_own_z(0, 0)
+    f_own_z(0, 1)
+    f_ready(1)
+    for j in range(4):
+        a_x(0, j)
+        a_yx(0, j)
+    a_c(0, y)
+    f_own_x(0, 0)
+    for i in THREE:
+        a_z(1, i)
+    f_own_x(0, 1)
+    f_own_z(1, 0)
+    f_own_z(1, 1)
+    tables()
+    turn(S, ST.at[0, 0], 0)
+    f_z(0, 0, 0)
+    for j in range(4):
+        a_x(1, j)
+    a_c(1, y)
+    a_yo(1, 0)
+    a_yo(1, 1)
+    f_z(0, 0, 1)
     attn_ready(0)
-    for l in LAY:
-        if l == 1:
-            attn_ready(1)
-        params(l)
-        project(l)
-        turn(S, ST.at[l, 0], 0)
-        attention(l)
-        if l == 0:
-            for k in ks:
-                f_z(0, k)
-        out_project(l)
-        norm(l, 0, MF.at[l, slot], None)
-        mid_exchange(l)
-        turn(AT, ST.at[l, 1], 0)
-        if l == 0:
-            for k in (0,) + ks:
-                f_x(0, k)
-        else:
-            for k in ks:
-                f_z(1, k)
-            for k in (0,) + ks:
-                f_x(1, k)
-        feed_forward(l)
-        extra = lambda rows, l=l: FD[l, slot, rows, :].astype(F32) + RY[l, rows, :].astype(F32)
-        norm(l, 1, y_ref if l == 1 else S, extra)
-    for i, (src, dst) in enumerate([(A, A_o), (F, F_o), (Q, Q_o), (ST, ST_o), (Pb, P_o), (TG, TG_o), (TT, TT_o), (N, N_o), (I, I_o), (PV, PV_o)]):
-        save(src, dst, i)
+    save(A.at[0], A_o.at[0], 0)
+    params(0)
+    project(0)
+    f_z(0, 0, 2)
+    f_z(0, 1, 0)
+    attention(0)
+    f_z(0, 1, 1)
+    f_z(0, 1, 2)
+    f_own_x(1, 0)
+    out_project(0)
+    norm(0, 0, MF.at[0, slot], None)
+    mid_exchange(0)
+    turn(AT, ST.at[0, 1], 0)
+    a_yo(1, 2)
+    a_yx(1, 0)
+    a_yx(1, 1)
+    feed_forward(
+        0,
+        before_up=[(f_own_x, 1, 1), (f_z, 1, 0, 0)],
+        before_down=[(f_z, 1, 0, 1)],
+        after_y=[(a_yx, 1, 2), (a_yx, 1, 3)],
+        before_ry=[(f_z, 1, 0, 2)],
+    )
+    save(F.at[0], F_o.at[0], 1)
+    save(TT.at[0], TT_o.at[0], 2)
+    save(TG.at[0], TG_o.at[0], 3)
+    feed = lambda l: lambda rows: FD[l, slot, rows, :].astype(F32) + RY[l, rows, :].astype(F32)
+    norm(0, 1, S, feed(0))
+    f_z(1, 1, 0)
+    attn_ready(1)
+    f_z(1, 1, 1)
+    save(A.at[1], A_o.at[1], 4)
+    params(1)
+    project(1)
+    attention(1)
+    f_z(1, 1, 2)
+    save(Pb, P_o, 5)
+    save(Q, Q_o, 6)
+    out_project(1)
+    norm(1, 0, MF.at[1, slot], None)
+    mid_exchange(1)
+    turn(S, ST.at[1, 0], 0)
+    turn(AT, ST.at[1, 1], 0)
+    save(ST, ST_o, 7)
+    feed_forward(1)
+    save(F.at[1], F_o.at[1], 8)
+    norm(1, 1, y_ref, feed(1))
+    save(TG.at[1], TG_o.at[1], 9)
+    save(TT.at[1], TT_o.at[1], 10)
+    save(N, N_o, 11)
+    save(I, I_o, 12)
+    save(PV, PV_o, 13)
     for copy in out_copies:
         copy.wait()
     ml.finish()
@@ -416,9 +540,11 @@
     vm = pl.BlockSpec(memory_space=pltpu.VMEM)
     return pl.pallas_call(
         forward_kernel,
-        out_shape=[jax.ShapeDtypeStruct((T, D), BF)] + [jax.ShapeDtypeStruct(s, d) for s, d in FWD_SHAPES],
-        in_specs=[vm] * 5 + [any_spec] * 5,
-        out_specs=[vm] + [any_spec] * len(FWD_SHAPES),
+        out_shape=[jax.ShapeDtypeStruct((T, D), BF)]
+        + [jax.ShapeDtypeStruct(s, d) for s, d in FWD_SHAPES]
+        + [jax.ShapeDtypeStruct((T, 128), F32)] * 2,
+        in_specs=[vm] * 3 + [any_spec] * 6,
+        out_specs=[vm] + [any_spec] * len(FWD_SHAPES) + [vm] * 2,
         scratch_shapes=[pltpu.VMEM(s, d) for s, d in FWD_SHAPES]
         + [
             pltpu.VMEM((T, D), BF),
@@ -430,18 +556,20 @@
             pltpu.VMEM((2, 4, T, D), BF),
             pltpu.VMEM((2, 2, T, D), BF),
             pltpu.VMEM((2, T, D), BF),
+            pltpu.VMEM((2, 2, 48, 4 * FS), BF),
+            pltpu.VMEM((2, 2, 2, 48, 2 * FS), BF),
             sems(2, 8),
             sems(2), sems(2),
+            sems(2, 5), sems(2, 3),
             sems(2, 4), sems(2, 4),
-            sems(2, 4), sems(2, 4),
-            sems(2, 8), sems(2, 8),
+            sems(2, 7), sems(2, 7),
             sems(2, 2), sems(2, 2),
-            sems(2, 4), sems(2, 4),
-            sems(2, 4), sems(2, 4),
+            sems(2, 2, 5), sems(2, 2, 3),
+            sems(2, 2, 4), sems(2, 2, 4),
             sems(2, 3), sems(2, 3),
             sems(2, 2), sems(2, 2),
             sems(2), sems(2),
-            sems(len(FWD_SHAPES)),
+            sems(14),
         ],
         compiler_params=pltpu.CompilerParams(collective_id=0, has_side_effects=True, vmem_limit_bytes=60 * 2**20),
         cost_estimate=pl.CostEstimate(flops=10**10, bytes_accessed=10**8, transcendentals=0),
@@ -480,7 +608,7 @@
 
     load(1, "PV", "N", "I", "TT", "F", "TG", "ST", "A", "P", "Q")
     U[...] = cot_ref[...].astype(F32)
-    greet(pc)
+    greet(pc.everyone())
 
     fcols = (pl.ds(2 * FS, D), pl.ds(0, FS), pl.ds(FS, FS))
 
@@ -847,15 +975,40 @@
     )(cot, cos, sin, *kept)
 
 
+def finish_kernel(gug, dng, af, qkv_o, out_o, gate_o, up_o, down_o, g1_o, b1_o, g2_o, b2_o):
+    for l in range(2):
+        for h in range(2):
+            qkv_o[l, :, h * QW:h * QW + QW] = af[l, h, :, 0:QW].astype(F32)
+            out_o[l, :, h * OW:h * OW + OW] = af[l, h, :, QW:QW + OW].astype(F32)
+            turned = af[l, h, :, QW + OW:].astype(F32).T
+            for i, ref in enumerate(((g1_o, b1_o), (g2_o, b2_o))[h]):
+                ref[l:l + 1, :] = turned[i:i + 1, :]
+            down_o[l, 96 * h:96 * h + 96, :] = dng[l, h].astype(F32)
+    def of(n, carry):
+        l, j = n // G, n % G
+        for w, ref in enumerate((gate_o, up_o)):
+            pairs = gug[l, w, :, :, :, tile(j // 4, 384)]
+            for m in range(4):
+                def put(m=m):
+                    pieces = [pairs[cc, yy, :, 96 * m:96 * m + 96].astype(F32) for cc in range(2) for yy in range(2)]
+                    ref[l, :, tile(j, 384)] = jnp.concatenate(pieces, axis=1)
+                pl.when(j % 4 == m)(put)
+        return carry
+    lax.fori_loop(0, 2 * G, of, 0)
+
+
 def epilogue(gug, dng, af):
-    def uncut(v):
-        return v.astype(F32).reshape(2, 2, 2, 48, G, 96).transpose(0, 3, 4, 1, 2, 5).reshape(2, 48, G * 4 * 96)
-    af = af.astype(F32)
-    both = lambda a, b: jnp.concatenate([af[:, 0, :, a:b], af[:, 1, :, a:b]], axis=-1)
-    return (
-        both(0, QW), both(QW, QW + OW), uncut(gug[:, 0]), uncut(gug[:, 1]), dng.astype(F32).reshape(2, 192, D),
-        af[:, 0, :, QW + OW], af[:, 0, :, QW + OW + 1], af[:, 1, :, QW + OW], af[:, 1, :, QW + OW + 1],
-    )
+    vm = pl.BlockSpec(memory_space=pltpu.VMEM)
+    shapes = [(2, 48, 3 * D), (2, 48, D), (2, 48, 4 * FS), (2, 48, 4 * FS), (2, 192, D)] + [(2, 48)] * 4
+    return tuple(pl.pallas_call(
+        finish_kernel,
+        out_shape=[jax.ShapeDtypeStruct(v, F32) for v in shapes],
+        in_specs=[vm] * 3,
+        out_specs=[vm] * len(shapes),
+        compiler_params=pltpu.CompilerParams(vmem_limit_bytes=40 * 2**20),
+        cost_estimate=pl.CostEstimate(flops=10**6, bytes_accessed=10**7, transcendentals=0),
+        name="finish",
+    )(gug, dng, af))
 
 
 def positions_of(segment_row):
@@ -874,19 +1027,11 @@
 
 def prologue(inputs, segment_ids, qkv_weight, out_weight, gate_weight, up_weight, down_weight,
              first_gain, first_bias, second_gain, second_bias):
-    seg = segment_ids[0]
-    cos, sin = rotary_tables(positions_of(seg))
-    cos = jnp.concatenate([cos] * 4, axis=1)
-    sin = jnp.concatenate([-sin, sin] * 2, axis=1)
-    segc = jnp.broadcast_to(seg[:, None], (T, 128))
-    segr = jnp.broadcast_to(seg[None, :], (8, T))
+    frequency = rope_base ** (-2.0 * np.arange(HEAD // 2, dtype=np.float32) / HEAD)
+    freq = jnp.asarray(np.tile(frequency.astype(np.float32)[None, :], (8, 4)))
     par = jnp.stack([jnp.stack([first_gain, first_bias], -1), jnp.stack([second_gain, second_bias], -1)], 1)
     par = jnp.pad(par, ((0, 0), (0, 0), (0, 0), (0, 126)))
-    def cut(w):
-        return w.reshape(2, 48, G, 2, 2, 96).transpose(0, 3, 4, 1, 2, 5).reshape(2, 2, 2, 48, FS)
-    gu = jnp.concatenate([cut(gate_weight), cut(up_weight)], -1)
-    dn = down_weight.reshape(2, 2, 96, D)
-    return inputs[0], cos, sin, segc, segr, qkv_weight, out_weight, par, gu, dn
+    return inputs[0], segment_ids, freq, qkv_weight, out_weight, par, gate_weight, up_weight, down_weight
 
 
 def rotate(values, cosine_table, sine_table):
@@ -1192,8 +1337,8 @@
             first_gain, first_bias, second_gain, second_bias, cotangent):
     staged = prologue(inputs, segment_ids, qkv_weight, out_weight, gate_weight, up_weight, down_weight,
                       first_gain, first_bias, second_gain, second_bias)
-    output, *kept = forward_call(staged)
-    gin, gug, dng, af = backward_call(cotangent[0], staged[1], staged[2], kept)
+    output, *kept, cos, sin = forward_call(staged)
+    gin, gug, dng, af = backward_call(cotangent[0], cos, sin, kept)
     return (output[None], gin[None]) + epilogue(gug, dng, af)
 
 

time: 443 us -> 372 us (0.84)
  Pallas kernels: 402 us -> 362 us
  local copies, waits for them, and re-layouts: 24.4 us -> 8.1 us
  other arithmetic: 9.88 us -> 0.73 us
    pallas_call x1, Pallas kernels: 196 us -> 150 us  [forward_call(): pl.pallas_call(forward_kernel, out_shape=[jax.ShapeDtypeStruct((T, D), BF...]
    reshape x12 -> x0, local copies, waits for them, and re-layouts: 14.4 us -> none  [the longest x6 11.4 us: uncut(): v.astype(F32).reshape(2, 2, 2, 48, G, 96).transpose(0, 3, 4, 1, 2, 5)]
    pallas_call x0 -> x1, Pallas kernels: none -> 6.33 us  [epilogue(): pl.pallas_call(finish_kernel, out_shape=[jax.ShapeDtypeStruct(v, F32) for...]
where the time goes in v2:
time: 372 us; the launch traced here: 371 us
  Pallas kernels  362 us (97%)
  local copies, waits for them, and re-layouts  8.1 us (2%)
    pallas_call x1, Pallas kernels, backward_call(): pl.pallas_call(backward_kernel, out_shape=[jax.ShapeDtypeStruct((T, D), F...  206 us
    pallas_call x1, Pallas kernels, forward_call(): pl.pallas_call(forward_kernel, out_shape=[jax.ShapeDtypeStruct((T, D), BF...  150 us

profile of v2, /device:TPU:0, one launch (start us, length us, event | category | flops | bytes accessed | tf_op | source)
XLA Modules:
  0.0 371.4 jit_solution(7731244962477103595)
XLA Ops:
  0.6 0.8 copy.41
  1.4 0.8 copy.42
  2.2 0.8 copy.43
  2.9 0.8 copy.44
  3.7 0.1 maximum_bitcast_fusion
  3.8 0.6 fusion.2.par_ref
  4.4 149.6 %forward.1 = (bf16[256,768]{1,0:T(8,128)(2,1)}, bf16[2,2,8,2,48,1664]{5,4,3,2,1,0:T(8,128)(2,1)}, bf16[2,768,2304]{2,1,0:T(8,128)(2,1)}, bf16[2,3,256,768]{3,2,1...) custom-call(bf16[256,768]{1,0:T(8,128)(2,1)} %bitcast.18, ...), custom_call_target="tpu_custom_call" | custom-call | flops 10000000000 | bytes 100000000 | tf_op jit(solution)/shard_map/forward/pallas_call | solution.py:541
  154.0 0.0 copy-start.4
  154.1 205.9 %backward.1 = (f32[256,768]{1,0:T(8,128)}, bf16[2,2,2,2,48,768]{5,4,3,2,1,0:T(8,128)(2,1)}, bf16[2,2,96,768]{3,2,1,0:T(8,128)(2,1)}, bf16[2,2,48,1664]{3,2,1,0:T(8,128)(2,1)}) custom-call(bf16[256,768]{1,0:T(8,128)(2,1)} %bitcast.19, f32[256,128]{1,0:T(8,128)} %get-tuple-element.38.cos_ref, f32[256,128]{1,0:T(8,128)} %get-tuple-element.39.sin_ref, ...), custom_call_target="tpu_custom_call" | custom-call | flops 20000000000 | bytes 100000000 | tf_op jit(solution)/shard_map/backward/pallas_call | solution.py:928
  360.0 0.0 copy-start
  360.0 1.3 copy-done
  361.2 0.0 copy-start.1
  361.2 1.1 copy-done.1
  362.3 0.0 copy-start.2
  362.3 1.1 copy-done.2
  363.4 0.0 copy-start.3
  363.4 6.3 %finish.1 = (f32[2,48,2304]{2,1,0:T(8,128)}, f32[2,48,768]{2,1,0:T(8,128)}, f32[2,48,3072]{2,1,0:T(8,128)}, f32[2,48,3072]{2,1,0:T(8,128)}, f32[2,192,768]{2,1,0...) custom-call(bf16[2,2,2,2,48,768]{5,4,3,2,1,0:T(8,128)(2,1)S(1)} %copy-done, ...), custom_call_target="tpu_custom_call" | custom-call | flops 1000000 | bytes 10000000 | tf_op jit(solution)/shard_map/finish/pallas_call | solution.py:1003
  369.7 0.0 copy-done.4
  369.7 0.7 copy.47
  370.5 0.0 copy-done.3
  370.5 0.9 copy.48
Async XLA Ops:
  154.0 215.7 %copy-start.4 = (bf16[256,768]{1,0:T(8,128)(2,1)S(1)}, bf16[256,768]{1,0:T(8,128)(2,1)}, u32[]{:S(2)}) copy-start(bf16[256,768]{1,0:T(8,128)(2,1)} %get-tuple-element.37) | copy-start | bytes 1179652
  360.0 1.3 copy-start
  361.2 1.1 copy-start.1
  362.3 1.1 copy-start.2
  363.4 7.1 %copy-start.3 = (f32[256,768]{1,0:T(8,128)S(1)}, f32[256,768]{1,0:T(8,128)}, u32[]{:S(2)}) copy-start(f32[256,768]{1,0:T(8,128)} %get-tuple-element.50) | copy-start | bytes 2359300

commit v3 on v2

--- a/solution.py
+++ b/solution.py
@@ -112,6 +112,11 @@
         copy.start()
         self.sent.append((tag, copy))
 
+    def later(self, src, dst, send_sem, recv_sem, who, cond):
+        copy = pltpu.make_async_remote_copy(src, dst, send_sem, recv_sem, device_id=who, device_id_type=MESH)
+        self.some.append((cond, copy))
+        return copy
+
     def send_if(self, cond, src, dst, send_sem, recv_sem, who):
         copy = pltpu.make_async_remote_copy(src, dst, send_sem, recv_sem, device_id=who, device_id_type=MESH)
         pl.when(cond)(copy.start)
@@ -248,19 +253,10 @@
         for j in range(4):
             ml.arrive(F.at[l, chip_rows(pc.chip_from(FOUR[j], 1 - x)), parts[p]], s_fx.at[l, p, j], r_fx.at[l, p, j], pc.xside())
 
-    def attn_ready(l):
-        for i in THREE:
-            a_y(l, i, x, i)
-        for j in range(4):
-            a_y(l, FOUR[j], 1 - x, 3 + j)
-        a_c(l, 1 - y)
-        a_c_arrive(l, y)
-        a_c_arrive(l, 1 - y)
-
     out_copies = []
 
-    def save(src, dst, i):
-        out_copies.append(ml.local(src, dst, os.at[i]))
+    def save(src, dst):
+        out_copies.append(ml.local(src, dst, os.at[len(out_copies)]))
 
     pair_mask = head_mask(T, 128)
     low_half = lax.broadcasted_iota(jnp.int32, (T, 128), 1) % HEAD < HEAD // 2
@@ -350,28 +346,26 @@
             return carry
         lax.fori_loop(0, T // 32, rows_of, 0)
 
-    def ffn_up(l, yy):
-        two = pl.ds(2 * yy, 2)
+    def ffn_up(l, first, count):
+        some = pl.ds(first, count)
         def cols_of(j, carry):
             cols = tile(j, 256)
-            xx = MF[l, two].reshape(2 * T, D)
+            xx = MF[l, some].reshape(count * T, D)
             gate = dot(xx, F[l, :, cols])
             up = dot(xx, F[l, :, pl.ds(pl.multiple_of(FS + j * 256, 256), 256)])
             act = gate * jax.nn.sigmoid(gate) * up
-            TG[l, 0, two, :, cols] = gate.astype(BF).reshape(2, T, 256)
-            TG[l, 1, two, :, cols] = up.astype(BF).reshape(2, T, 256)
-            AC[two, :, cols] = act.astype(BF).reshape(2, T, 256)
+            TG[l, 0, some, :, cols] = gate.astype(BF).reshape(count, T, 256)
+            TG[l, 1, some, :, cols] = up.astype(BF).reshape(count, T, 256)
+            AC[some, :, cols] = act.astype(BF).reshape(count, T, 256)
             return carry
         lax.fori_loop(0, FS // 256, cols_of, 0)
 
-    def ffn_down(l, yy, cc, add):
-        s_ = 2 * yy + cc
+    def ffn_down(l, s_, plus=None):
         def cols_of(j, carry):
             cols = tile(j, 256)
-            w = F[l, :, pl.ds(pl.multiple_of(2 * FS + j * 256, 256), 256)]
-            r = dot(AC[s_], w)
-            if add:
-                r = r + RC[l, yy, :, cols].astype(F32)
+            r = dot(AC[s_], F[l, :, pl.ds(pl.multiple_of(2 * FS + j * 256, 256), 256)])
+            if plus is not None:
+                r = r + plus[:, cols].astype(F32)
             FD[l, s_, :, cols] = r.astype(BF)
             return carry
         lax.fori_loop(0, D // 256, cols_of, 0)
@@ -389,129 +383,199 @@
             return carry
         lax.fori_loop(0, 4, slot_of, 0)
 
-    def mid_exchange(l):
+    def begin():
+        H[...] = x_ref[...].astype(F32)
+        S[...] = x_ref[...]
+        permute()
+        gu_send(0)
+        gu_send(1)
+
+    def projected(l):
+        params(l)
+        project(l)
+        turn(S, ST.at[l, 0], 0)
+
+    def scores(l):
+        attention(l)
+        save(Pb.at[l], P_o.at[l])
+        save(Q.at[l], Q_o.at[l])
+
+    def first_norm(l):
+        out_project(l)
+        norm(l, 0, MF.at[l, slot], None)
         mine = MF.at[l, slot]
         ml.send(mine, mine, s_m.at[l, 0], r_m.at[l, 0], pc.yside())
         ml.send(mine, mine, s_m.at[l, 1], r_m.at[l, 1], pc.core())
 
-    def feed_forward(l, before_up=(), before_down=(), after_y=(), before_ry=()):
-        run(before_up)
-        other_y = MF.at[l, 2 * (1 - y) + c]
+    def turn_attended(l):
+        turn(AT, ST.at[l, 1], 0)
+        save(ST.at[l], ST_o.at[l])
+
+    def half_sums(l, i, yy):
+        s_ = 2 * yy + 1 - c
+        ffn_down(l, s_)
+        ml.send(FD.at[l, s_], RC.at[l, yy], s_rc.at[l, i], r_rc.at[l, i], pc.core())
+
+    def own_up(l):
         ml.arrive(MF.at[l, 2 * y + 1 - c], s_m.at[l, 1], r_m.at[l, 1], pc.core())
         f_x(l, 0)
-        ffn_up(l, y)
-        ml.arrive(other_y, s_m.at[l, 0], r_m.at[l, 0], pc.yside())
-        ml.send(other_y, other_y, s_m.at[l, 2], r_m.at[l, 2], pc.core())
-        ml.arrive(MF.at[l, 2 * (1 - y) + 1 - c], s_m.at[l, 2], r_m.at[l, 2], pc.core())
-        ffn_up(l, 1 - y)
-        run(before_down)
+        ffn_up(l, 2 * y, 2)
+
+    def own_down(l):
         f_x(l, 1)
-        def to_core(i, yy):
-            ffn_down(l, yy, 1 - c, False)
-            ml.send(FD.at[l, 2 * yy + 1 - c], RC.at[l, yy], s_rc.at[l, i], r_rc.at[l, i], pc.core())
-        to_core(0, 1 - y)
+        half_sums(l, 1, y)
+        ffn_down(l, slot)
+
+    def pass_on(l):
+        block = MF.at[l, 2 * (1 - y) + c]
+        ml.arrive(block, s_m.at[l, 0], r_m.at[l, 0], pc.yside())
+        ml.send(block, block, s_m.at[l, 2], r_m.at[l, 2], pc.core())
+
+    def other_up(l):
+        others = 2 * (1 - y)
+        ffn_up(l, others + c, 1)
+        ml.arrive(MF.at[l, others + 1 - c], s_m.at[l, 2], r_m.at[l, 2], pc.core())
+        ffn_up(l, others + 1 - c, 1)
+
+    def other_down(l):
+        others = 2 * (1 - y)
+        half_sums(l, 0, 1 - y)
         ml.arrive(RC.at[l, 1 - y], s_rc.at[l, 0], r_rc.at[l, 0], pc.core())
-        ffn_down(l, 1 - y, c, True)
-        ml.send(FD.at[l, 2 * (1 - y) + c], RY.at[l], s_ry.at[l], r_ry.at[l], pc.yside())
-        run(after_y)
-        to_core(1, y)
+        ffn_down(l, others + c, RC.at[l, 1 - y])
+        ml.send(FD.at[l, others + c], RY.at[l], s_ry.at[l], r_ry.at[l], pc.yside())
+
+    def turn_middle(l):
+        turn_slots(MF.at[l], TT.at[l, 0])
+
+    def turn_activated(l):
+        turn_slots(AC, TT.at[l, 1])
+        save(F.at[l], F_o.at[l])
+        save(TT.at[l], TT_o.at[l])
+        save(TG.at[l], TG_o.at[l])
+
+    def second_norm(l):
         ml.arrive(RC.at[l, y], s_rc.at[l, 1], r_rc.at[l, 1], pc.core())
-        ffn_down(l, y, c, True)
-        turn_slots(MF.at[l], TT.at[l, 0])
-        turn_slots(AC, TT.at[l, 1])
-        run(before_ry)
         ml.arrive(RY.at[l], s_ry.at[l], r_ry.at[l], pc.yside())
-
-    def run(steps):
-        for step, *what in steps:
-            step(*what)
+        feed = lambda rows: FD[l, slot, rows, :].astype(F32) + RC[l, y, rows, :].astype(F32) + RY[l, rows, :].astype(F32)
+        norm(l, 1, S if l == 0 else y_ref, feed)
+
+    def ay_arrive(l, n):
+        if n < 3:
+            a_y(l, n, x, n)
+        else:
+            a_y(l, FOUR[n - 3], 1 - x, n)
+
+    def ac_own(l):
+        a_c(l, y)
+
+    def ac_other(l):
+        a_c(l, 1 - y)
+
+    def attn_ready(l):
+        a_c_arrive(l, y)
+        a_c_arrive(l, 1 - y)
+        save(A.at[l], A_o.at[l])
 
     a_own(0)
+    begin()
+    f_ready(0)
     a_own(1)
-    permute()
-    gu_send(0)
-    gu_send(1)
-    H[...] = x_ref[...].astype(F32)
-    S[...] = x_ref[...]
-    for i in THREE:
-        a_z(0, i)
-        a_yo(0, i)
-    f_ready(0)
+    a_z(0, 0)
+    tables()
+    a_yo(0, 0)
+    f_own_x(0, 0)
+    a_x(0, 0)
+    f_own_z(0, 1)
+    a_yx(0, 0)
+    a_z(0, 1)
+    a_z(1, 0)
+    a_z(0, 2)
+    a_x(1, 0)
+    a_x(0, 1)
+    f_z(0, 1, 0)
+    ay_arrive(0, 0)
+    a_yo(0, 1)
     f_own_z(0, 0)
-    f_own_z(0, 1)
+    a_yo(0, 2)
+    a_yo(1, 0)
+    a_yx(0, 1)
+    a_x(0, 2)
+    ay_arrive(0, 1)
+    ay_arrive(0, 2)
+    a_z(1, 1)
+    a_z(1, 2)
+    a_yx(0, 2)
+    a_x(0, 3)
+    a_yx(0, 3)
     f_ready(1)
-    for j in range(4):
-        a_x(0, j)
-        a_yx(0, j)
-    a_c(0, y)
-    f_own_x(0, 0)
-    for i in THREE:
-        a_z(1, i)
+    a_x(1, 1)
+    f_z(0, 0, 0)
+    f_z(0, 0, 1)
+    ay_arrive(0, 3)
+    ac_own(0)
+    ay_arrive(0, 4)
+    ay_arrive(0, 5)
+    a_yo(1, 1)
+    a_yx(1, 0)
     f_own_x(0, 1)
+    ay_arrive(0, 6)
+    ac_other(0)
+    a_x(1, 2)
+    a_yo(1, 2)
+    f_z(0, 0, 2)
+    attn_ready(0)
     f_own_z(1, 0)
+    ay_arrive(1, 0)
+    a_yx(1, 1)
+    a_x(1, 3)
+    ay_arrive(1, 1)
+    projected(0)
+    scores(0)
+    first_norm(0)
+    ay_arrive(1, 2)
+    f_z(0, 1, 1)
+    ac_own(1)
+    ay_arrive(1, 3)
+    f_z(0, 1, 2)
+    a_yx(1, 2)
+    f_z(1, 0, 0)
+    f_own_x(1, 1)
+    f_z(1, 0, 1)
+    ay_arrive(1, 4)
+    own_up(0)
+    pass_on(0)
+    turn_attended(0)
+    a_yx(1, 3)
+    other_up(0)
     f_own_z(1, 1)
-    tables()
-    turn(S, ST.at[0, 0], 0)
-    f_z(0, 0, 0)
-    for j in range(4):
-        a_x(1, j)
-    a_c(1, y)
-    a_yo(1, 0)
-    a_yo(1, 1)
-    f_z(0, 0, 1)
-    attn_ready(0)
-    save(A.at[0], A_o.at[0], 0)
-    params(0)
-    project(0)
-    f_z(0, 0, 2)
-    f_z(0, 1, 0)
-    attention(0)
-    f_z(0, 1, 1)
-    f_z(0, 1, 2)
     f_own_x(1, 0)
-    out_project(0)
-    norm(0, 0, MF.at[0, slot], None)
-    mid_exchange(0)
-    turn(AT, ST.at[0, 1], 0)
-    a_yo(1, 2)
-    a_yx(1, 0)
-    a_yx(1, 1)
-    feed_forward(
-        0,
-        before_up=[(f_own_x, 1, 1), (f_z, 1, 0, 0)],
-        before_down=[(f_z, 1, 0, 1)],
-        after_y=[(a_yx, 1, 2), (a_yx, 1, 3)],
-        before_ry=[(f_z, 1, 0, 2)],
-    )
-    save(F.at[0], F_o.at[0], 1)
-    save(TT.at[0], TT_o.at[0], 2)
-    save(TG.at[0], TG_o.at[0], 3)
-    feed = lambda l: lambda rows: FD[l, slot, rows, :].astype(F32) + RY[l, rows, :].astype(F32)
-    norm(0, 1, S, feed(0))
+    ay_arrive(1, 5)
+    own_down(0)
+    other_down(0)
+    ay_arrive(1, 6)
+    f_z(1, 0, 2)
+    ac_other(1)
+    turn_middle(0)
     f_z(1, 1, 0)
+    f_z(1, 1, 1)
     attn_ready(1)
-    f_z(1, 1, 1)
-    save(A.at[1], A_o.at[1], 4)
-    params(1)
-    project(1)
-    attention(1)
+    second_norm(0)
+    projected(1)
+    scores(1)
+    first_norm(1)
     f_z(1, 1, 2)
-    save(Pb, P_o, 5)
-    save(Q, Q_o, 6)
-    out_project(1)
-    norm(1, 0, MF.at[1, slot], None)
-    mid_exchange(1)
-    turn(S, ST.at[1, 0], 0)
-    turn(AT, ST.at[1, 1], 0)
-    save(ST, ST_o, 7)
-    feed_forward(1)
-    save(F.at[1], F_o.at[1], 8)
-    norm(1, 1, y_ref, feed(1))
-    save(TG.at[1], TG_o.at[1], 9)
-    save(TT.at[1], TT_o.at[1], 10)
-    save(N, N_o, 11)
-    save(I, I_o, 12)
-    save(PV, PV_o, 13)
+    turn_activated(0)
+    own_up(1)
+    own_down(1)
+    pass_on(1)
+    other_up(1)
+    other_down(1)
+    turn_middle(1)
+    turn_attended(1)
+    turn_activated(1)
+    second_norm(1)
+    for src, dst in ((N, N_o), (I, I_o), (PV, PV_o)):
+        save(src, dst)
     for copy in out_copies:
         copy.wait()
     ml.finish()
@@ -569,7 +633,7 @@
             sems(2, 3), sems(2, 3),
             sems(2, 2), sems(2, 2),
             sems(2), sems(2),
-            sems(14),
+            sems(17),
         ],
         compiler_params=pltpu.CompilerParams(collective_id=0, has_side_effects=True, vmem_limit_bytes=60 * 2**20),
         cost_estimate=pl.CostEstimate(flops=10**10, bytes_accessed=10**8, transcendentals=0),
@@ -581,7 +645,7 @@
     cot_ref, cos_ref, sin_ref, A_i, F_i, Q_i, ST_i, P_i, TG_i, TT_i, N_i, I_i, PV_i,
     gin_ref, GUG, DNG, AF,
     A, F, Q, ST, Pb, TG, TT, N, I, PV,
-    U, GF, GB, GA, GP, FD, RC, RY, FG, RFX, RFZ, FR, AG, RAC, RAY, RAX, RAZ, V,
+    U, GF, GB, GP, FD, RC, RY, FG, RFX, RFZ, FR, AG, RAC, RAY, RAX, RAZ, V,
     ls, s_m, r_m, s_rc, r_rc, s_ry, r_ry,
     s_fx, r_fx, s_fz, r_fz, s_fc, r_fc, s_fy, r_fy,
     s_ac, r_ac, s_ay, r_ay, s_ax, r_ax, s_az, r_az, s_af, r_af,
@@ -589,7 +653,10 @@
     pc = Place()
     y, z, x, c, slot = pc.y, pc.z, pc.x, pc.c, pc.slot
     ml = Mail()
-    ks = (1, 3, 2)
+    mid = z % 3 != 0
+    zn = pc.near()
+    near, across = pc.zto(zn), pc.zto(3 - z)
+    planes = (3 - zn, 3 - z, zn, z)
     places = {
         "PV": (PV_i, PV, 0), "N": (N_i, N, 1), "I": (I_i, I, 2), "TT": (TT_i, TT, 3), "F": (F_i, F, 4), "TG": (TG_i, TG, 5),
         "ST": (ST_i, ST, 6), "A": (A_i, A, 7), "P": (P_i, Pb, 8), "Q": (Q_i, Q, 9),
@@ -608,33 +675,76 @@
 
     load(1, "PV", "N", "I", "TT", "F", "TG", "ST", "A", "P", "Q")
     U[...] = cot_ref[...].astype(F32)
-    greet(pc.everyone())
+    greet(pc.line())
 
     fcols = (pl.ds(2 * FS, D), pl.ds(0, FS), pl.ds(FS, FS))
 
     def fx_send(l, j):
-        ml.send(FG.at[:, 1 - x, :, fcols[j]], RFX.at[l, j], s_fx.at[l, j], r_fx.at[l, j], pc.xside(), ("fx", l, j))
-
-    def fx_task(l, j):
-        ml.arrive(RFX.at[l, j], s_fx.at[l, j], r_fx.at[l, j], pc.xside())
-        def add(zz, carry):
+        for n in range(4):
+            ml.send(FG.at[planes[n], 1 - x, :, fcols[j]], RFX.at[l, j, planes[n]], s_fx.at[l, j, n], r_fx.at[l, j, n], pc.xside(), ("fx", l, j))
+
+    def line_start(n, part, R, ss, rs):
+        slot_of = (1, 2, 0)[n]
+        ml.send_if(z % 3 == 0, part(planes[n]), R.at[slot_of], ss.at[n], rs.at[slot_of], near)
+
+    def plus(dst, src, rows, widths):
+        for r in range(0, rows, 48):
+            at = 0
+            for w in widths:
+                here = (pl.ds(r, 48), pl.ds(at, w))
+                dst[here] = (dst[here].astype(F32) + src[here].astype(F32)).astype(BF)
+                at += w
+
+    def line_middle(part, R, ss, rs, rows, widths):
+        far = [pltpu.make_async_remote_copy(R.at[n], R.at[n], ss.at[0], rs.at[n], device_id=near, device_id_type=MESH) for n in (1, 2)]
+        on = [
+            ml.later(part(plane), R.at[3 + n], ss.at[3 + n], rs.at[3 + n], across, mid)
+            for n, plane in enumerate((3 - z, 3 - zn))
+        ]
+        dsts = [part(3 - z), part(3 - zn)]
+        def go():
+            for n in range(2):
+                far[n].wait_recv()
+                plus(dsts[n], R.at[1 + n], rows, widths)
+                on[n].start()
+        pl.when(mid)(go)
+
+    def line_end(part, R, ss, rs, rows, widths):
+        back = [pltpu.make_async_remote_copy(R.at[n], R.at[n], ss.at[0], rs.at[n], device_id=across, device_id_type=MESH) for n in (3, 4)]
+        last = ml.later(part(zn), R.at[0], ss.at[5], rs.at[0], near, mid)
+        dsts = [part(z), part(zn)]
+        def go():
+            back[1].wait_recv()
+            plus(dsts[1], R.at[4], rows, widths)
+            last.start()
+            back[0].wait_recv()
+            plus(dsts[0], R.at[3], rows, widths)
+        pl.when(mid)(go)
+        ml.arrive(R.at[0], ss.at[0], rs.at[0], near)
+
+    FW, AWS = (D,), (768, 896)
+
+    def fpart(l, j):
+        return lambda zz: RFX.at[l, j, zz]
+
+    def fx_task(l, j, n):
+        if True:
+            p = planes[n]
+            ml.arrive(RFX.at[l, j, p], s_fx.at[l, j, n], r_fx.at[l, j, n], pc.xside())
             for half in range(2):
                 rows = pl.ds(48 * half, 48)
-                RFX[l, j, zz, rows, :] = (RFX[l, j, zz, rows, :].astype(F32) + FG[zz, x, rows, fcols[j]].astype(F32)).astype(BF)
-            return carry
-        lax.fori_loop(0, 4, add, 0)
-        for k in ks:
-            ml.send(RFX.at[l, j, (z + k) % 4], RFZ.at[l, j, k - 1], s_fz.at[l, j, k], r_fz.at[l, j, k], pc.zside(k))
+                RFX[l, j, p, rows, :] = (RFX[l, j, p, rows, :].astype(F32) + FG[p, x, rows, fcols[j]].astype(F32)).astype(BF)
+            if n < 3:
+                line_start(n, fpart(l, j), RFZ.at[l, j], s_fz.at[l, j], r_fz.at[l, j])
+
+    def fm_task(l, j):
+        line_middle(fpart(l, j), RFZ.at[l, j], s_fz.at[l, j], r_fz.at[l, j], 96, FW)
 
     def fz_task(l, j):
-        for k in ks:
-            ml.arrive(RFZ.at[l, j, k - 1], s_fz.at[l, j, k], r_fz.at[l, j, k], pc.zside(k))
+        line_end(fpart(l, j), RFZ.at[l, j], s_fz.at[l, j], r_fz.at[l, j], 96, FW)
         def total(start):
             rows = pl.ds(start, 48)
-            t = RFX[l, j, z, rows, :].astype(F32)
-            for k in range(3):
-                t = t + RFZ[l, j, k, rows, :].astype(F32)
-            return t.astype(BF)
+            return (RFX[l, j, z, rows, :].astype(F32) + RFZ[l, j, 0, rows, :].astype(F32)).astype(BF)
         if j == 0:
             for half in range(2):
                 DNG[l, y, pl.ds(48 * half, 48), :] = total(48 * half)
@@ -653,54 +763,54 @@
         block = DNG.at[l, 1 - y] if j == 0 else GUG.at[l, j - 1, :, 1 - y]
         ml.arrive(block, s_fy.at[l, j], r_fy.at[l, j], pc.yside())
 
-    def ac_send(l, i):
+    acols = (pl.ds(0, QW), pl.ds(QW, AW - QW))
+    awide = ((768, 384), (512,))
+
+    def ac_send(l, p, i):
         h = (1 - y, y)[i]
-        ml.send(AG.at[h, :, :, 1 - c], RAC.at[l, i], s_ac.at[l, i], r_ac.at[l, i], pc.core(), ("ac", l))
-
-    def ac_task(l, i):
+        ml.send(AG.at[h, :, :, 1 - c, :, acols[p]], RAC.at[l, i, :, :, :, acols[p]], s_ac.at[l, p, i], r_ac.at[l, p, i], pc.core(), ("ac", l))
+
+    def ac_sum(l, p, i):
         h = (1 - y, y)[i]
-        ml.arrive(RAC.at[l, i], s_ac.at[l, i], r_ac.at[l, i], pc.core())
+        ml.arrive(RAC.at[l, i, :, :, :, acols[p]], s_ac.at[l, p, i], r_ac.at[l, p, i], pc.core())
         def add(n, carry):
             zz, xx = n // 2, n % 2
-            for cols in (pl.ds(0, 768), pl.ds(768, 896)):
-                RAC[l, i, zz, xx, :, cols] = (RAC[l, i, zz, xx, :, cols].astype(F32) + AG[h, zz, xx, c, :, cols].astype(F32)).astype(BF)
+            plus(RAC.at[l, i, zz, xx, :, acols[p]], AG.at[h, zz, xx, c, :, acols[p]], 48, awide[p])
             return carry
         lax.fori_loop(0, 8, add, 0)
-        if i == 0:
-            ml.send(RAC.at[l, 0], RAY.at[l], s_ay.at[l], r_ay.at[l], pc.yside())
-
-    def ay_task(l):
-        ml.arrive(RAY.at[l], s_ay.at[l], r_ay.at[l], pc.yside())
-        def add(n, carry):
-            zz, xx = n // 2, n % 2
-            for cols in (pl.ds(0, 768), pl.ds(768, 896)):
-                RAC[l, 1, zz, xx, :, cols] = (RAC[l, 1, zz, xx, :, cols].astype(F32) + RAY[l, zz, xx, :, cols].astype(F32)).astype(BF)
-            return carry
-        lax.fori_loop(0, 8, add, 0)
-        ml.send(RAC.at[l, 1, :, 1 - x], RAX.at[l], s_ax.at[l], r_ax.at[l], pc.xside())
-
-    def ax_task(l):
-        ml.arrive(RAX.at[l], s_ax.at[l], r_ax.at[l], pc.xside())
-        def add(zz, carry):
-            for cols in (pl.ds(0, 768), pl.ds(768, 896)):
-                RAX[l, zz, :, cols] = (RAX[l, zz, :, cols].astype(F32) + RAC[l, 1, zz, x, :, cols].astype(F32)).astype(BF)
-            return carry
-        lax.fori_loop(0, 4, add, 0)
-        for k in ks:
-            ml.send(RAX.at[l, (z + k) % 4], RAZ.at[l, k - 1], s_az.at[l, k], r_az.at[l, k], pc.zside(k))
-
-    def az_task(l):
-        for k in ks:
-            ml.arrive(RAZ.at[l, k - 1], s_az.at[l, k], r_az.at[l, k], pc.zside(k))
-        for cols in (pl.ds(0, 768), pl.ds(768, 896)):
-            t = RAX[l, z, :, cols].astype(F32)
-            for k in range(3):
-                t = t + RAZ[l, k, :, cols].astype(F32)
-            AF[l, y, :, cols] = t.astype(BF)
-        ml.send(AF.at[l, y], AF.at[l, y], s_af.at[l], r_af.at[l], pc.yside())
-
-    def af_task(l):
-        ml.arrive(AF.at[l, 1 - y], s_af.at[l], r_af.at[l], pc.yside())
+
+    def ay_send(l, p, n):
+        q = planes[n]
+        ml.send(RAC.at[l, 0, q, :, :, acols[p]], RAY.at[l, q, :, :, acols[p]], s_ay.at[l, p, n], r_ay.at[l, p, n], pc.yside())
+
+    def ay_task(l, p, n):
+        q = planes[n]
+        ml.arrive(RAY.at[l, q, :, :, acols[p]], s_ay.at[l, p, n], r_ay.at[l, p, n], pc.yside())
+        for xx in range(2):
+            plus(RAC.at[l, 1, q, xx, :, acols[p]], RAY.at[l, q, xx, :, acols[p]], 48, awide[p])
+        ml.send(RAC.at[l, 1, q, 1 - x, :, acols[p]], RAX.at[l, q, :, acols[p]], s_ax.at[l, p, n], r_ax.at[l, p, n], pc.xside())
+
+    def apart(l, p):
+        return lambda zz: RAX.at[l, zz, :, acols[p]]
+
+    def ax_task(l, p, n):
+        q = planes[n]
+        ml.arrive(RAX.at[l, q, :, acols[p]], s_ax.at[l, p, n], r_ax.at[l, p, n], pc.xside())
+        plus(RAX.at[l, q, :, acols[p]], RAC.at[l, 1, q, x, :, acols[p]], 48, awide[p])
+        if n < 3:
+            line_start(n, apart(l, p), RAZ.at[l, :, :, acols[p]], s_az.at[l, p], r_az.at[l, p])
+
+    def am_task(l, p):
+        line_middle(apart(l, p), RAZ.at[l, :, :, acols[p]], s_az.at[l, p], r_az.at[l, p], 48, awide[p])
+
+    def az_task(l, p):
+        line_end(apart(l, p), RAZ.at[l, :, :, acols[p]], s_az.at[l, p], r_az.at[l, p], 48, awide[p])
+        mine = AF.at[l, y, :, acols[p]]
+        mine[...] = (RAX[l, z, :, acols[p]].astype(F32) + RAZ[l, 0, :, acols[p]].astype(F32)).astype(BF)
+        ml.send(mine, mine, s_af.at[l, p], r_af.at[l, p], pc.yside())
+
+    def af_task(l, p):
+        ml.arrive(AF.at[l, 1 - y, :, acols[p]], s_af.at[l, p], r_af.at[l, p], pc.yside())
 
     pair_mask = head_mask(T, 128)
     low_half = lax.broadcasted_iota(jnp.int32, (T, 128), 1) % HEAD < HEAD // 2
@@ -729,28 +839,27 @@
         row = lax.broadcasted_iota(jnp.int32, (8, D), 0)
         V[i] = jnp.where(row == 0, gs.sum(0, keepdims=True), jnp.where(row == 1, bs.sum(0, keepdims=True), 0.0))
 
-    def act_back(l, yy):
-        two = pl.ds(2 * yy, 2)
+    def act_back(l, first, count):
+        some = pl.ds(first, count)
         def cols_of(j, carry):
             cols = tile(j, 256)
-            ga = dot_t(GF[l, two].reshape(2 * T, D), F[cols, 2 * FS:])
-            gate = TG[0, two, :, cols].reshape(2 * T, 256).astype(F32)
-            up = TG[1, two, :, cols].reshape(2 * T, 256).astype(F32)
+            ga = dot_t(GF[l, some].reshape(count * T, D), F[cols, 2 * FS:])
+            gate = TG[0, some, :, cols].reshape(count * T, 256).astype(F32)
+            up = TG[1, some, :, cols].reshape(count * T, 256).astype(F32)
             sg = jax.nn.sigmoid(gate)
             gg = ga * up * sg * (1.0 + gate * (1.0 - sg))
             gu = ga * gate * sg
-            TG[0, two, :, cols] = gg.astype(BF).reshape(2, T, 256)
-            TG[1, two, :, cols] = gu.astype(BF).reshape(2, T, 256)
+            TG[0, some, :, cols] = gg.astype(BF).reshape(count, T, 256)
+            TG[1, some, :, cols] = gu.astype(BF).reshape(count, T, 256)
             return carry
         lax.fori_loop(0, FS // 256, cols_of, 0)
 
-    def mid_back(yy, cc, add, l):
-        s_ = 2 * yy + cc
+    def mid_back(s_, plus=None):
         def cols_of(j, carry):
             cols = tile(j, 256)
             r = dot_t(TG[0, s_], F[cols, 0:FS]) + dot_t(TG[1, s_], F[cols, FS:2 * FS])
-            if add:
-                r = r + RC[l, yy, :, cols].astype(F32)
+            if plus is not None:
+                r = r + plus[:, cols].astype(F32)
             FD[s_, :, cols] = r.astype(BF)
             return carry
         lax.fori_loop(0, D // 256, cols_of, 0)
@@ -768,18 +877,6 @@
             return carry
         lax.fori_loop(0, 3, cols_of, 0)
 
-    def mid_sums(l):
-        def to_core(i, yy):
-            mid_back(yy, 1 - c, False, l)
-            ml.send(FD.at[2 * yy + 1 - c], RC.at[l, yy], s_rc.at[l, i], r_rc.at[l, i], pc.core(), ("fd", l))
-        to_core(0, 1 - y)
-        ml.arrive(RC.at[l, 1 - y], s_rc.at[l, 0], r_rc.at[l, 0], pc.core())
-        mid_back(1 - y, c, True, l)
-        ml.send(FD.at[2 * (1 - y) + c], RY.at[l], s_ry.at[l], r_ry.at[l], pc.yside(), ("fd", l))
-        to_core(1, y)
-        ml.arrive(RC.at[l, y], s_rc.at[l, 1], r_rc.at[l, 1], pc.core())
-        mid_back(y, c, True, l)
-
     def out_back():
         acc = None
         for h in range(2):
@@ -788,12 +885,12 @@
         for h in range(2):
             t = dot_t(GB[:, h * OW:h * OW + OW], A[h, :, :, :, QW:QW + OW].reshape(D, OW))
             acc = t if acc is None else acc + t
-        GA[...] = acc.astype(BF)
+        GP[2] = acc.astype(BF)
 
     def attention_back():
         def pair(p, carry):
             cols = tile(p, 128)
-            q, kk, v, ga = Q[0, :, cols], Q[1, :, cols], Q[2, :, cols], GA[:, cols]
+            q, kk, v, ga = Q[0, :, cols], Q[1, :, cols], Q[2, :, cols], GP[2, :, cols]
             dq, dk, dv = [], [], []
             for h in range(2):
                 pl_ = Pb[2 * p + h]
@@ -835,90 +932,225 @@
             acc = acc + dot_t(gp_chunk(j), A[j // 3, :, :, :, off:off + 384].reshape(D, 384))
         U[...] = acc
 
-    for l in (1, 0):
+    def run(steps):
+        for step, *what in steps:
+            step(*what)
+
+    def upper(l):
         need("PV", "N", "I")
         norm_back(1, None, GF.at[l, slot])
         mine = GF.at[l, slot]
         ml.send(mine, mine, s_m.at[l, 0], r_m.at[l, 0], pc.yside())
         ml.send(mine, mine, s_m.at[l, 1], r_m.at[l, 1], pc.core())
-        if l == 0:
-            ml.gone(("fd", 1))
-            ay_task(1)
-            fz_task(1, 0)
+
+    def half_sums(l, i, yy):
+        s_ = 2 * yy + 1 - c
+        mid_back(s_)
+        ml.send(FD.at[s_], RC.at[yy], s_rc.at[l, i], r_rc.at[l, i], pc.core(), ("fd", l))
+
+    def own_tokens(l):
         need("TT", "F", "TG")
+        ml.gone(("fd", 1))
         ml.arrive(GF.at[l, 2 * y + 1 - c], s_m.at[l, 1], r_m.at[l, 1], pc.core())
-        act_back(l, y)
-        other = GF.at[l, 2 * (1 - y) + c]
-        ml.arrive(other, s_m.at[l, 0], r_m.at[l, 0], pc.yside())
-        ml.send(other, other, s_m.at[l, 2], r_m.at[l, 2], pc.core())
-        ml.arrive(GF.at[l, 2 * (1 - y) + 1 - c], s_m.at[l, 2], r_m.at[l, 2], pc.core())
-        ml.gone(("fx", 1, 0)) if l == 0 else None
-        weight_grad(l, 0)
-        fx_send(l, 0)
-        act_back(l, 1 - y)
-        mid_sums(l)
+        act_back(l, 2 * y, 2)
+        half_sums(l, 1, y)
+        mid_back(slot)
+
+    def other_tokens(l):
+        others = 2 * (1 - y)
+        block = GF.at[l, others + c]
+        ml.arrive(block, s_m.at[l, 0], r_m.at[l, 0], pc.yside())
+        ml.send(block, block, s_m.at[l, 2], r_m.at[l, 2], pc.core())
+        act_back(l, others + c, 1)
+        ml.arrive(GF.at[l, others + 1 - c], s_m.at[l, 2], r_m.at[l, 2], pc.core())
+        act_back(l, others + 1 - c, 1)
+
+    def other_sums(l):
+        others = 2 * (1 - y)
+        half_sums(l, 0, 1 - y)
+        ml.arrive(RC.at[1 - y], s_rc.at[l, 0], r_rc.at[l, 0], pc.core())
+        mid_back(others + c, RC.at[1 - y])
+        ml.send(FD.at[others + c], RY, s_ry.at[l], r_ry.at[l], pc.yside(), ("fd", l))
         if l == 1:
             load(0, "F")
-        ml.gone(("fx", 1, 1)) if l == 0 else None
-        weight_grad(l, 1)
-        fx_send(l, 1)
-        ml.gone(("fx", 1, 2)) if l == 0 else None
-        weight_grad(l, 2)
-        fx_send(l, 2)
+
+    def weights(l, j):
+        ml.gone(("fx", 1, j) if l == 0 else None)
+        weight_grad(l, j)
+        fx_send(l, j)
+        if l == 1 and j == 2:
+            load(0, "TT", "TG")
+
+    def middle(l):
+        ml.arrive(RC.at[y], s_rc.at[l, 1], r_rc.at[l, 1], pc.core())
+        ml.arrive(RY, s_ry.at[l], r_ry.at[l], pc.yside())
+        norm_back(0, lambda rows: FD[slot, rows, :].astype(F32) + RC[y, rows, :].astype(F32) + RY[rows, :].astype(F32), GB)
         if l == 1:
-            load(0, "TT", "TG")
-        ml.arrive(RY.at[l], s_ry.at[l], r_ry.at[l], pc.yside())
-        norm_back(0, lambda rows: FD[slot, rows, :].astype(F32) + RY[l, rows, :].astype(F32), GB)
-        if l == 1:
-            load(0, "N", "I")
+            load(0, "PV", "N", "I")
+
+    QKV, OUT = 0, 1
+
+    def out_sums(l):
+        need("ST", "A")
         if l == 0:
-            ax_task(1)
-            fz_task(1, 1)
-            fz_task(1, 2)
-            fc_task(1, 1)
-            fc_task(1, 2)
-        need("ST", "A")
+            ml.gone(("ac", 1))
         param_grad()
         out_back()
-        if l == 1:
-            load(0, "PV")
-        fx_task(l, 0)
+        for i in range(2):
+            ac_send(l, OUT, i)
+
+    def scores(l):
         need("P", "Q")
         attention_back()
         if l == 1:
             load(0, "P", "Q")
-        for i in range(2):
-            for h in range(2):
-                pass
+
+    def below(l):
+        input_back()
+        if l == 0:
+            gin_ref[...] = U[...]
+
+    def qkv_sums(l):
         qkv_grad(0)
         qkv_grad(1)
-        ac_send(l, 0)
-        ac_send(l, 1)
+        for i in range(2):
+            ac_send(l, QKV, i)
         if l == 1:
-            load(0, "ST")
-        fx_task(l, 1)
-        input_back()
-        if l == 1:
-            load(0, "A")
-        fx_task(l, 2)
-        ac_task(l, 0)
-        ac_task(l, 1)
-        if l == 1:
-            ml.gone(("ac", 1))
-    gin_ref[...] = U[...]
-    ay_task(0)
-    az_task(1)
+            load(0, "ST", "A")
+
+    upper(1)
+    own_tokens(1)
+    other_tokens(1)
+    other_sums(1)
+    weights(1, 0)
+    weights(1, 1)
+    weights(1, 2)
+    fx_task(1, 0, 0)
+    middle(1)
+    out_sums(1)
+    scores(1)
+    ac_sum(1, 1, 0)
+    ay_send(1, 1, 0)
+    below(1)
+    upper(0)
+    fx_task(1, 1, 0)
+    fx_task(1, 0, 1)
+    qkv_sums(1)
+    ay_send(1, 1, 1)
+    own_tokens(0)
+    ay_send(1, 1, 2)
+    fx_task(1, 1, 1)
+    ac_sum(1, 0, 0)
+    fm_task(1, 0)
+    fx_task(1, 0, 2)
+    ay_send(1, 0, 0)
+    ac_sum(1, 1, 1)
+    ac_sum(1, 0, 1)
+    ay_task(1, 1, 0)
+    other_tokens(0)
+    fx_task(1, 2, 0)
+    ay_send(1, 1, 3)
+    fx_task(1, 1, 2)
+    fm_task(1, 1)
+    fx_task(1, 0, 3)
+    other_sums(0)
+    weights(0, 0)
+    fx_task(1, 1, 3)
+    fz_task(1, 1)
+    ay_send(1, 0, 1)
+    fx_task(1, 2, 1)
+    ax_task(1, 1, 0)
+    weights(0, 1)
+    ay_send(1, 0, 2)
+    fx_task(0, 0, 0)
+    fx_task(1, 2, 2)
+    ay_task(1, 1, 1)
+    middle(0)
+    out_sums(0)
+    scores(0)
+    ay_send(1, 0, 3)
+    qkv_sums(0)
+    fx_task(1, 2, 3)
+    ac_sum(0, 1, 1)
+    fx_task(0, 1, 0)
+    fx_task(0, 0, 1)
+    ac_sum(0, 1, 0)
+    ay_send(0, 1, 0)
+    ay_task(1, 0, 0)
+    ay_send(0, 1, 1)
+    fm_task(1, 2)
+    ac_sum(0, 0, 0)
+    weights(0, 2)
+    ac_sum(0, 0, 1)
+    ay_send(0, 1, 2)
+    fx_task(0, 1, 1)
+    ay_task(0, 1, 0)
+    ay_send(0, 0, 0)
+    ay_send(0, 0, 1)
+    fx_task(0, 0, 2)
+    ay_send(0, 0, 2)
+    fm_task(0, 0)
+    fc_task(1, 1)
+    ax_task(1, 1, 1)
+    fx_task(0, 2, 0)
+    ay_task(1, 1, 2)
+    ay_send(0, 0, 3)
+    ax_task(1, 0, 0)
+    ay_task(0, 0, 0)
+    fx_task(0, 0, 3)
+    fx_task(0, 1, 2)
+    fz_task(1, 0)
+    ay_task(1, 0, 1)
+    ay_task(1, 1, 3)
+    below(0)
+    fm_task(0, 1)
+    fx_task(0, 2, 1)
+    fz_task(1, 2)
+    fm_task(0, 2)
+    ax_task(0, 0, 0)
+    ay_task(1, 0, 2)
+    fx_task(0, 2, 2)
+    ax_task(1, 0, 1)
+    ay_task(0, 0, 1)
+    ay_task(0, 1, 1)
+    ay_task(0, 1, 2)
+    fx_task(0, 1, 3)
+    fc_task(1, 2)
+    ay_task(0, 0, 2)
+    fz_task(0, 1)
+    ax_task(1, 0, 2)
+    ax_task(1, 1, 2)
+    fx_task(0, 2, 3)
+    ay_send(0, 1, 3)
+    am_task(1, 1)
+    ay_task(0, 0, 3)
     fz_task(0, 0)
-    fz_task(0, 1)
+    ax_task(0, 0, 1)
+    fc_task(0, 1)
+    ax_task(1, 1, 3)
+    ax_task(0, 1, 0)
     fz_task(0, 2)
-    fc_task(0, 1)
+    ax_task(0, 1, 1)
+    am_task(1, 0)
     fc_task(0, 2)
-    ax_task(0)
-    az_task(0)
+    ay_task(1, 0, 3)
+    ax_task(0, 1, 2)
+    az_task(1, 1)
+    am_task(0, 0)
+    ax_task(1, 0, 3)
+    ax_task(0, 0, 2)
+    ay_task(0, 1, 3)
+    am_task(0, 1)
+    az_task(1, 0)
+    ax_task(0, 1, 3)
+    ax_task(0, 0, 3)
+    az_task(0, 0)
+    az_task(0, 1)
     for l in (1, 0):
         for j in range(3):
             fy_task(l, j)
-        af_task(l)
+        for p in range(2):
+            af_task(l, p)
     ml.finish()
 
 
@@ -940,34 +1172,33 @@
             pltpu.VMEM((T, D), F32),
             pltpu.VMEM((2, 4, T, D), BF),
             pltpu.VMEM((T, D), BF),
-            pltpu.VMEM((T, D), BF),
             pltpu.VMEM((3, T, D), BF),
             pltpu.VMEM((4, T, D), BF),
-            pltpu.VMEM((2, 2, T, D), BF),
             pltpu.VMEM((2, T, D), BF),
+            pltpu.VMEM((T, D), BF),
             pltpu.VMEM((4, 2, 96, 2 * FS + D), BF),
             pltpu.VMEM((2, 3, 4, 96, D), BF),
-            pltpu.VMEM((2, 3, 3, 96, D), BF),
+            pltpu.VMEM((2, 3, 5, 96, D), BF),
             pltpu.VMEM((2, 2, 48, D), BF),
             pltpu.VMEM((2, 4, 2, 2, 48, AW), BF),
             pltpu.VMEM((2, 2, 4, 2, 48, AW), BF),
             pltpu.VMEM((2, 4, 2, 48, AW), BF),
             pltpu.VMEM((2, 4, 48, AW), BF),
-            pltpu.VMEM((2, 3, 48, AW), BF),
+            pltpu.VMEM((2, 5, 48, AW), BF),
             pltpu.VMEM((2, 8, D), F32),
             sems(10),
             sems(2, 3), sems(2, 3),
             sems(2, 2), sems(2, 2),
             sems(2), sems(2),
-            sems(2, 3), sems(2, 3),
             sems(2, 3, 4), sems(2, 3, 4),
+            sems(2, 3, 6), sems(2, 3, 5),
             sems(2, 3), sems(2, 3),
             sems(2, 3), sems(2, 3),
+            sems(2, 2, 2), sems(2, 2, 2),
+            sems(2, 2, 4), sems(2, 2, 4),
+            sems(2, 2, 4), sems(2, 2, 4),
+            sems(2, 2, 6), sems(2, 2, 5),
             sems(2, 2), sems(2, 2),
-            sems(2), sems(2),
-            sems(2), sems(2),
-            sems(2, 4), sems(2, 4),
-            sems(2), sems(2),
         ],
         compiler_params=pltpu.CompilerParams(collective_id=1, has_side_effects=True, vmem_limit_bytes=60 * 2**20),
         cost_estimate=pl.CostEstimate(flops=2 * 10**10, bytes_accessed=10**8, transcendentals=0),

time: 372 us -> 294 us (0.79)
  Pallas kernels: 362 us -> 284 us
    pallas_call x1, Pallas kernels: 206 us -> 142 us  [backward_call(): pl.pallas_call(backward_kernel, out_shape=[jax.ShapeDtypeStruct((T, D), F...]
    pallas_call x1, Pallas kernels: 150 us -> 136 us  [forward_call(): pl.pallas_call(forward_kernel, out_shape=[jax.ShapeDtypeStruct((T, D), BF...]
where the time goes in v3:
time: 294 us
  Pallas kernels  284 us (97%)
  local copies, waits for them, and re-layouts  8.1 us (3%)
    pallas_call x1, Pallas kernels, backward_call(): pl.pallas_call(backward_kernel, out_shape=[jax.ShapeDtypeStruct((T, D), F...  142 us
    pallas_call x1, Pallas kernels, forward_call(): pl.pallas_call(forward_kernel, out_shape=[jax.ShapeDtypeStruct((T, D), BF...  136 us
    pallas_call x1, Pallas kernels, epilogue(): pl.pallas_call(finish_kernel, out_shape=[jax.ShapeDtypeStruct(v, F32) for...  6.33 us

profile of v3, /device:TPU:0, one launch (start us, length us, event | category | flops | bytes accessed | tf_op | source)
XLA Modules:
  0.0 293.9 jit_solution(13162265311099874443)
XLA Ops:
  0.6 0.8 copy.41
  1.4 0.8 copy.42
  2.2 0.8 copy.43
  2.9 0.8 copy.44
  3.7 0.1 maximum_bitcast_fusion
  3.8 0.6 fusion.2.par_ref
  4.4 135.6 %forward.1 = (bf16[256,768]{1,0:T(8,128)(2,1)}, bf16[2,2,8,2,48,1664]{5,4,3,2,1,0:T(8,128)(2,1)}, bf16[2,768,2304]{2,1,0:T(8,128)(2,1)}, bf16[2,3,256,768]{3,2,1...) custom-call(bf16[256,768]{1,0:T(8,128)(2,1)} %bitcast.18, ...), custom_call_target="tpu_custom_call" | custom-call | flops 10000000000 | bytes 100000000 | tf_op jit(solution)/shard_map/forward/pallas_call | solution.py:605
  140.0 0.0 copy-start.4
  140.0 142.5 %backward.1 = (f32[256,768]{1,0:T(8,128)}, bf16[2,2,2,2,48,768]{5,4,3,2,1,0:T(8,128)(2,1)}, bf16[2,2,96,768]{3,2,1,0:T(8,128)(2,1)}, bf16[2,2,48,1664]{3,2,1,0:T(8,128)(2,1)}) custom-call(bf16[256,768]{1,0:T(8,128)(2,1)} %bitcast.19, f32[256,128]{1,0:T(8,128)} %get-tuple-element.38.cos_ref, f32[256,128]{1,0:T(8,128)} %get-tuple-element.39.sin_ref, ...), custom_call_target="tpu_custom_call" | custom-call | flops 20000000000 | bytes 100000000 | tf_op jit(solution)/shard_map/backward/pallas_call | solution.py:1160
  282.5 0.0 copy-start
  282.5 1.3 copy-done
  283.8 0.0 copy-start.1
  283.8 1.1 copy-done.1
  284.8 0.0 copy-start.2
  284.9 1.1 copy-done.2
  285.9 0.0 copy-start.3
  285.9 6.3 %finish.1 = (f32[2,48,2304]{2,1,0:T(8,128)}, f32[2,48,768]{2,1,0:T(8,128)}, f32[2,48,3072]{2,1,0:T(8,128)}, f32[2,48,3072]{2,1,0:T(8,128)}, f32[2,192,768]{2,1,0...) custom-call(bf16[2,2,2,2,48,768]{5,4,3,2,1,0:T(8,128)(2,1)S(1)} %copy-done, ...), custom_call_target="tpu_custom_call" | custom-call | flops 1000000 | bytes 10000000 | tf_op jit(solution)/shard_map/finish/pallas_call | solution.py:1234
  292.2 0.0 copy-done.4
  292.2 0.7 copy.47
  293.0 0.0 copy-done.3
  293.0 0.9 copy.48
Async XLA Ops:
  140.0 152.2 %copy-start.4 = (bf16[256,768]{1,0:T(8,128)(2,1)S(1)}, bf16[256,768]{1,0:T(8,128)(2,1)}, u32[]{:S(2)}) copy-start(bf16[256,768]{1,0:T(8,128)(2,1)} %get-tuple-element.37) | copy-start | bytes 1179652
  282.5 1.3 copy-start
  283.8 1.1 copy-start.1
  284.8 1.1 copy-start.2
  285.9 7.1 %copy-start.3 = (f32[256,768]{1,0:T(8,128)S(1)}, f32[256,768]{1,0:T(8,128)}, u32[]{:S(2)}) copy-start(f32[256,768]{1,0:T(8,128)} %get-tuple-element.50) | copy-start | bytes 2359300

commit v4 on v3

--- a/solution.py
+++ b/solution.py
@@ -99,7 +99,7 @@
     barrier = pltpu.get_barrier_semaphore()
     for who in partners:
         pl.semaphore_signal(barrier, inc=1, device_id=who, device_id_type=MESH)
-    pl.semaphore_wait(barrier, len(partners))
+    return lambda: pl.semaphore_wait(barrier, len(partners))
 
 
 class Mail:
@@ -152,10 +152,10 @@
 
 
 def forward_kernel(
-    x_ref, seg_ref, freq_ref, qkv_ref, outw_ref, par_ref, gate_ref, up_ref, dn_ref,
+    x_ref, seg_ref, freq_ref, g1_ref, b1_ref, g2_ref, b2_ref, qkv_ref, outw_ref, gate_ref, up_ref, dn_ref,
     y_ref, A_o, F_o, Q_o, ST_o, P_o, TG_o, TT_o, N_o, I_o, PV_o, cos_ref, sin_ref,
     A, F, Q, ST, Pb, TG, TT, N, I, PV, S, AT, MF, AC, H, bias, FD, RC, RY, W, GU,
-    ls, s_gu, r_gu, s_az, r_az, s_ax, r_ax, s_ay, r_ay, s_ac, r_ac, s_fz, r_fz, s_fx, r_fx,
+    ls, s_gu, r_gu, s_az, r_az, s_ax, r_ax, s_ay, r_ay, s_ac, r_ac, s_fz, r_fz, s_fx, r_fx, s_fw, r_fw,
     s_m, r_m, s_rc, r_rc, s_ry, r_ry, os,
 ):
     pc = Place()
@@ -166,6 +166,8 @@
     near, across = pc.zto(pc.near()), pc.zto(pc.across())
     THREE = (0, 1, 2)
 
+    met = greet(pc.line())
+
     own_a, own_f = [], []
     for l in LAY:
         own_a.append([])
@@ -173,11 +175,9 @@
             dst = A.at[l, h, g, c]
             own_a[l].append(ml.local(qkv_ref.at[l, :, pl.ds(QW * h, QW)], dst.at[:, pl.ds(0, QW)], ls.at[l, h]))
             own_a[l].append(ml.local(outw_ref.at[l, :, pl.ds(OW * h, OW)], dst.at[:, pl.ds(QW, OW)], ls.at[l, 2 + h]))
-            own_a[l].append(ml.local(par_ref.at[l, h], dst.at[:, pl.ds(QW + OW, 128)], ls.at[l, 4 + h]))
     wide = [ml.local(gate_ref, W.at[0], ls.at[0, 6]), ml.local(up_ref, W.at[1], ls.at[1, 6])]
     for l in LAY:
         own_f.append(ml.local(dn_ref.at[l, pl.ds(pl.multiple_of(y * 96, 96), 96)], F.at[l, chip_rows(g), pl.ds(2 * FS, D)], ls.at[l, 7]))
-    greet(pc.line())
 
     def gu_send(l):
         ml.send(GU.at[l, 1 - c, y], F.at[l, shard_rows(g, c), pl.ds(0, 2 * FS)], s_gu.at[l], r_gu.at[l], pc.core())
@@ -193,6 +193,14 @@
         ml.arrive(block, ss.at[0], rs.at[i], near)
         to, at = ((across, 2), (near, 1), (near, 2))[i]
         ml.send_if(mid, block, block, ss.at[2 + i], rs.at[at], to)
+
+    def own_params():
+        for l in LAY:
+            for h, refs in enumerate(((g1_ref, b1_ref), (g2_ref, b2_ref))):
+                two = [ref[l:l + 1, :].astype(F32) for ref in refs]
+                rows = jnp.concatenate(two + [jnp.zeros((6, 48), F32)], axis=0).astype(BF)
+                wide_rows = lax.dot_general(rows, onehot, (((0,), (0,)), ((), ())), preferred_element_type=F32)
+                A[l, h, g, c, :, QW + OW:] = wide_rows.astype(BF)
 
     def a_own(l):
         for copy in own_a[l]:
@@ -230,6 +238,7 @@
         ml.arrive(A.at[l, h, :, 1 - c], s_ac.at[l, h], r_ac.at[l, h], pc.core())
 
     parts = (pl.ds(0, 2 * FS), pl.ds(2 * FS, D))
+    ALONG = (1, 1)
 
     def f_ready(l):
         for w in range(2):
@@ -247,9 +256,22 @@
     def f_z(l, p, i):
         block = F.at[l, chip_rows(pc.chip_from(i, x)), parts[p]]
         line_pass(i, block, s_fz.at[l, p], r_fz.at[l, p])
-        ml.send(block, block, s_fx.at[l, p, 1 + i], r_fx.at[l, p, 1 + i], pc.xside())
+        if (l, p) != ALONG:
+            ml.send(block, block, s_fx.at[l, p, 1 + i], r_fx.at[l, p, 1 + i], pc.xside())
+
+    def f_cross():
+        l, p = ALONG
+        block = F.at[l, chip_rows(pc.chip_from(None, 1 - x)), parts[p]]
+        ml.arrive(block, s_fx.at[l, p, 0], r_fx.at[l, p, 0], pc.xside())
+        line_own(block, s_fw, r_fw)
+
+    def f_w(i):
+        l, p = ALONG
+        line_pass(i, F.at[l, chip_rows(pc.chip_from(i, 1 - x)), parts[p]], s_fw, r_fw)
 
     def f_x(l, p):
+        if (l, p) == ALONG:
+            return
         for j in range(4):
             ml.arrive(F.at[l, chip_rows(pc.chip_from(FOUR[j], 1 - x)), parts[p]], s_fx.at[l, p, j], r_fx.at[l, p, j], pc.xside())
 
@@ -393,6 +415,8 @@
     def projected(l):
         params(l)
         project(l)
+
+    def turn_state(l):
         turn(S, ST.at[l, 0], 0)
 
     def scores(l):
@@ -476,102 +500,110 @@
         a_c_arrive(l, 1 - y)
         save(A.at[l], A_o.at[l])
 
+    own_params()
+    met()
     a_own(0)
     begin()
-    f_ready(0)
     a_own(1)
     a_z(0, 0)
+    f_ready(0)
+    a_yo(0, 0)
+    f_ready(1)
+    a_z(0, 1)
     tables()
-    a_yo(0, 0)
+    a_z(1, 0)
+    a_yo(0, 1)
+    a_z(1, 1)
+    a_x(0, 0)
+    a_z(0, 2)
+    a_yo(0, 2)
+    a_x(0, 1)
     f_own_x(0, 0)
-    a_x(0, 0)
-    f_own_z(0, 1)
+    a_x(0, 2)
+    ay_arrive(0, 0)
+    f_own_z(0, 0)
     a_yx(0, 0)
-    a_z(0, 1)
-    a_z(1, 0)
-    a_z(0, 2)
+    a_yo(1, 0)
     a_x(1, 0)
-    a_x(0, 1)
-    f_z(0, 1, 0)
-    ay_arrive(0, 0)
-    a_yo(0, 1)
-    f_own_z(0, 0)
-    a_yo(0, 2)
-    a_yo(1, 0)
+    ay_arrive(0, 1)
     a_yx(0, 1)
-    a_x(0, 2)
-    ay_arrive(0, 1)
+    f_own_z(1, 1)
+    a_x(0, 3)
+    a_x(1, 1)
+    ay_arrive(1, 0)
     ay_arrive(0, 2)
-    a_z(1, 1)
     a_z(1, 2)
     a_yx(0, 2)
-    a_x(0, 3)
+    f_own_z(0, 1)
     a_yx(0, 3)
-    f_ready(1)
-    a_x(1, 1)
+    ac_own(0)
+    turn_state(0)
+    ay_arrive(0, 3)
     f_z(0, 0, 0)
+    ay_arrive(0, 4)
+    a_yo(1, 1)
     f_z(0, 0, 1)
-    ay_arrive(0, 3)
-    ac_own(0)
-    ay_arrive(0, 4)
     ay_arrive(0, 5)
-    a_yo(1, 1)
-    a_yx(1, 0)
-    f_own_x(0, 1)
+    a_yo(1, 2)
     ay_arrive(0, 6)
     ac_other(0)
     a_x(1, 2)
-    a_yo(1, 2)
+    attn_ready(0)
+    projected(0)
     f_z(0, 0, 2)
-    attn_ready(0)
+    a_yx(1, 0)
     f_own_z(1, 0)
-    ay_arrive(1, 0)
     a_yx(1, 1)
+    f_z(0, 1, 0)
+    scores(0)
+    f_own_x(0, 1)
+    f_z(1, 1, 0)
+    first_norm(0)
+    ay_arrive(1, 1)
+    f_z(0, 1, 1)
+    f_z(0, 1, 2)
+    ay_arrive(1, 2)
+    a_yx(1, 2)
+    own_up(0)
+    turn_attended(0)
+    f_own_x(1, 1)
+    f_z(1, 1, 1)
+    ay_arrive(1, 3)
+    f_z(1, 0, 0)
+    pass_on(0)
+    f_own_x(1, 0)
     a_x(1, 3)
-    ay_arrive(1, 1)
-    projected(0)
-    scores(0)
-    first_norm(0)
-    ay_arrive(1, 2)
-    f_z(0, 1, 1)
-    ac_own(1)
-    ay_arrive(1, 3)
-    f_z(0, 1, 2)
-    a_yx(1, 2)
-    f_z(1, 0, 0)
-    f_own_x(1, 1)
+    ay_arrive(1, 4)
+    other_up(0)
+    a_yx(1, 3)
     f_z(1, 0, 1)
-    ay_arrive(1, 4)
-    own_up(0)
-    pass_on(0)
-    turn_attended(0)
-    a_yx(1, 3)
-    other_up(0)
-    f_own_z(1, 1)
-    f_own_x(1, 0)
-    ay_arrive(1, 5)
     own_down(0)
     other_down(0)
+    ay_arrive(1, 5)
     ay_arrive(1, 6)
+    ac_other(1)
+    ac_own(1)
+    f_z(1, 1, 2)
+    turn_middle(0)
     f_z(1, 0, 2)
-    ac_other(1)
-    turn_middle(0)
-    f_z(1, 1, 0)
-    f_z(1, 1, 1)
+    f_cross()
     attn_ready(1)
     second_norm(0)
     projected(1)
     scores(1)
     first_norm(1)
-    f_z(1, 1, 2)
+    turn_state(1)
+    f_w(0)
+    f_w(1)
     turn_activated(0)
+    turn_attended(1)
     own_up(1)
+    f_w(2)
     own_down(1)
     pass_on(1)
     other_up(1)
     other_down(1)
     turn_middle(1)
-    turn_attended(1)
     turn_activated(1)
     second_norm(1)
     for src, dst in ((N, N_o), (I, I_o), (PV, PV_o)):
@@ -607,7 +639,7 @@
         out_shape=[jax.ShapeDtypeStruct((T, D), BF)]
         + [jax.ShapeDtypeStruct(s, d) for s, d in FWD_SHAPES]
         + [jax.ShapeDtypeStruct((T, 128), F32)] * 2,
-        in_specs=[vm] * 3 + [any_spec] * 6,
+        in_specs=[vm] * 7 + [any_spec] * 5,
         out_specs=[vm] + [any_spec] * len(FWD_SHAPES) + [vm] * 2,
         scratch_shapes=[pltpu.VMEM(s, d) for s, d in FWD_SHAPES]
         + [
@@ -630,6 +662,7 @@
             sems(2, 2), sems(2, 2),
             sems(2, 2, 5), sems(2, 2, 3),
             sems(2, 2, 4), sems(2, 2, 4),
+            sems(5), sems(3),
             sems(2, 3), sems(2, 3),
             sems(2, 2), sems(2, 2),
             sems(2), sems(2),
@@ -673,9 +706,9 @@
             if name in loading:
                 loading.pop(name).wait()
 
-    load(1, "PV", "N", "I", "TT", "F", "TG", "ST", "A", "P", "Q")
+    met = greet(pc.line())
+    load(1, "PV", "N", "I", "F", "TG", "TT", "ST", "A", "P", "Q")
     U[...] = cot_ref[...].astype(F32)
-    greet(pc.line())
 
     fcols = (pl.ds(2 * FS, D), pl.ds(0, FS), pl.ds(FS, FS))
 
@@ -939,6 +972,8 @@
     def upper(l):
         need("PV", "N", "I")
         norm_back(1, None, GF.at[l, slot])
+        if l == 1:
+            met()
         mine = GF.at[l, slot]
         ml.send(mine, mine, s_m.at[l, 0], r_m.at[l, 0], pc.yside())
         ml.send(mine, mine, s_m.at[l, 1], r_m.at[l, 1], pc.core())
@@ -949,7 +984,7 @@
         ml.send(FD.at[s_], RC.at[yy], s_rc.at[l, i], r_rc.at[l, i], pc.core(), ("fd", l))
 
     def own_tokens(l):
-        need("TT", "F", "TG")
+        need("F", "TG")
         ml.gone(("fd", 1))
         ml.arrive(GF.at[l, 2 * y + 1 - c], s_m.at[l, 1], r_m.at[l, 1], pc.core())
         act_back(l, 2 * y, 2)
@@ -975,6 +1010,7 @@
             load(0, "F")
 
     def weights(l, j):
+        need("TT")
         ml.gone(("fx", 1, j) if l == 0 else None)
         weight_grad(l, j)
         fx_send(l, j)
@@ -1206,40 +1242,60 @@
     )(cot, cos, sin, *kept)
 
 
-def finish_kernel(gug, dng, af, qkv_o, out_o, gate_o, up_o, down_o, g1_o, b1_o, g2_o, b2_o):
+def finish_kernel(
+    y_i, gin_i, gug_i, dng_i, af_i, y_o, gin_o, qkv_o, out_o, gate_o, up_o, down_o, g1_o, b1_o, g2_o, b2_o,
+    y_v, gin_v, gug, dng, af, qkv, out, gate, up, down, in_sem, out_sem,
+):
+    def copy(src, dst, sem):
+        c = pltpu.make_async_copy(src, dst, sem)
+        c.start()
+        return c
+    arriving = [[copy(src.at[l], dst.at[l], in_sem.at[l, i]) for i, (src, dst) in enumerate(((af_i, af), (gug_i, gug), (dng_i, dng)))] for l in range(2)]
+    passing = [copy(y_i, y_v, in_sem.at[0, 3]), copy(gin_i, gin_v, in_sem.at[1, 3])]
+    leaving = []
     for l in range(2):
+        arriving[l][0].wait()
         for h in range(2):
-            qkv_o[l, :, h * QW:h * QW + QW] = af[l, h, :, 0:QW].astype(F32)
-            out_o[l, :, h * OW:h * OW + OW] = af[l, h, :, QW:QW + OW].astype(F32)
+            qkv[l, :, h * QW:h * QW + QW] = af[l, h, :, 0:QW].astype(F32)
+            out[l, :, h * OW:h * OW + OW] = af[l, h, :, QW:QW + OW].astype(F32)
             turned = af[l, h, :, QW + OW:].astype(F32).T
             for i, ref in enumerate(((g1_o, b1_o), (g2_o, b2_o))[h]):
                 ref[l:l + 1, :] = turned[i:i + 1, :]
-            down_o[l, 96 * h:96 * h + 96, :] = dng[l, h].astype(F32)
-    def of(n, carry):
-        l, j = n // G, n % G
-        for w, ref in enumerate((gate_o, up_o)):
-            pairs = gug[l, w, :, :, :, tile(j // 4, 384)]
-            for m in range(4):
-                def put(m=m):
-                    pieces = [pairs[cc, yy, :, 96 * m:96 * m + 96].astype(F32) for cc in range(2) for yy in range(2)]
-                    ref[l, :, tile(j, 384)] = jnp.concatenate(pieces, axis=1)
-                pl.when(j % 4 == m)(put)
-        return carry
-    lax.fori_loop(0, 2 * G, of, 0)
-
-
-def epilogue(gug, dng, af):
+        leaving.append(copy(qkv.at[l], qkv_o.at[l], out_sem.at[l, 0]))
+        leaving.append(copy(out.at[l], out_o.at[l], out_sem.at[l, 1]))
+        arriving[l][1].wait()
+        for w, ref in enumerate((gate, up)):
+            for j in range(G):
+                pieces = [gug[l, w, cc, yy, :, 96 * j:96 * j + 96] for cc in range(2) for yy in range(2)]
+                ref[l, :, 384 * j:384 * j + 384] = jnp.concatenate(pieces, axis=1).astype(F32)
+            leaving.append(copy(ref.at[l], (gate_o, up_o)[w].at[l], out_sem.at[l, 2 + w]))
+        passing[l].wait()
+        leaving.append(copy((y_v, gin_v)[l], (y_o, gin_o)[l], out_sem.at[l, 5]))
+        arriving[l][2].wait()
+        for h in range(2):
+            down[l, 96 * h:96 * h + 96, :] = dng[l, h].astype(F32)
+        leaving.append(copy(down.at[l], down_o.at[l], out_sem.at[l, 4]))
+    for c in leaving:
+        c.wait()
+
+
+def epilogue(y, gin, gug, dng, af):
     vm = pl.BlockSpec(memory_space=pltpu.VMEM)
-    shapes = [(2, 48, 3 * D), (2, 48, D), (2, 48, 4 * FS), (2, 48, 4 * FS), (2, 192, D)] + [(2, 48)] * 4
+    any_spec = pl.BlockSpec(memory_space=pl.ANY)
+    large = [(2, 48, 3 * D), (2, 48, D), (2, 48, 4 * FS), (2, 48, 4 * FS), (2, 192, D)]
     return tuple(pl.pallas_call(
         finish_kernel,
-        out_shape=[jax.ShapeDtypeStruct(v, F32) for v in shapes],
-        in_specs=[vm] * 3,
-        out_specs=[vm] * len(shapes),
-        compiler_params=pltpu.CompilerParams(vmem_limit_bytes=40 * 2**20),
+        out_shape=[jax.ShapeDtypeStruct(v.shape, v.dtype) for v in (y, gin)]
+        + [jax.ShapeDtypeStruct(v, F32) for v in large + [(2, 48)] * 4],
+        in_specs=[any_spec] * 5,
+        out_specs=[any_spec] * 7 + [vm] * 4,
+        scratch_shapes=[pltpu.VMEM(v.shape, v.dtype) for v in (y, gin, gug, dng, af)]
+        + [pltpu.VMEM(v, F32) for v in large]
+        + [sems(2, 4), sems(2, 6)],
+        compiler_params=pltpu.CompilerParams(vmem_limit_bytes=60 * 2**20),
         cost_estimate=pl.CostEstimate(flops=10**6, bytes_accessed=10**7, transcendentals=0),
         name="finish",
-    )(gug, dng, af))
+    )(y, gin, gug, dng, af))
 
 
 def positions_of(segment_row):
@@ -1260,9 +1316,8 @@
              first_gain, first_bias, second_gain, second_bias):
     frequency = rope_base ** (-2.0 * np.arange(HEAD // 2, dtype=np.float32) / HEAD)
     freq = jnp.asarray(np.tile(frequency.astype(np.float32)[None, :], (8, 4)))
-    par = jnp.stack([jnp.stack([first_gain, first_bias], -1), jnp.stack([second_gain, second_bias], -1)], 1)
-    par = jnp.pad(par, ((0, 0), (0, 0), (0, 0), (0, 126)))
-    return inputs[0], segment_ids, freq, qkv_weight, out_weight, par, gate_weight, up_weight, down_weight
+    return (inputs[0], segment_ids, freq, first_gain, first_bias, second_gain, second_bias, qkv_weight, out_weight,
+            gate_weight, up_weight, down_weight)
 
 
 def rotate(values, cosine_table, sine_table):
@@ -1570,7 +1625,8 @@
                       first_gain, first_bias, second_gain, second_bias)
     output, *kept, cos, sin = forward_call(staged)
     gin, gug, dng, af = backward_call(cotangent[0], cos, sin, kept)
-    return (output[None], gin[None]) + epilogue(gug, dng, af)
+    output, gin, *gradients = epilogue(output, gin, gug, dng, af)
+    return (output[None], gin[None], *gradients)
 
 
 IN_SPECS = (

time: 294 us -> 282 us (0.959)
  local copies, waits for them, and re-layouts: 8.1 us -> 0 us
  Pallas kernels: 284 us -> 281 us
    unnamed x12 -> x0, local copies, waits for them, and re-layouts: 5.04 us -> none
    another operation x4 -> x0, local copies, waits for them, and re-layouts: 3.06 us -> none  [the longest x2 1.53 us: prologue(): jnp.stack([first_gain, first_bias], -1)]
where the time goes in v4:
time: 282 us
  Pallas kernels  281 us (100%)
    pallas_call x1, Pallas kernels, backward_call(): pl.pallas_call(backward_kernel, out_shape=[jax.ShapeDtypeStruct((T, D), F...  143 us
    pallas_call x1, Pallas kernels, forward_call(): pl.pallas_call(forward_kernel, out_shape=[jax.ShapeDtypeStruct((T, D), BF...  133 us

profile of v4, /device:TPU:0, one launch (start us, length us, event | category | flops | bytes accessed | tf_op | source)
XLA Modules:
  0.0 281.6 jit_solution(8664326988044830103)
XLA Ops:
  0.6 133.4 %forward.1 = (bf16[256,768]{1,0:T(8,128)(2,1)}, bf16[2,2,8,2,48,1664]{5,4,3,2,1,0:T(8,128)(2,1)}, bf16[2,768,2304]{2,1,0:T(8,128)(2,1)}, bf16[2,3,256,768]{3,2,1...) custom-call(bf16[256,768]{1,0:T(8,128)(2,1)} %bitcast.5, ...), custom_call_target="tpu_custom_call" | custom-call | flops 10000000000 | bytes 100000000 | tf_op jit(solution)/shard_map/forward/pallas_call | solution.py:637
  134.1 142.9 %backward.1 = (f32[256,768]{1,0:T(8,128)}, bf16[2,2,2,2,48,768]{5,4,3,2,1,0:T(8,128)(2,1)}, bf16[2,2,96,768]{3,2,1,0:T(8,128)(2,1)}, bf16[2,2,48,1664]{3,2,1,0:T(8,128)(2,1)}) custom-call(bf16[256,768]{1,0:T(8,128)(2,1)} %bitcast.6, f32[256,128]{1,0:T(8,128)} %get-tuple-element.40.cos_ref, f32[256,128]{1,0:T(8,128)} %get-tuple-element.41.sin_ref, ...), custom_call_target="tpu_custom_call" | custom-call | flops 20000000000 | bytes 100000000 | tf_op jit(solution)/shard_map/backward/pallas_call | solution.py:1196
  277.0 4.4 %finish.1 = (bf16[256,768]{1,0:T(8,128)(2,1)}, f32[256,768]{1,0:T(8,128)}, f32[2,48,2304]{2,1,0:T(8,128)}, f32[2,48,768]{2,1,0:T(8,128)}, f32[2,48,3072]{2,1,0:T...) custom-call(bf16[256,768]{1,0:T(8,128)(2,1)} %get-tuple-element.39.y, ...), custom_call_target="tpu_custom_call" | custom-call | flops 1000000 | bytes 10000000 | tf_op jit(solution)/shard_map/finish/pallas_call | solution.py:1286

commit v5 on v4

--- a/solution.py
+++ b/solution.py
@@ -25,6 +25,11 @@
 AW = QW + OW + 128
 FS = 768
 PAIRS = HEADS // 2
+HT = T // 2
+
+
+def part_of(half):
+    return pl.ds(half * HT, HT)
 
 
 def dot(a, b):
@@ -327,11 +332,11 @@
     def attention(l):
         def pair(p, carry):
             cols = tile(p, 128)
-            q, kk, v = Q[l, 0, :, cols], Q[l, 1, :, cols], Q[l, 2, :, cols]
+            q, kk, v = Q[l, 0, :, cols] * jnp.asarray(0.125, BF), Q[l, 1, :, cols], Q[l, 2, :, cols]
             outs = []
             for h in range(2):
                 qh = jnp.where(pair_mask == (h == 0), q, jnp.zeros_like(q))
-                s = dot_t(qh, kk) * 0.125 + bias[...]
+                s = dot_t(qh, kk) + bias[...]
                 e = jnp.exp(s - jnp.max(s, axis=1, keepdims=True))
                 pr = (e * (1.0 / jnp.sum(e, axis=1, keepdims=True))).astype(BF)
                 Pb[l, 2 * p + h] = pr
@@ -350,7 +355,7 @@
             w = A[l, h, :, :, :, QW:QW + OW].reshape(D, OW)
             H[:, h * OW:h * OW + OW] = H[:, h * OW:h * OW + OW] + dot(AT[...], w)
 
-    def norm(l, i, dst, extra):
+    def norm(l, i, dst, extra, half):
         gain, shift = PV[l, i, 0:1, :], PV[l, i, 1:2, :]
         def rows_of(j, carry):
             rows = tile(j, 32)
@@ -366,29 +371,29 @@
             H[rows, :] = m
             dst[rows, :] = m.astype(BF)
             return carry
-        lax.fori_loop(0, T // 32, rows_of, 0)
-
-    def ffn_up(l, first, count):
-        some = pl.ds(first, count)
+        lax.fori_loop(half * (HT // 32), (half + 1) * (HT // 32), rows_of, 0)
+
+    def ffn_up(l, first, toks):
+        two, n = pl.ds(first, 2), toks.size
         def cols_of(j, carry):
             cols = tile(j, 256)
-            xx = MF[l, some].reshape(count * T, D)
+            xx = MF[l, two, toks].reshape(2 * n, D)
             gate = dot(xx, F[l, :, cols])
             up = dot(xx, F[l, :, pl.ds(pl.multiple_of(FS + j * 256, 256), 256)])
             act = gate * jax.nn.sigmoid(gate) * up
-            TG[l, 0, some, :, cols] = gate.astype(BF).reshape(count, T, 256)
-            TG[l, 1, some, :, cols] = up.astype(BF).reshape(count, T, 256)
-            AC[some, :, cols] = act.astype(BF).reshape(count, T, 256)
+            TG[l, 0, two, toks, cols] = gate.astype(BF).reshape(2, n, 256)
+            TG[l, 1, two, toks, cols] = up.astype(BF).reshape(2, n, 256)
+            AC[two, toks, cols] = act.astype(BF).reshape(2, n, 256)
             return carry
         lax.fori_loop(0, FS // 256, cols_of, 0)
 
-    def ffn_down(l, s_, plus=None):
+    def ffn_down(l, s_, toks, plus=None):
         def cols_of(j, carry):
             cols = tile(j, 256)
-            r = dot(AC[s_], F[l, :, pl.ds(pl.multiple_of(2 * FS + j * 256, 256), 256)])
+            r = dot(AC[s_, toks], F[l, :, pl.ds(pl.multiple_of(2 * FS + j * 256, 256), 256)])
             if plus is not None:
-                r = r + plus[:, cols].astype(F32)
-            FD[l, s_, :, cols] = r.astype(BF)
+                r = r + plus[toks, cols].astype(F32)
+            FD[l, s_, toks, cols] = r.astype(BF)
             return carry
         lax.fori_loop(0, D // 256, cols_of, 0)
 
@@ -424,49 +429,54 @@
         save(Pb.at[l], P_o.at[l])
         save(Q.at[l], Q_o.at[l])
 
-    def first_norm(l):
+    WHOLE = pl.ds(0, T)
+
+    def branch(l):
         out_project(l)
-        norm(l, 0, MF.at[l, slot], None)
-        mine = MF.at[l, slot]
-        ml.send(mine, mine, s_m.at[l, 0], r_m.at[l, 0], pc.yside())
-        ml.send(mine, mine, s_m.at[l, 1], r_m.at[l, 1], pc.core())
+
+    def first_norm(l, h):
+        norm(l, 0, MF.at[l, slot], None, h)
+        mine = MF.at[l, slot, part_of(h)]
+        ml.send(mine, mine, s_m.at[l, 0, h], r_m.at[l, 0, h], pc.yside())
+        ml.send(mine, mine, s_m.at[l, 1, h], r_m.at[l, 1, h], pc.core())
 
     def turn_attended(l):
         turn(AT, ST.at[l, 1], 0)
         save(ST.at[l], ST_o.at[l])
 
-    def half_sums(l, i, yy):
-        s_ = 2 * yy + 1 - c
-        ffn_down(l, s_)
-        ml.send(FD.at[l, s_], RC.at[l, yy], s_rc.at[l, i], r_rc.at[l, i], pc.core())
-
     def own_up(l):
-        ml.arrive(MF.at[l, 2 * y + 1 - c], s_m.at[l, 1], r_m.at[l, 1], pc.core())
+        for h in range(2):
+            ml.arrive(MF.at[l, 2 * y + 1 - c, part_of(h)], s_m.at[l, 1, h], r_m.at[l, 1, h], pc.core())
         f_x(l, 0)
-        ffn_up(l, 2 * y, 2)
+        ffn_up(l, 2 * y, WHOLE)
 
     def own_down(l):
         f_x(l, 1)
-        half_sums(l, 1, y)
-        ffn_down(l, slot)
-
-    def pass_on(l):
-        block = MF.at[l, 2 * (1 - y) + c]
-        ml.arrive(block, s_m.at[l, 0], r_m.at[l, 0], pc.yside())
-        ml.send(block, block, s_m.at[l, 2], r_m.at[l, 2], pc.core())
-
-    def other_up(l):
+        s_ = 2 * y + 1 - c
+        ffn_down(l, s_, WHOLE)
+        ml.send(FD.at[l, s_], RC.at[l, y], s_rc.at[l, 2], r_rc.at[l, 2], pc.core())
+        ffn_down(l, slot, WHOLE)
+
+    def pass_on(l, h):
+        block = MF.at[l, 2 * (1 - y) + c, part_of(h)]
+        ml.arrive(block, s_m.at[l, 0, h], r_m.at[l, 0, h], pc.yside())
+        ml.send(block, block, s_m.at[l, 2, h], r_m.at[l, 2, h], pc.core())
+
+    def other_up(l, h):
         others = 2 * (1 - y)
-        ffn_up(l, others + c, 1)
-        ml.arrive(MF.at[l, others + 1 - c], s_m.at[l, 2], r_m.at[l, 2], pc.core())
-        ffn_up(l, others + 1 - c, 1)
-
-    def other_down(l):
-        others = 2 * (1 - y)
-        half_sums(l, 0, 1 - y)
-        ml.arrive(RC.at[l, 1 - y], s_rc.at[l, 0], r_rc.at[l, 0], pc.core())
-        ffn_down(l, others + c, RC.at[l, 1 - y])
-        ml.send(FD.at[l, others + c], RY.at[l], s_ry.at[l], r_ry.at[l], pc.yside())
+        ml.arrive(MF.at[l, others + 1 - c, part_of(h)], s_m.at[l, 2, h], r_m.at[l, 2, h], pc.core())
+        ffn_up(l, others, part_of(h))
+
+    def other_down(l, h):
+        s_ = 2 * (1 - y) + 1 - c
+        ffn_down(l, s_, part_of(h))
+        ml.send(FD.at[l, s_, part_of(h)], RC.at[l, 1 - y, part_of(h)], s_rc.at[l, h], r_rc.at[l, h], pc.core())
+
+    def other_sum(l, h):
+        s_ = 2 * (1 - y) + c
+        ml.arrive(RC.at[l, 1 - y, part_of(h)], s_rc.at[l, h], r_rc.at[l, h], pc.core())
+        ffn_down(l, s_, part_of(h), RC.at[l, 1 - y])
+        ml.send(FD.at[l, s_, part_of(h)], RY.at[l, part_of(h)], s_ry.at[l, h], r_ry.at[l, h], pc.yside())
 
     def turn_middle(l):
         turn_slots(MF.at[l], TT.at[l, 0])
@@ -477,11 +487,12 @@
         save(TT.at[l], TT_o.at[l])
         save(TG.at[l], TG_o.at[l])
 
-    def second_norm(l):
-        ml.arrive(RC.at[l, y], s_rc.at[l, 1], r_rc.at[l, 1], pc.core())
-        ml.arrive(RY.at[l], s_ry.at[l], r_ry.at[l], pc.yside())
+    def second_norm(l, h):
+        if h == 0:
+            ml.arrive(RC.at[l, y], s_rc.at[l, 2], r_rc.at[l, 2], pc.core())
+        ml.arrive(RY.at[l, part_of(h)], s_ry.at[l, h], r_ry.at[l, h], pc.yside())
         feed = lambda rows: FD[l, slot, rows, :].astype(F32) + RC[l, y, rows, :].astype(F32) + RY[l, rows, :].astype(F32)
-        norm(l, 1, S if l == 0 else y_ref, feed)
+        norm(l, 1, S if l == 0 else y_ref, feed, h)
 
     def ay_arrive(l, n):
         if n < 3:
@@ -503,109 +514,125 @@
     own_params()
     met()
     a_own(0)
-    begin()
     a_own(1)
     a_z(0, 0)
+    a_z(0, 1)
+    begin()
+    a_x(1, 0)
+    a_x(0, 0)
+    a_z(1, 0)
     f_ready(0)
+    a_z(1, 1)
     a_yo(0, 0)
+    a_z(0, 2)
+    a_yx(0, 0)
+    a_yo(0, 1)
+    ay_arrive(0, 0)
+    f_own_x(0, 1)
+    a_x(0, 1)
+    f_own_z(0, 0)
+    a_yo(0, 2)
+    a_z(1, 2)
     f_ready(1)
-    a_z(0, 1)
+    a_x(1, 1)
+    a_x(0, 2)
     tables()
-    a_z(1, 0)
-    a_yo(0, 1)
-    a_z(1, 1)
-    a_x(0, 0)
-    a_z(0, 2)
-    a_yo(0, 2)
-    a_x(0, 1)
+    a_yx(0, 1)
+    ay_arrive(0, 1)
+    ay_arrive(0, 2)
+    a_x(1, 2)
+    ay_arrive(0, 3)
+    a_yo(1, 0)
     f_own_x(0, 0)
-    a_x(0, 2)
-    ay_arrive(0, 0)
-    f_own_z(0, 0)
-    a_yx(0, 0)
-    a_yo(1, 0)
-    a_x(1, 0)
-    ay_arrive(0, 1)
-    a_yx(0, 1)
+    f_own_z(0, 1)
+    ay_arrive(0, 4)
+    a_x(0, 3)
+    a_yx(0, 2)
     f_own_z(1, 1)
-    a_x(0, 3)
-    a_x(1, 1)
-    ay_arrive(1, 0)
-    ay_arrive(0, 2)
-    a_z(1, 2)
-    a_yx(0, 2)
-    f_own_z(0, 1)
     a_yx(0, 3)
     ac_own(0)
+    a_yx(1, 0)
     turn_state(0)
-    ay_arrive(0, 3)
     f_z(0, 0, 0)
-    ay_arrive(0, 4)
-    a_yo(1, 1)
     f_z(0, 0, 1)
     ay_arrive(0, 5)
+    ay_arrive(0, 6)
+    f_z(0, 0, 2)
+    ay_arrive(1, 0)
+    ac_other(0)
+    a_yo(1, 1)
+    f_z(1, 1, 0)
     a_yo(1, 2)
-    ay_arrive(0, 6)
-    ac_other(0)
-    a_x(1, 2)
+    f_z(0, 1, 0)
+    a_yx(1, 1)
     attn_ready(0)
     projected(0)
-    f_z(0, 0, 2)
-    a_yx(1, 0)
     f_own_z(1, 0)
-    a_yx(1, 1)
-    f_z(0, 1, 0)
+    a_x(1, 3)
     scores(0)
-    f_own_x(0, 1)
-    f_z(1, 1, 0)
-    first_norm(0)
+    f_z(0, 1, 1)
+    branch(0)
     ay_arrive(1, 1)
-    f_z(0, 1, 1)
+    first_norm(0, 0)
+    first_norm(0, 1)
+    turn_attended(0)
+    ay_arrive(1, 2)
+    ay_arrive(1, 3)
     f_z(0, 1, 2)
-    ay_arrive(1, 2)
+    own_up(0)
+    ay_arrive(1, 4)
+    f_own_x(1, 0)
     a_yx(1, 2)
-    own_up(0)
-    turn_attended(0)
+    a_yx(1, 3)
+    f_z(1, 1, 1)
+    pass_on(0, 0)
+    ac_own(1)
+    other_up(0, 0)
     f_own_x(1, 1)
-    f_z(1, 1, 1)
-    ay_arrive(1, 3)
+    pass_on(0, 1)
     f_z(1, 0, 0)
-    pass_on(0)
-    f_own_x(1, 0)
-    a_x(1, 3)
-    ay_arrive(1, 4)
-    other_up(0)
-    a_yx(1, 3)
     f_z(1, 0, 1)
     own_down(0)
-    other_down(0)
+    other_down(0, 0)
+    other_up(0, 1)
     ay_arrive(1, 5)
+    other_sum(0, 0)
+    f_z(1, 1, 2)
     ay_arrive(1, 6)
+    other_down(0, 1)
+    other_sum(0, 1)
     ac_other(1)
-    ac_own(1)
-    f_z(1, 1, 2)
-    turn_middle(0)
     f_z(1, 0, 2)
     f_cross()
     attn_ready(1)
-    second_norm(0)
+    turn_middle(0)
+    second_norm(0, 0)
+    second_norm(0, 1)
     projected(1)
     scores(1)
-    first_norm(1)
+    f_w(0)
+    branch(1)
+    first_norm(1, 0)
+    f_w(1)
+    first_norm(1, 1)
+    turn_activated(0)
+    f_w(2)
+    own_up(1)
+    pass_on(1, 0)
+    own_down(1)
+    other_up(1, 0)
+    other_down(1, 0)
+    pass_on(1, 1)
     turn_state(1)
-    f_w(0)
-    f_w(1)
-    turn_activated(0)
+    other_sum(1, 0)
+    other_up(1, 1)
+    other_down(1, 1)
+    turn_middle(1)
+    other_sum(1, 1)
+    turn_activated(1)
+    second_norm(1, 0)
     turn_attended(1)
-    own_up(1)
-    f_w(2)
-    own_down(1)
-    pass_on(1)
-    other_up(1)
-    other_down(1)
-    turn_middle(1)
-    turn_activated(1)
-    second_norm(1)
+    second_norm(1, 1)
     for src, dst in ((N, N_o), (I, I_o), (PV, PV_o)):
         save(src, dst)
     for copy in out_copies:
@@ -663,9 +690,9 @@
             sems(2, 2, 5), sems(2, 2, 3),
             sems(2, 2, 4), sems(2, 2, 4),
             sems(5), sems(3),
+            sems(2, 3, 2), sems(2, 3, 2),
             sems(2, 3), sems(2, 3),
             sems(2, 2), sems(2, 2),
-            sems(2), sems(2),
             sems(17),
         ],
         compiler_params=pltpu.CompilerParams(collective_id=0, has_side_effects=True, vmem_limit_bytes=60 * 2**20),
@@ -678,10 +705,10 @@
     cot_ref, cos_ref, sin_ref, A_i, F_i, Q_i, ST_i, P_i, TG_i, TT_i, N_i, I_i, PV_i,
     gin_ref, GUG, DNG, AF,
     A, F, Q, ST, Pb, TG, TT, N, I, PV,
-    U, GF, GB, GP, FD, RC, RY, FG, RFX, RFZ, FR, AG, RAC, RAY, RAX, RAZ, V,
+    U, GF, GB, GP, FD, RC, RY, FG, RFX, RFZ, FR, AG, RAC, RAY, RAX, RAZ, RO, OX, OR, OT, OY, V,
     ls, s_m, r_m, s_rc, r_rc, s_ry, r_ry,
     s_fx, r_fx, s_fz, r_fz, s_fc, r_fc, s_fy, r_fy,
-    s_ac, r_ac, s_ay, r_ay, s_ax, r_ax, s_az, r_az, s_af, r_af,
+    s_ac, r_ac, s_ay, r_ay, s_ax, r_ax, s_az, r_az, s_af, r_af, s_oz, r_oz, s_ox, r_ox, s_oy, r_oy,
 ):
     pc = Place()
     y, z, x, c, slot = pc.y, pc.z, pc.x, pc.c, pc.slot
@@ -728,7 +755,7 @@
                 dst[here] = (dst[here].astype(F32) + src[here].astype(F32)).astype(BF)
                 at += w
 
-    def line_middle(part, R, ss, rs, rows, widths):
+    def line_middle(part, R, ss, rs, add):
         far = [pltpu.make_async_remote_copy(R.at[n], R.at[n], ss.at[0], rs.at[n], device_id=near, device_id_type=MESH) for n in (1, 2)]
         on = [
             ml.later(part(plane), R.at[3 + n], ss.at[3 + n], rs.at[3 + n], across, mid)
@@ -738,24 +765,33 @@
         def go():
             for n in range(2):
                 far[n].wait_recv()
-                plus(dsts[n], R.at[1 + n], rows, widths)
+                add(dsts[n], R.at[1 + n])
                 on[n].start()
         pl.when(mid)(go)
 
-    def line_end(part, R, ss, rs, rows, widths):
+    def line_end(part, R, ss, rs, add):
         back = [pltpu.make_async_remote_copy(R.at[n], R.at[n], ss.at[0], rs.at[n], device_id=across, device_id_type=MESH) for n in (3, 4)]
         last = ml.later(part(zn), R.at[0], ss.at[5], rs.at[0], near, mid)
         dsts = [part(z), part(zn)]
         def go():
             back[1].wait_recv()
-            plus(dsts[1], R.at[4], rows, widths)
+            add(dsts[1], R.at[4])
             last.start()
             back[0].wait_recv()
-            plus(dsts[0], R.at[3], rows, widths)
+            add(dsts[0], R.at[3])
         pl.when(mid)(go)
         ml.arrive(R.at[0], ss.at[0], rs.at[0], near)
 
-    FW, AWS = (D,), (768, 896)
+    def add_f(dst, src):
+        plus(dst, src, 96, (D,))
+
+    def add_a(dst, src):
+        plus(dst, src, 48, awide[0])
+
+    def add_o(dst, src):
+        for i in range(2):
+            for xx in range(2):
+                plus(dst.at[i, xx], src.at[i, xx], 48, awide[1])
 
     def fpart(l, j):
         return lambda zz: RFX.at[l, j, zz]
@@ -771,10 +807,10 @@
                 line_start(n, fpart(l, j), RFZ.at[l, j], s_fz.at[l, j], r_fz.at[l, j])
 
     def fm_task(l, j):
-        line_middle(fpart(l, j), RFZ.at[l, j], s_fz.at[l, j], r_fz.at[l, j], 96, FW)
+        line_middle(fpart(l, j), RFZ.at[l, j], s_fz.at[l, j], r_fz.at[l, j], add_f)
 
     def fz_task(l, j):
-        line_end(fpart(l, j), RFZ.at[l, j], s_fz.at[l, j], r_fz.at[l, j], 96, FW)
+        line_end(fpart(l, j), RFZ.at[l, j], s_fz.at[l, j], r_fz.at[l, j], add_f)
         def total(start):
             rows = pl.ds(start, 48)
             return (RFX[l, j, z, rows, :].astype(F32) + RFZ[l, j, 0, rows, :].astype(F32)).astype(BF)
@@ -814,42 +850,71 @@
 
     def ay_send(l, p, n):
         q = planes[n]
-        ml.send(RAC.at[l, 0, q, :, :, acols[p]], RAY.at[l, q, :, :, acols[p]], s_ay.at[l, p, n], r_ay.at[l, p, n], pc.yside())
+        ml.send(RAC.at[l, 0, q, :, :, acols[p]], RAY.at[l, q], s_ay.at[l, p, n], r_ay.at[l, p, n], pc.yside())
 
     def ay_task(l, p, n):
         q = planes[n]
-        ml.arrive(RAY.at[l, q, :, :, acols[p]], s_ay.at[l, p, n], r_ay.at[l, p, n], pc.yside())
+        ml.arrive(RAY.at[l, q], s_ay.at[l, p, n], r_ay.at[l, p, n], pc.yside())
         for xx in range(2):
-            plus(RAC.at[l, 1, q, xx, :, acols[p]], RAY.at[l, q, xx, :, acols[p]], 48, awide[p])
-        ml.send(RAC.at[l, 1, q, 1 - x, :, acols[p]], RAX.at[l, q, :, acols[p]], s_ax.at[l, p, n], r_ax.at[l, p, n], pc.xside())
+            plus(RAC.at[l, 1, q, xx, :, acols[p]], RAY.at[l, q, xx], 48, awide[p])
+        ml.send(RAC.at[l, 1, q, 1 - x, :, acols[p]], RAX.at[l, q], s_ax.at[l, p, n], r_ax.at[l, p, n], pc.xside())
 
     def apart(l, p):
-        return lambda zz: RAX.at[l, zz, :, acols[p]]
+        return lambda zz: RAX.at[l, zz]
 
     def ax_task(l, p, n):
         q = planes[n]
-        ml.arrive(RAX.at[l, q, :, acols[p]], s_ax.at[l, p, n], r_ax.at[l, p, n], pc.xside())
-        plus(RAX.at[l, q, :, acols[p]], RAC.at[l, 1, q, x, :, acols[p]], 48, awide[p])
+        ml.arrive(RAX.at[l, q], s_ax.at[l, p, n], r_ax.at[l, p, n], pc.xside())
+        plus(RAX.at[l, q], RAC.at[l, 1, q, x, :, acols[p]], 48, awide[p])
         if n < 3:
-            line_start(n, apart(l, p), RAZ.at[l, :, :, acols[p]], s_az.at[l, p], r_az.at[l, p])
+            line_start(n, apart(l, p), RAZ.at[l], s_az.at[l, p], r_az.at[l, p])
 
     def am_task(l, p):
-        line_middle(apart(l, p), RAZ.at[l, :, :, acols[p]], s_az.at[l, p], r_az.at[l, p], 48, awide[p])
+        line_middle(apart(l, p), RAZ.at[l], s_az.at[l, p], r_az.at[l, p], add_a)
 
     def az_task(l, p):
-        line_end(apart(l, p), RAZ.at[l, :, :, acols[p]], s_az.at[l, p], r_az.at[l, p], 48, awide[p])
+        line_end(apart(l, p), RAZ.at[l], s_az.at[l, p], r_az.at[l, p], add_a)
         mine = AF.at[l, y, :, acols[p]]
-        mine[...] = (RAX[l, z, :, acols[p]].astype(F32) + RAZ[l, 0, :, acols[p]].astype(F32)).astype(BF)
+        mine[...] = (RAX[l, z].astype(F32) + RAZ[l, 0].astype(F32)).astype(BF)
         ml.send(mine, mine, s_af.at[l, p], r_af.at[l, p], pc.yside())
 
     def af_task(l, p):
         ml.arrive(AF.at[l, 1 - y, :, acols[p]], s_af.at[l, p], r_af.at[l, p], pc.yside())
+
+    def opart(l):
+        return lambda zz: RAC.at[l, :, zz, :, :, acols[1]]
+
+    def o_start(l):
+        for n in range(3):
+            line_start(n, opart(l), RO.at[l], s_oz.at[l], r_oz.at[l])
+
+    def om_task(l):
+        line_middle(opart(l), RO.at[l], s_oz.at[l], r_oz.at[l], add_o)
+
+    def oz_task(l):
+        line_end(opart(l), RO.at[l], s_oz.at[l], r_oz.at[l], add_o)
+        for i, h in ((0, 1 - y), (1, y)):
+            both = lambda xx: (RAC[l, i, z, xx, :, acols[1]].astype(F32) + RO[l, 0, i, xx].astype(F32)).astype(BF)
+            OX[l, h] = both(1 - x)
+            OT[l, h] = both(x)
+        ml.send(OX.at[l], OR.at[l], s_ox.at[l], r_ox.at[l], pc.xside())
+
+    def ox_task(l):
+        ml.arrive(OR.at[l], s_ox.at[l], r_ox.at[l], pc.xside())
+        for h in range(2):
+            plus(OT.at[l, h], OR.at[l, h], 48, awide[1])
+        ml.send(OT.at[l], OY.at[l], s_oy.at[l], r_oy.at[l], pc.yside())
+
+    def oy_task(l):
+        ml.arrive(OY.at[l], s_oy.at[l], r_oy.at[l], pc.yside())
+        for h in range(2):
+            AF[l, h, :, acols[1]] = (OT[l, h].astype(F32) + OY[l, h].astype(F32)).astype(BF)
 
     pair_mask = head_mask(T, 128)
     low_half = lax.broadcasted_iota(jnp.int32, (T, 128), 1) % HEAD < HEAD // 2
     onehot = (lax.broadcasted_iota(jnp.int32, (8, 128), 0) == lax.broadcasted_iota(jnp.int32, (8, 128), 1)).astype(F32).astype(BF)
 
-    def norm_back(i, extra, dst):
+    def norm_back(i, extra, dst, half):
         gain = PV[i, 0:1, :]
         def rows_of(j, carry):
             gs, bs = carry
@@ -868,32 +933,33 @@
             dst[rows, :] = r.astype(BF)
             return gs, bs
         zero = jnp.zeros((8, D), F32)
-        gs, bs = lax.fori_loop(0, T // 32, rows_of, (zero, zero))
+        gs, bs = lax.fori_loop(half * (HT // 32), (half + 1) * (HT // 32), rows_of, (zero, zero))
         row = lax.broadcasted_iota(jnp.int32, (8, D), 0)
-        V[i] = jnp.where(row == 0, gs.sum(0, keepdims=True), jnp.where(row == 1, bs.sum(0, keepdims=True), 0.0))
-
-    def act_back(l, first, count):
-        some = pl.ds(first, count)
+        sums = jnp.where(row == 0, gs.sum(0, keepdims=True), jnp.where(row == 1, bs.sum(0, keepdims=True), 0.0))
+        V[i] = sums if half == 0 else V[i] + sums
+
+    def act_back(l, first, toks):
+        two, n = pl.ds(first, 2), toks.size
         def cols_of(j, carry):
             cols = tile(j, 256)
-            ga = dot_t(GF[l, some].reshape(count * T, D), F[cols, 2 * FS:])
-            gate = TG[0, some, :, cols].reshape(count * T, 256).astype(F32)
-            up = TG[1, some, :, cols].reshape(count * T, 256).astype(F32)
+            ga = dot_t(GF[l, two, toks].reshape(2 * n, D), F[cols, 2 * FS:])
+            gate = TG[0, two, toks, cols].reshape(2 * n, 256).astype(F32)
+            up = TG[1, two, toks, cols].reshape(2 * n, 256).astype(F32)
             sg = jax.nn.sigmoid(gate)
             gg = ga * up * sg * (1.0 + gate * (1.0 - sg))
             gu = ga * gate * sg
-            TG[0, some, :, cols] = gg.astype(BF).reshape(count, T, 256)
-            TG[1, some, :, cols] = gu.astype(BF).reshape(count, T, 256)
+            TG[0, two, toks, cols] = gg.astype(BF).reshape(2, n, 256)
+            TG[1, two, toks, cols] = gu.astype(BF).reshape(2, n, 256)
             return carry
         lax.fori_loop(0, FS // 256, cols_of, 0)
 
-    def mid_back(s_, plus=None):
+    def mid_back(s_, toks, plus=None):
         def cols_of(j, carry):
             cols = tile(j, 256)
-            r = dot_t(TG[0, s_], F[cols, 0:FS]) + dot_t(TG[1, s_], F[cols, FS:2 * FS])
+            r = dot_t(TG[0, s_, toks], F[cols, 0:FS]) + dot_t(TG[1, s_, toks], F[cols, FS:2 * FS])
             if plus is not None:
-                r = r + plus[:, cols].astype(F32)
-            FD[s_, :, cols] = r.astype(BF)
+                r = r + plus[toks, cols].astype(F32)
+            FD[s_, toks, cols] = r.astype(BF)
             return carry
         lax.fori_loop(0, D // 256, cols_of, 0)
 
@@ -969,44 +1035,49 @@
         for step, *what in steps:
             step(*what)
 
-    def upper(l):
+    WHOLE = pl.ds(0, T)
+
+    def upper(l, h):
         need("PV", "N", "I")
-        norm_back(1, None, GF.at[l, slot])
-        if l == 1:
+        norm_back(1, None, GF.at[l, slot], h)
+        if l == 1 and h == 0:
             met()
-        mine = GF.at[l, slot]
-        ml.send(mine, mine, s_m.at[l, 0], r_m.at[l, 0], pc.yside())
-        ml.send(mine, mine, s_m.at[l, 1], r_m.at[l, 1], pc.core())
-
-    def half_sums(l, i, yy):
-        s_ = 2 * yy + 1 - c
-        mid_back(s_)
-        ml.send(FD.at[s_], RC.at[yy], s_rc.at[l, i], r_rc.at[l, i], pc.core(), ("fd", l))
+        mine = GF.at[l, slot, part_of(h)]
+        ml.send(mine, mine, s_m.at[l, 0, h], r_m.at[l, 0, h], pc.yside())
+        ml.send(mine, mine, s_m.at[l, 1, h], r_m.at[l, 1, h], pc.core())
 
     def own_tokens(l):
         need("F", "TG")
         ml.gone(("fd", 1))
-        ml.arrive(GF.at[l, 2 * y + 1 - c], s_m.at[l, 1], r_m.at[l, 1], pc.core())
-        act_back(l, 2 * y, 2)
-        half_sums(l, 1, y)
-        mid_back(slot)
-
-    def other_tokens(l):
+        for h in range(2):
+            ml.arrive(GF.at[l, 2 * y + 1 - c, part_of(h)], s_m.at[l, 1, h], r_m.at[l, 1, h], pc.core())
+        act_back(l, 2 * y, WHOLE)
+        s_ = 2 * y + 1 - c
+        mid_back(s_, WHOLE)
+        ml.send(FD.at[s_], RC.at[y], s_rc.at[l, 2], r_rc.at[l, 2], pc.core(), ("fd", l))
+        mid_back(slot, WHOLE)
+
+    def pass_on(l, h):
+        block = GF.at[l, 2 * (1 - y) + c, part_of(h)]
+        ml.arrive(block, s_m.at[l, 0, h], r_m.at[l, 0, h], pc.yside())
+        ml.send(block, block, s_m.at[l, 2, h], r_m.at[l, 2, h], pc.core())
+
+    def other_tokens(l, h):
         others = 2 * (1 - y)
-        block = GF.at[l, others + c]
-        ml.arrive(block, s_m.at[l, 0], r_m.at[l, 0], pc.yside())
-        ml.send(block, block, s_m.at[l, 2], r_m.at[l, 2], pc.core())
-        act_back(l, others + c, 1)
-        ml.arrive(GF.at[l, others + 1 - c], s_m.at[l, 2], r_m.at[l, 2], pc.core())
-        act_back(l, others + 1 - c, 1)
-
-    def other_sums(l):
-        others = 2 * (1 - y)
-        half_sums(l, 0, 1 - y)
-        ml.arrive(RC.at[1 - y], s_rc.at[l, 0], r_rc.at[l, 0], pc.core())
-        mid_back(others + c, RC.at[1 - y])
-        ml.send(FD.at[others + c], RY, s_ry.at[l], r_ry.at[l], pc.yside(), ("fd", l))
-        if l == 1:
+        ml.arrive(GF.at[l, others + 1 - c, part_of(h)], s_m.at[l, 2, h], r_m.at[l, 2, h], pc.core())
+        act_back(l, others, part_of(h))
+
+    def other_mids(l, h):
+        s_ = 2 * (1 - y) + 1 - c
+        mid_back(s_, part_of(h))
+        ml.send(FD.at[s_, part_of(h)], RC.at[1 - y, part_of(h)], s_rc.at[l, h], r_rc.at[l, h], pc.core(), ("fd", l))
+
+    def other_sums(l, h):
+        s_ = 2 * (1 - y) + c
+        ml.arrive(RC.at[1 - y, part_of(h)], s_rc.at[l, h], r_rc.at[l, h], pc.core())
+        mid_back(s_, part_of(h), RC.at[1 - y])
+        ml.send(FD.at[s_, part_of(h)], RY.at[part_of(h)], s_ry.at[l, h], r_ry.at[l, h], pc.yside(), ("fd", l))
+        if l == 1 and h == 1:
             load(0, "F")
 
     def weights(l, j):
@@ -1017,11 +1088,12 @@
         if l == 1 and j == 2:
             load(0, "TT", "TG")
 
-    def middle(l):
-        ml.arrive(RC.at[y], s_rc.at[l, 1], r_rc.at[l, 1], pc.core())
-        ml.arrive(RY, s_ry.at[l], r_ry.at[l], pc.yside())
-        norm_back(0, lambda rows: FD[slot, rows, :].astype(F32) + RC[y, rows, :].astype(F32) + RY[rows, :].astype(F32), GB)
-        if l == 1:
+    def middle(l, h):
+        if h == 0:
+            ml.arrive(RC.at[y], s_rc.at[l, 2], r_rc.at[l, 2], pc.core())
+        ml.arrive(RY.at[part_of(h)], s_ry.at[l, h], r_ry.at[l, h], pc.yside())
+        norm_back(0, lambda rows: FD[slot, rows, :].astype(F32) + RC[y, rows, :].astype(F32) + RY[rows, :].astype(F32), GB, h)
+        if l == 1 and h == 1:
             load(0, "PV", "N", "I")
 
     QKV, OUT = 0, 1
@@ -1054,139 +1126,135 @@
         if l == 1:
             load(0, "ST", "A")
 
-    upper(1)
+    upper(1, 0)
+    upper(1, 1)
     own_tokens(1)
-    other_tokens(1)
-    other_sums(1)
+    pass_on(1, 0)
+    other_tokens(1, 0)
+    other_mids(1, 0)
+    pass_on(1, 1)
+    other_sums(1, 0)
+    other_tokens(1, 1)
+    other_mids(1, 1)
     weights(1, 0)
+    other_sums(1, 1)
+    fx_task(1, 0, 0)
+    middle(1, 0)
     weights(1, 1)
+    middle(1, 1)
+    fx_task(1, 0, 1)
+    out_sums(1)
     weights(1, 2)
-    fx_task(1, 0, 0)
-    middle(1)
-    out_sums(1)
+    fx_task(1, 0, 2)
+    ac_sum(1, 1, 0)
+    ac_sum(1, 1, 1)
+    o_start(1)
     scores(1)
-    ac_sum(1, 1, 0)
-    ay_send(1, 1, 0)
     below(1)
-    upper(0)
+    upper(0, 0)
     fx_task(1, 1, 0)
-    fx_task(1, 0, 1)
+    upper(0, 1)
     qkv_sums(1)
-    ay_send(1, 1, 1)
     own_tokens(0)
-    ay_send(1, 1, 2)
+    ac_sum(1, 0, 1)
     fx_task(1, 1, 1)
+    fx_task(1, 0, 3)
+    pass_on(0, 0)
     ac_sum(1, 0, 0)
+    ay_send(1, 0, 0)
+    other_tokens(0, 0)
+    fx_task(1, 1, 2)
+    pass_on(0, 1)
+    other_mids(0, 0)
+    om_task(1)
+    fx_task(1, 1, 3)
+    fx_task(1, 2, 0)
+    other_tokens(0, 1)
+    other_sums(0, 0)
+    other_mids(0, 1)
+    weights(0, 0)
     fm_task(1, 0)
-    fx_task(1, 0, 2)
-    ay_send(1, 0, 0)
-    ac_sum(1, 1, 1)
-    ac_sum(1, 0, 1)
-    ay_task(1, 1, 0)
-    other_tokens(0)
-    fx_task(1, 2, 0)
-    ay_send(1, 1, 3)
-    fx_task(1, 1, 2)
+    ay_task(1, 0, 0)
+    fx_task(1, 2, 1)
+    other_sums(0, 1)
+    weights(0, 1)
+    fx_task(1, 2, 2)
+    middle(0, 0)
+    fx_task(0, 0, 0)
+    ay_send(1, 0, 1)
+    middle(0, 1)
     fm_task(1, 1)
-    fx_task(1, 0, 3)
-    other_sums(0)
-    weights(0, 0)
-    fx_task(1, 1, 3)
+    out_sums(0)
+    ay_send(1, 0, 2)
+    fx_task(1, 2, 3)
+    ac_sum(0, 1, 0)
+    fx_task(0, 0, 1)
+    ac_sum(0, 1, 1)
+    fm_task(1, 2)
+    o_start(0)
+    ay_send(1, 0, 3)
+    scores(0)
+    qkv_sums(0)
+    fx_task(0, 0, 2)
+    ay_task(1, 0, 1)
+    ac_sum(0, 0, 0)
+    fx_task(0, 0, 3)
+    ay_send(0, 0, 0)
+    fz_task(1, 0)
+    weights(0, 2)
+    fx_task(0, 1, 0)
+    ay_send(0, 0, 1)
+    ac_sum(0, 0, 1)
+    om_task(0)
+    ay_send(0, 0, 2)
+    ax_task(1, 0, 0)
     fz_task(1, 1)
-    ay_send(1, 0, 1)
-    fx_task(1, 2, 1)
-    ax_task(1, 1, 0)
-    weights(0, 1)
-    ay_send(1, 0, 2)
-    fx_task(0, 0, 0)
-    fx_task(1, 2, 2)
-    ay_task(1, 1, 1)
-    middle(0)
-    out_sums(0)
-    scores(0)
-    ay_send(1, 0, 3)
-    qkv_sums(0)
-    fx_task(1, 2, 3)
-    ac_sum(0, 1, 1)
-    fx_task(0, 1, 0)
-    fx_task(0, 0, 1)
-    ac_sum(0, 1, 0)
-    ay_send(0, 1, 0)
-    ay_task(1, 0, 0)
-    ay_send(0, 1, 1)
-    fm_task(1, 2)
-    ac_sum(0, 0, 0)
-    weights(0, 2)
-    ac_sum(0, 0, 1)
-    ay_send(0, 1, 2)
+    below(0)
+    ay_task(0, 0, 0)
     fx_task(0, 1, 1)
-    ay_task(0, 1, 0)
-    ay_send(0, 0, 0)
-    ay_send(0, 0, 1)
-    fx_task(0, 0, 2)
-    ay_send(0, 0, 2)
+    fc_task(1, 1)
+    oz_task(1)
     fm_task(0, 0)
-    fc_task(1, 1)
-    ax_task(1, 1, 1)
     fx_task(0, 2, 0)
-    ay_task(1, 1, 2)
     ay_send(0, 0, 3)
-    ax_task(1, 0, 0)
-    ay_task(0, 0, 0)
-    fx_task(0, 0, 3)
+    ax_task(1, 0, 1)
+    fz_task(1, 2)
+    fx_task(0, 2, 1)
+    oz_task(0)
+    ay_task(0, 0, 1)
     fx_task(0, 1, 2)
-    fz_task(1, 0)
-    ay_task(1, 0, 1)
-    ay_task(1, 1, 3)
-    below(0)
     fm_task(0, 1)
-    fx_task(0, 2, 1)
-    fz_task(1, 2)
+    fx_task(0, 2, 2)
+    fz_task(0, 0)
+    ay_task(1, 0, 2)
+    ay_task(0, 0, 2)
+    fx_task(0, 1, 3)
     fm_task(0, 2)
+    fc_task(1, 2)
     ax_task(0, 0, 0)
-    ay_task(1, 0, 2)
-    fx_task(0, 2, 2)
-    ax_task(1, 0, 1)
-    ay_task(0, 0, 1)
-    ay_task(0, 1, 1)
-    ay_task(0, 1, 2)
-    fx_task(0, 1, 3)
-    fc_task(1, 2)
-    ay_task(0, 0, 2)
+    am_task(1, 0)
+    ay_task(1, 0, 3)
+    ox_task(0)
+    fx_task(0, 2, 3)
+    ay_task(0, 0, 3)
+    ax_task(0, 0, 1)
+    ox_task(1)
     fz_task(0, 1)
     ax_task(1, 0, 2)
-    ax_task(1, 1, 2)
-    fx_task(0, 2, 3)
-    ay_send(0, 1, 3)
-    am_task(1, 1)
-    ay_task(0, 0, 3)
-    fz_task(0, 0)
-    ax_task(0, 0, 1)
     fc_task(0, 1)
-    ax_task(1, 1, 3)
-    ax_task(0, 1, 0)
     fz_task(0, 2)
-    ax_task(0, 1, 1)
-    am_task(1, 0)
     fc_task(0, 2)
-    ay_task(1, 0, 3)
-    ax_task(0, 1, 2)
-    az_task(1, 1)
     am_task(0, 0)
     ax_task(1, 0, 3)
     ax_task(0, 0, 2)
-    ay_task(0, 1, 3)
-    am_task(0, 1)
     az_task(1, 0)
-    ax_task(0, 1, 3)
     ax_task(0, 0, 3)
     az_task(0, 0)
-    az_task(0, 1)
     for l in (1, 0):
         for j in range(3):
             fy_task(l, j)
-        for p in range(2):
-            af_task(l, p)
+        af_task(l, 0)
+        oy_task(l)
     ml.finish()
 
 
@@ -1218,14 +1286,19 @@
             pltpu.VMEM((2, 2, 48, D), BF),
             pltpu.VMEM((2, 4, 2, 2, 48, AW), BF),
             pltpu.VMEM((2, 2, 4, 2, 48, AW), BF),
-            pltpu.VMEM((2, 4, 2, 48, AW), BF),
-            pltpu.VMEM((2, 4, 48, AW), BF),
-            pltpu.VMEM((2, 5, 48, AW), BF),
+            pltpu.VMEM((2, 4, 2, 48, QW), BF),
+            pltpu.VMEM((2, 4, 48, QW), BF),
+            pltpu.VMEM((2, 5, 48, QW), BF),
+            pltpu.VMEM((2, 5, 2, 2, 48, AW - QW), BF),
+            pltpu.VMEM((2, 2, 48, AW - QW), BF),
+            pltpu.VMEM((2, 2, 48, AW - QW), BF),
+            pltpu.VMEM((2, 2, 48, AW - QW), BF),
+            pltpu.VMEM((2, 2, 48, AW - QW), BF),
             pltpu.VMEM((2, 8, D), F32),
             sems(10),
+            sems(2, 3, 2), sems(2, 3, 2),
             sems(2, 3), sems(2, 3),
             sems(2, 2), sems(2, 2),
-            sems(2), sems(2),
             sems(2, 3, 4), sems(2, 3, 4),
             sems(2, 3, 6), sems(2, 3, 5),
             sems(2, 3), sems(2, 3),
@@ -1235,8 +1308,11 @@
             sems(2, 2, 4), sems(2, 2, 4),
             sems(2, 2, 6), sems(2, 2, 5),
             sems(2, 2), sems(2, 2),
+            sems(2, 6), sems(2, 5),
+            sems(2), sems(2),
+            sems(2), sems(2),
         ],
-        compiler_params=pltpu.CompilerParams(collective_id=1, has_side_effects=True, vmem_limit_bytes=60 * 2**20),
+        compiler_params=pltpu.CompilerParams(collective_id=1, has_side_effects=True, vmem_limit_bytes=62 * 2**20),
         cost_estimate=pl.CostEstimate(flops=2 * 10**10, bytes_accessed=10**8, transcendentals=0),
         name="backward",
     )(cot, cos, sin, *kept)

time: 282 us -> 271 us (0.961)
  Pallas kernels: 281 us -> 270 us
    pallas_call x1, Pallas kernels: 143 us -> 136 us  [backward_call(): pl.pallas_call(backward_kernel, out_shape=[jax.ShapeDtypeStruct((T, D), F...]
    pallas_call x1, Pallas kernels: 133 us -> 130 us  [forward_call(): pl.pallas_call(forward_kernel, out_shape=[jax.ShapeDtypeStruct((T, D), BF...]
where the time goes in v5:
time: 271 us
  Pallas kernels  270 us (100%)
    pallas_call x1, Pallas kernels, backward_call(): pl.pallas_call(backward_kernel, out_shape=[jax.ShapeDtypeStruct((T, D), F...  136 us
    pallas_call x1, Pallas kernels, forward_call(): pl.pallas_call(forward_kernel, out_shape=[jax.ShapeDtypeStruct((T, D), BF...  130 us

profile of v5, /device:TPU:0, one launch (start us, length us, event | category | flops | bytes accessed | tf_op | source)
XLA Modules:
  0.0 270.6 jit_solution(1534379352889693456)
XLA Ops:
  0.6 129.6 %forward.1 = (bf16[256,768]{1,0:T(8,128)(2,1)}, bf16[2,2,8,2,48,1664]{5,4,3,2,1,0:T(8,128)(2,1)}, bf16[2,768,2304]{2,1,0:T(8,128)(2,1)}, bf16[2,3,256,768]{3,2,1...) custom-call(bf16[256,768]{1,0:T(8,128)(2,1)} %bitcast.5, ...), custom_call_target="tpu_custom_call" | custom-call | flops 10000000000 | bytes 100000000 | tf_op jit(solution)/shard_map/forward/pallas_call | solution.py:664
  130.3 135.7 %backward.1 = (f32[256,768]{1,0:T(8,128)}, bf16[2,2,2,2,48,768]{5,4,3,2,1,0:T(8,128)(2,1)}, bf16[2,2,96,768]{3,2,1,0:T(8,128)(2,1)}, bf16[2,2,48,1664]{3,2,1,0:T(8,128)(2,1)}) custom-call(bf16[256,768]{1,0:T(8,128)(2,1)} %bitcast.6, f32[256,128]{1,0:T(8,128)} %get-tuple-element.40.cos_ref, f32[256,128]{1,0:T(8,128)} %get-tuple-element.41.sin_ref, ...), custom_call_target="tpu_custom_call" | custom-call | flops 20000000000 | bytes 100000000 | tf_op jit(solution)/shard_map/backward/pallas_call | solution.py:1264
  266.0 4.4 %finish.1 = (bf16[256,768]{1,0:T(8,128)(2,1)}, f32[256,768]{1,0:T(8,128)}, f32[2,48,2304]{2,1,0:T(8,128)}, f32[2,48,768]{2,1,0:T(8,128)}, f32[2,48,3072]{2,1,0:T...) custom-call(bf16[256,768]{1,0:T(8,128)(2,1)} %get-tuple-element.39.y, ...), custom_call_target="tpu_custom_call" | custom-call | flops 1000000 | bytes 10000000 | tf_op jit(solution)/shard_map/finish/pallas_call | solution.py:1362
